TPU v7x, 32 devices: a whole 2x2x4 slice. The times are simulated.
32 devices in a mesh: dp: 8 (over z, x), mp: 4 (over y, core).
Axes of the slice: x: 2, y: 2, z: 4, core: 2. Of those that a mesh axis runs over, the one named last changes fastest.
Arguments:
- grad_out: bfloat16 [2048, 3072], P(('dp', 'mp')), may hold values from -6 to 6
- attn_out: bfloat16 [2048, 4096], P('dp', 'mp'), may hold values from -6 to 6
- weight_codes: bfloat16 [4096, 3072], P('mp', 'dp'), may hold values from -6 to 6
- block_scales: bfloat16 [128, 3072], P('mp', 'dp'), may hold values from 0.0029907227 to 0.049804688
Outputs:
- grad_attn: bfloat16 [2048, 4096], P('dp', 'mp')
- grad_weight_t: bfloat16 [3072, 4096], P('dp', 'mp')
All inputs are finite; a program needn't handle non-finite values.
Results may differ from a plain program's by a relative error of at most 0.0049.
Values may be sent and summed in bfloat16 or wider, within the bound.
No kernel may reach another device: no remote copies, remote signals or barrier semaphores. Data moves between devices by JAX's collectives and lax.ppermute only.
A program may use at most 64 MiB of HBM per device.

v0:
```python
import math

import jax
import jax.numpy as jnp
from jax import lax
from jax.sharding import PartitionSpec as P

BLOCK = 32


def dequantize(codes_part, scales_part):
    expanded = jnp.repeat(scales_part.astype(jnp.float32), BLOCK, axis=0)
    return (codes_part.astype(jnp.float32) * expanded).astype(jnp.bfloat16)


def body(grad_out, attn_out, weight_codes, block_scales):
    group_rows = attn_out.shape[0]
    scaling = 1.0 / math.sqrt(group_rows * lax.axis_size("dp"))
    codes_all, scales_all = (
        lax.all_gather(weight_codes, "dp", axis=1, tiled=True),
        lax.all_gather(block_scales, "dp", axis=1, tiled=True),
    )
    weight_slab = dequantize(codes_all, scales_all)
    by_feature = (((1,), (1,)), ((), ()))
    by_token = (((0,), (0,)), ((), ()))
    whole_rows = lax.all_gather(grad_out, "mp", axis=0, tiled=True)
    grad_rows = lax.dot_general(
        whole_rows, weight_slab, by_feature, preferred_element_type=jnp.float32
    )
    grad_weight_t = lax.psum_scatter(
        scaling
        * lax.dot_general(whole_rows, attn_out, by_token, preferred_element_type=jnp.float32),
        "dp",
        scatter_dimension=0,
        tiled=True,
    )
    return (grad_rows.astype(jnp.bfloat16), grad_weight_t.astype(jnp.bfloat16))


def solution(mesh):
    placed = (P(("dp", "mp"), None), P("dp", "mp"), P("mp", "dp"), P("mp", "dp"))
    return jax.shard_map(
        body, mesh=mesh, in_specs=placed, out_specs=(P("dp", "mp"), P("dp", "mp")), check_vma=False
    )
```

profile of v0, /device:TPU:0, one launch (start us, length us, event | category | flops | bytes accessed | tf_op | source)
XLA Modules:
  0.0 355.2 jit_solution(13233549465432704904)
XLA Ops:
  7.2 0.0 copy-start
  7.2 0.0 all-gather.5.cloned.1.call-start
  7.2 0.7 all-gather.5.cloned.1.call-update
  7.9 0.0 all-gather.3.cloned.1.call-start
  8.0 0.7 all-gather.3.cloned.1.call-update
  8.7 0.0 reduce-scatter.2.cloned.1.call-start
  8.7 23.3 %all-gather.5.cloned.1.call-done = bf16[256,3072]{1,0:T(8,128)(2,1)} async-done(((bf16[64,3072]{1,0:T(8,128)(2,1)}), bf16[256,3072]{1,0:T(8,128)(2,1)}) %all-gather.5.cloned.1.call-update) | async-done | bytes 1572880 | tf_op jit(solution)/shard_map/all_gather | solution.py:26
  32.0 0.0 copy-done
  32.0 7.8 %convolution_multiply_fusion = f32[3072,1024]{1,0:T(8,128)} fusion(bf16[256,3072]{1,0:T(8,128)(2,1)} %all-gather.5.cloned.1.call-done, bf16[256,1024]{1,0:T(8,128)(2,1)S(1)} %copy-done), kind=kOutput, calls=%fused_computation.2 | convolution fusion | flops 1613758464 | bytes 14680064 | tf_op jit(solution)/shard_map/dot_general | solution.py:32
  39.7 0.0 copy-start.2
  39.7 0.0 reduce-scatter.2.cloned.1.call-update
  39.8 0.7 copy-done.2
  40.5 32.3 %all_gather.10 = bf16[32,3072]{1,0:T(8,128)(2,1)S(1)} all-gather(bf16[32,384]{1,0:T(8,128)(2,1)S(1)} %copy-done.2), channel_id=1, replica_groups=mesh['dp'=8,'mp'=4] {'dp'}, dimensions={1}, use_global_device_ids=true | all-gather | bytes 221184 | tf_op jit(solution)/shard_map/all_gather | solution.py:21
  72.8 0.0 copy-start.1
  72.8 64.4 %all-gather.3.cloned.1.call-done = bf16[1024,3072]{1,0:T(8,128)(2,1)} async-done(((bf16[1024,384]{1,0:T(8,128)(2,1)}), bf16[1024,3072]{1,0:T(8,128)(2,1)}) %all-gather.3.cloned.1.call-update) | async-done | bytes 6291472 | tf_op jit(solution)/shard_map/all_gather | solution.py:20
  137.2 4.5 %fusion = bf16[1024,3072]{1,0:T(8,128)(2,1)S(1)} fusion(bf16[1024,3072]{1,0:T(8,128)(2,1)} %all-gather.3.cloned.1.call-done, f32[32,3072]{1,0:T(8,128)S(1)} %convert_element_type.19), kind=kLoop, calls=%fused_computation.1 | loop fusion | flops 9437184 | bytes 12976128 | tf_op jit(solution)/shard_map/convert_element_type | solution.py:13
  141.7 0.0 copy-done.1
  141.7 1.8 fusion.1
  143.5 1.0 copy.6
  144.5 201.8 %reduce-scatter.2.cloned.1.call-done = f32[384,1024]{1,0:T(8,128)} async-done(((f32[3072,1024]{1,0:T(8,128)}), f32[384,1024]{1,0:T(8,128)}) %reduce-scatter.2.cloned.1.call-update) | async-done | bytes 1572880 | tf_op jit(solution)/shard_map/reduce_scatter | solution.py:30
  346.3 2.4 convert_element_type.23
  (1 shorter events, 0.0 us)
Async XLA Ops:
  7.2 24.8 %copy-start = (bf16[256,1024]{1,0:T(8,128)(2,1)S(1)}, bf16[256,1024]{1,0:T(8,128)(2,1)}, u32[]{:S(2)}) copy-start(bf16[256,1024]{1,0:T(8,128)(2,1)} %param.5) | copy-start | bytes 1572868
  7.2 24.8 %all-gather.5.cloned.1.call-start = ((), (), s32[]{:S(2)}) async-start(), calls=%async_computation.2 | async-start | bytes 1966080 | tf_op jit(solution)/shard_map/all_gather | solution.py:26
  7.9 129.3 %all-gather.3.cloned.1.call-start = ((), (), s32[]{:S(2)}) async-start(), calls=%async_computation.1 | async-start | bytes 7077888 | tf_op jit(solution)/shard_map/all_gather | solution.py:20
  8.7 337.6 %reduce-scatter.2.cloned.1.call-start = ((), (), s32[]{:S(2)}) async-start(), calls=%async_computation.3 | async-start | bytes 14155776 | tf_op jit(solution)/shard_map/reduce_scatter | solution.py:30
  39.7 0.7 copy-start.2
  72.8 68.9 %copy-start.1 = (bf16[256,3072]{1,0:T(8,128)(2,1)S(1)}, bf16[256,3072]{1,0:T(8,128)(2,1)}, u32[]{:S(2)}) copy-start(bf16[256,3072]{1,0:T(8,128)(2,1)} %all-gather.5.cloned.1.call-done) | copy-start | bytes 4718596
Sparse Core Ops, SparseCore 0:
  9.6 22.3 all-gather.4
  34.0 103.1 all-gather.2
  140.8 205.4 reduce-scatter.1
where the time goes:
time: 355 us
  waiting for transfers between devices  291 us (82%)
  blocking collectives  32.3 us (9%)
  between operations  13.8 us (4%)
  matrix products  9.6 us (3%)
  other arithmetic  6.9 us (2%)
    reduce_scatter x1, waiting for transfers between devices, body(): lax.psum_scatter(scaling * lax.dot_general(whole_rows, attn_out, by_token...  202 us
    all_gather x1, waiting for transfers between devices, body(): lax.all_gather(weight_codes, 'dp', axis=1, tiled=True)  64.4 us
    all_gather x1, blocking collectives, body(): lax.all_gather(block_scales, 'dp', axis=1, tiled=True)  32.3 us
    all_gather x1, waiting for transfers between devices, body(): whole_rows = lax.all_gather(grad_out, 'mp', axis=0, tiled=True)  23.3 us
    dot_general x1, matrix products, body(): lax.dot_general(whole_rows, attn_out, by_token, preferred_element_type=jn...  7.77 us
  transfers between devices with their start and end apart: 3, of which 3 were waited for; matrix products, arithmetic and copies ran while one was open for 4% of the time, Pallas kernels for 0%

commit v1 on v0

v1 whole, which is shorter than its diff:
```python
import math

import jax
import jax.numpy as jnp
from jax import lax
from jax.sharding import PartitionSpec as P

BLOCK = 32
PAIR = 2


def dequantize(codes_part, scales_part):
    expanded = jnp.repeat(scales_part.astype(jnp.float32), BLOCK, axis=0)
    return (codes_part.astype(jnp.float32) * expanded).astype(jnp.bfloat16)


def by_own_bits(blocks, place, first_axis, count):
    for k in range(count):
        axis = first_axis + k
        bit = (place >> (count - 1 - k)) & 1
        blocks = jnp.where(bit == 1, jnp.flip(blocks, axis), blocks)
    return blocks


def halves(own, other, side, axis):
    first = jnp.where(side == 0, own, other)
    second = jnp.where(side == 0, other, own)
    return jnp.concatenate([first, second], axis)


def body(grad_out, attn_out, weight_codes, block_scales):
    n_dp, n_mp = lax.axis_size("dp"), lax.axis_size("mp")
    layers = n_dp // PAIR
    bits = n_mp.bit_length() - 1
    rows, features = grad_out.shape
    group_rows, heads = attn_out.shape
    own_features = weight_codes.shape[1]
    half = heads // PAIR
    layer_features = PAIR * own_features
    scaling = 1.0 / math.sqrt(group_rows * n_dp)

    dp, mp = lax.axis_index("dp"), lax.axis_index("mp")
    layer, side = dp // PAIR, dp % PAIR

    across = [(i, i ^ 1) for i in range(n_dp)]

    def layer_moves(step, keep=lambda z: True):
        return [
            (z * PAIR + x, (z + step) * PAIR + x)
            for z in range(layers)
            for x in range(PAIR)
            if 0 <= z + step < layers and keep(z)
        ]

    def swap_x(piece):
        return lax.ppermute(piece, "dp", across)

    def swap_mp(piece, bit):
        return lax.ppermute(piece, "mp", [(i, i ^ bit) for i in range(n_mp)])

    slots = []
    for r in range(layers):
        piece = lax.dynamic_slice_in_dim(
            grad_out, ((layer + r) % layers) * layer_features, layer_features, 1
        )
        if r:
            piece = lax.ppermute(
                piece,
                "dp",
                [
                    (z * PAIR + x, ((z + r) % layers) * PAIR + x)
                    for z in range(layers)
                    for x in range(PAIR)
                ],
            )
        slots.append(piece)
    own = jnp.stack(slots)

    by_token = attn_out.reshape((2,) * bits + (rows, heads))
    by_token = by_own_bits(by_token, mp, 0, bits).reshape(group_rows, heads)
    attn_own = lax.dynamic_slice_in_dim(by_token, side * half, half, 1)
    attn_other = swap_x(lax.dynamic_slice_in_dim(by_token, (1 - side) * half, half, 1))
    attn_layer = jnp.concatenate([attn_own, attn_other], 0)

    weight = dequantize(weight_codes, block_scales)
    weight_own = lax.dynamic_slice_in_dim(weight, side * half, half, 0)
    weight_other = swap_x(lax.dynamic_slice_in_dim(weight, (1 - side) * half, half, 0))
    weight_slab = halves(weight_own, weight_other, side, 1)

    top = n_mp // 2
    via_x = swap_x(own)
    via_mp = swap_mp(own, top)
    mixed = []
    for i in range(n_dp):
        for j in range(n_mp):
            there = ((i ^ 1), j) if j % 2 == 0 else (i, j ^ top)
            mixed.append((i * n_mp + j, there[0] * n_mp + there[1]))
    far = lax.ppermute(jnp.where(mp % 2 == 0, via_mp, via_x), ("dp", "mp"), mixed)
    gathered = jnp.stack([jnp.stack([own, via_mp], 1), jnp.stack([via_x, far], 1)], 1)
    for k in range(1, bits):
        bit = top >> k
        gathered = jnp.stack([gathered, swap_mp(gathered, bit)], 2 + k)
    layer_rows = PAIR * group_rows
    columns = gathered.reshape(layers, layer_rows, layer_features)

    up, down = [attn_layer], [attn_layer]
    for r in range(1, layers):
        up.append(lax.ppermute(up[-1], "dp", layer_moves(1, lambda z: z >= r - 1)))
        down.append(lax.ppermute(down[-1], "dp", layer_moves(-1, lambda z: z <= layers - r)))
    total = None
    for r in range(layers):
        rows_r = attn_layer if r == 0 else jnp.where(layer >= r, up[r], down[layers - r])
        term = lax.dot_general(
            columns[r], rows_r, (((0,), (0,)), ((), ())), preferred_element_type=jnp.float32
        )
        total = term if total is None else total + term
    gw = (scaling * total).astype(jnp.bfloat16)
    gw_own = lax.dynamic_slice_in_dim(gw, side * own_features, own_features, 0)
    gw_other = swap_x(lax.dynamic_slice_in_dim(gw, (1 - side) * own_features, own_features, 0))
    grad_weight_t = halves(gw_own, gw_other, side, 1)

    def terms(r):
        return lax.dot_general(
            columns[r], weight_slab, (((1,), (1,)), ((), ())), preferred_element_type=jnp.float32
        )

    parts = [terms(r) for r in range(layers)]
    from_below = from_above = None
    for k in range(1, layers):
        send_up, send_down = parts[k], parts[layers - k]
        if k > 1:
            send_up = send_up + from_below.astype(jnp.float32)
            send_down = send_down + from_above.astype(jnp.float32)
        from_below = lax.ppermute(
            send_up.astype(jnp.bfloat16), "dp", layer_moves(1, lambda z: z <= k - 1)
        )
        from_above = lax.ppermute(
            send_down.astype(jnp.bfloat16), "dp", layer_moves(-1, lambda z: z >= layers - k)
        )
    ga = parts[0] + from_below.astype(jnp.float32) + from_above.astype(jnp.float32)
    ga = ga.astype(jnp.bfloat16)
    ga_other = swap_x(ga[group_rows:])
    grad_attn = halves(ga[:group_rows], ga_other, side, 1)
    grad_attn = by_own_bits(grad_attn.reshape((2,) * bits + (rows, heads)), mp, 0, bits)
    return grad_attn.reshape(group_rows, heads), grad_weight_t


def solution(mesh):
    placed = (P(("dp", "mp"), None), P("dp", "mp"), P("mp", "dp"), P("mp", "dp"))
    return jax.shard_map(
        body, mesh=mesh, in_specs=placed, out_specs=(P("dp", "mp"), P("dp", "mp")), check_vma=False
    )
```

time: 355 us -> 192 us (0.54)
  waiting for transfers between devices: 291 us -> 126 us
  starting transfers between devices: 0.11 us -> 46 us
  blocking collectives: 32.3 us -> 0 us
  between operations: 13.8 us -> 1.14 us
    reduce_scatter x1 -> x0, waiting for transfers between devices: 202 us -> none  [body(): lax.psum_scatter(scaling * lax.dot_general(whole_rows, attn_out, by_token...]
    ppermute x0 -> x23, waiting for transfers between devices: none -> 126 us  [the longest x3 28.2 us: body(): lax.ppermute(send_up.astype(jnp.bfloat16), 'dp', layer_moves(1, lambda z:...]
    all_gather x2 -> x0, waiting for transfers between devices: 87.6 us -> none  [the longest x1 64.4 us: body(): lax.all_gather(weight_codes, 'dp', axis=1, tiled=True)]
    ppermute x0 -> x23, starting transfers between devices: none -> 46 us  [the longest x3 14 us: body(): lax.ppermute(send_up.astype(jnp.bfloat16), 'dp', layer_moves(1, lambda z:...]
    all_gather x1 -> x0, blocking collectives: 32.3 us -> none  [body(): lax.all_gather(block_scales, 'dp', axis=1, tiled=True)]
    convert_element_type x1, other arithmetic: 4.46 us -> 0.15 us  [dequantize(): return (codes_part.astype(jnp.float32) * expanded).astype(jnp.bfloat16)]
    dot_general x2 -> x8, matrix products: 9.6 us -> 7.18 us  [the longest x4 4.74 us: body(): lax.dot_general(columns[r], rows_r, (((0,), (0,)), ((), ())), preferred_e...]
  transfers between devices with their start and end apart: 3 -> 23, of which waited for: 3 -> 16; matrix products, arithmetic and copies ran while one was open for 4% -> 3% of each run, Pallas kernels for 0% -> 0%
where the time goes in v1:
time: 192 us; the launch traced here: 189 us
  waiting for transfers between devices  126 us (66%)
  starting transfers between devices  46 us (24%)
  matrix products  7.18 us (4%)
  other arithmetic  6.02 us (3%)
  local copies, waits for them, and re-layouts  2.65 us (1%)
    ppermute x3, waiting for transfers between devices, body(): lax.ppermute(send_up.astype(jnp.bfloat16), 'dp', layer_moves(1, lambda z:...  28.2 us
    ppermute x5, waiting for transfers between devices, swap_x(): return lax.ppermute(piece, 'dp', across)  28.1 us
    ppermute x3, waiting for transfers between devices, body(): lax.ppermute(down[-1], 'dp', layer_moves(-1, lambda z: z <= layers - r))  26.9 us
    ppermute x3, waiting for transfers between devices, body(): lax.ppermute(send_down.astype(jnp.bfloat16), 'dp', layer_moves(-1, lambda...  23.1 us
    ppermute x3, starting transfers between devices, body(): lax.ppermute(send_up.astype(jnp.bfloat16), 'dp', layer_moves(1, lambda z:...  14 us
    ppermute x2, waiting for transfers between devices, swap_mp(): return lax.ppermute(piece, 'mp', [(i, i ^ bit) for i in range(n_mp)])  7.89 us
    ppermute x5, starting transfers between devices, swap_x(): return lax.ppermute(piece, 'dp', across)  7.74 us
    ppermute x3, starting transfers between devices, body(): up.append(lax.ppermute(up[-1], 'dp', layer_moves(1, lambda z: z >= r - 1)))  7.57 us
  transfers between devices with their start and end apart: 23, of which 16 were waited for; matrix products, arithmetic and copies ran while one was open for 3% of the time, Pallas kernels for 0%

profile of v1, /device:TPU:0, one launch (start us, length us, event | category | flops | bytes accessed | tf_op | source)
XLA Modules:
  0.0 188.9 jit_solution(8801975739079639194)
XLA Ops:
  0.7 1.1 dynamic-slice_bitcast_fusion
  1.8 3.1 %collective-permute-start = (bf16[64,768]{1,0:T(8,128)(2,1)S(1)}, bf16[64,768]{1,0:T(8,128)(2,1)S(1)}, u32[]{:S(2)}, u32[]{:S(2)}) collective-permute-start(bf16[64,768]{1,0:T(8,128)(2,1)S(1)} %get-tuple-element.25), channel_id=1, source_target_pairs={{0,8},{4,12},{8,16},{12,20},{16,24},{20,28},{24,0},{28,4},{1,9},{5... | collective-permute-start | bytes 294920 | tf_op jit(solution)/shard_map/ppermute | solution.py:67
  4.9 2.6 %collective-permute-start.1 = (bf16[64,768]{1,0:T(8,128)(2,1)S(1)}, bf16[64,768]{1,0:T(8,128)(2,1)S(1)}, u32[]{:S(2)}, u32[]{:S(2)}) collective-permute-start(bf16[64,768]{1,0:T(8,128)(2,1)S(1)} %get-tuple-element.27), channel_id=1, source_target_pairs={{0,16},{4,20},{8,24},{12,28},{16,0},{20,4},{24,8},{28,12},{1,17},{... | collective-permute-start | bytes 294920 | tf_op jit(solution)/shard_map/ppermute | solution.py:67
  7.5 1.3 collective-permute-start.2
  8.8 1.7 collective-permute-done
  10.6 3.5 %collective-permute-done.1 = bf16[64,768]{1,0:T(8,128)(2,1)S(1)} collective-permute-done((bf16[64,768]{1,0:T(8,128)(2,1)S(1)}, bf16[64,768]{1,0:T(8,128)(2,1)S(1)}, u32[]{:S(2)}, u32[]{:S(2)}) %collective-permute-start.1) | collective-permute-done | bytes 98336 | tf_op jit(solution)/shard_map/ppermute | solution.py:67
  14.2 1.6 collective-permute-start.3
  15.8 1.5 collective-permute-start.4
  17.2 7.9 %collective-permute-done.3 = bf16[4,64,768]{2,1,0:T(8,128)(2,1)S(1)} collective-permute-done((bf16[4,64,768]{2,1,0:T(8,128)(2,1)S(1)}, bf16[4,64,768]{2,1,0:T(8,128)(2,1)S(1)}, u32[]{:S(2)}, u32[]{:S(2)}) %collective-permute-start.3) | collective-permute-done | bytes 393248 | tf_op jit(solution)/shard_map/ppermute | solution.py:59
  25.1 1.2 collective-permute-done.4
  26.4 1.6 collective-permute-start.5
  28.0 6.3 %collective-permute-done.5 = bf16[4,64,768]{2,1,0:T(8,128)(2,1)S(1)} collective-permute-done((bf16[4,64,768]{2,1,0:T(8,128)(2,1)S(1)}, bf16[4,64,768]{2,1,0:T(8,128)(2,1)S(1)}, u32[]{:S(2)}, u32[]{:S(2)}) %collective-permute-start.5) | collective-permute-done | bytes 393248 | tf_op jit(solution)/shard_map/ppermute | solution.py:98
  34.4 1.6 pad_maximum_fusion
  36.2 1.6 collective-permute-start.7
  37.7 10.0 %collective-permute-done.7 = bf16[512,384]{1,0:T(8,128)(2,1)S(1)} collective-permute-done((bf16[512,384]{1,0:T(8,128)(2,1)S(1)}, bf16[512,384]{1,0:T(8,128)(2,1)S(1)}, u32[]{:S(2)}, u32[]{:S(2)}) %collective-permute-start.7) | collective-permute-done | bytes 393248 | tf_op jit(solution)/shard_map/ppermute | solution.py:56
  48.0 1.6 fusion.5
  50.2 4.6 %collective-permute-start.8 = (bf16[512,512]{0,1:T(8,128)(2,1)S(1)}, bf16[512,512]{0,1:T(8,128)(2,1)S(1)}, u32[]{:S(2)}, u32[]{:S(2)}) collective-permute-start(bf16[512,512]{0,1:T(8,128)(2,1)S(1)} %get-tuple-element.28), channel_id=1, source_target_pairs={{0,8},{4,12},{1,9},{5,13},{2,10},{6,14},{3,11},{7,15}} | collective-permute-start | bytes 1572872 | tf_op jit(solution)/shard_map/ppermute | solution.py:134
  55.5 10.4 %collective-permute-done.8 = bf16[512,512]{0,1:T(8,128)(2,1)S(1)} collective-permute-done((bf16[512,512]{0,1:T(8,128)(2,1)S(1)}, bf16[512,512]{0,1:T(8,128)(2,1)S(1)}, u32[]{:S(2)}, u32[]{:S(2)}) %collective-permute-start.8) | collective-permute-done | bytes 524320 | tf_op jit(solution)/shard_map/ppermute | solution.py:134
  66.1 4.4 %collective-permute-start.9 = (bf16[512,512]{0,1:T(8,128)(2,1)S(1)}, bf16[512,512]{0,1:T(8,128)(2,1)S(1)}, u32[]{:S(2)}, u32[]{:S(2)}) collective-permute-start(bf16[512,512]{0,1:T(8,128)(2,1)S(1)} %add_convert_fusion.3), channel_id=1, source_target_pairs={{0,8},{4,12},{8,16},{12,20},{1,9},{5,13},{9,17},{13,21},{2,10},{6,... | collective-permute-start | bytes 1572872 | tf_op jit(solution)/shard_map/ppermute | solution.py:134
  70.5 10.1 %collective-permute-done.9 = bf16[512,512]{0,1:T(8,128)(2,1)S(1)} collective-permute-done((bf16[512,512]{0,1:T(8,128)(2,1)S(1)}, bf16[512,512]{0,1:T(8,128)(2,1)S(1)}, u32[]{:S(2)}, u32[]{:S(2)}) %collective-permute-start.9) | collective-permute-done | bytes 524320 | tf_op jit(solution)/shard_map/ppermute | solution.py:134
  81.3 0.7 collective-permute-start.11
  82.2 0.7 collective-permute-start.12
  82.9 5.0 %collective-permute-start.10 = (bf16[512,512]{0,1:T(8,128)(2,1)S(1)}, bf16[512,512]{0,1:T(8,128)(2,1)S(1)}, u32[]{:S(2)}, u32[]{:S(2)}) collective-permute-start(bf16[512,512]{0,1:T(8,128)(2,1)S(1)} %get-tuple-element.16), channel_id=1, source_target_pairs={{0,8},{4,12},{8,16},{12,20},{16,24},{20,28},{1,9},{5,13},{9,17},{1... | collective-permute-start | bytes 1572872 | tf_op jit(solution)/shard_map/ppermute | solution.py:134
  88.1 1.3 collective-permute-start.13
  89.4 7.7 %collective-permute-done.10 = bf16[512,512]{0,1:T(8,128)(2,1)S(1)} collective-permute-done((bf16[512,512]{0,1:T(8,128)(2,1)S(1)}, bf16[512,512]{0,1:T(8,128)(2,1)S(1)}, u32[]{:S(2)}, u32[]{:S(2)}) %collective-permute-start.10) | collective-permute-done | bytes 524320 | tf_op jit(solution)/shard_map/ppermute | solution.py:134
  97.1 23.1 %collective-permute-done.13 = bf16[512,512]{0,1:T(8,128)(2,1)S(1)} collective-permute-done((bf16[512,512]{0,1:T(8,128)(2,1)S(1)}, bf16[512,512]{0,1:T(8,128)(2,1)S(1)}, u32[]{:S(2)}, u32[]{:S(2)}) %collective-permute-start.13) | collective-permute-done | bytes 524320 | tf_op jit(solution)/shard_map/ppermute | solution.py:137
  120.2 0.6 fusion.2
  120.9 1.6 collective-permute-start.14
  122.5 6.6 %collective-permute-done.14 = bf16[256,512]{0,1:T(8,128)(2,1)S(1)} collective-permute-done((bf16[256,512]{0,1:T(8,128)(2,1)S(1)}, bf16[256,512]{0,1:T(8,128)(2,1)S(1)}, u32[]{:S(2)}, u32[]{:S(2)}) %collective-permute-start.14) | collective-permute-done | bytes 262176 | tf_op jit(solution)/shard_map/ppermute | solution.py:56
  129.8 1.6 collective-permute-start.15
  131.4 4.9 %collective-permute-done.15 = bf16[256,512]{1,0:T(8,128)(2,1)S(1)} collective-permute-done((bf16[256,512]{1,0:T(8,128)(2,1)S(1)}, bf16[256,512]{1,0:T(8,128)(2,1)S(1)}, u32[]{:S(2)}, u32[]{:S(2)}) %collective-permute-start.15) | collective-permute-done | bytes 262176 | tf_op jit(solution)/shard_map/ppermute | solution.py:56
  136.3 1.3 collective-permute-start.17
  137.6 5.4 %collective-permute-start.16 = (bf16[512,512]{1,0:T(8,128)(2,1)S(1)}, bf16[512,512]{1,0:T(8,128)(2,1)}, u32[]{:S(2)}, u32[]{:S(2)}) collective-permute-start(bf16[512,512]{1,0:T(8,128)(2,1)S(1)} %pad_maximum_fusion.5), channel_id=1, source_target_pairs={{0,8},{4,12},{8,16},{12,20},{16,24},{20,28},{1,9},{5,13},{9,17},{1... | collective-permute-start | bytes 1572872 | tf_op jit(solution)/shard_map/ppermute | solution.py:108
  143.0 7.1 %collective-permute-done.17 = bf16[512,512]{1,0:T(8,128)(2,1)} collective-permute-done((bf16[512,512]{1,0:T(8,128)(2,1)S(1)}, bf16[512,512]{1,0:T(8,128)(2,1)}, u32[]{:S(2)}, u32[]{:S(2)}) %collective-permute-start.17) | collective-permute-done | bytes 524320 | tf_op jit(solution)/shard_map/ppermute | solution.py:109
  150.2 1.3 collective-permute-start.18
  151.5 1.5 collective-permute-start.20
  152.9 12.9 %collective-permute-done.18 = bf16[512,512]{1,0:T(8,128)(2,1)} collective-permute-done((bf16[512,512]{1,0:T(8,128)(2,1)}, bf16[512,512]{1,0:T(8,128)(2,1)}, u32[]{:S(2)}, u32[]{:S(2)}) %collective-permute-start.18) | collective-permute-done | bytes 524320 | tf_op jit(solution)/shard_map/ppermute | solution.py:109
  165.8 1.3 collective-permute-start.19
  167.1 0.6 fusion.17
  167.7 0.7 collective-permute-start.21
  168.4 1.7 fusion.7
  170.1 6.9 %collective-permute-done.19 = bf16[512,512]{1,0:T(8,128)(2,1)S(1)} collective-permute-done((bf16[512,512]{1,0:T(8,128)(2,1)}, bf16[512,512]{1,0:T(8,128)(2,1)S(1)}, u32[]{:S(2)}, u32[]{:S(2)}) %collective-permute-start.19) | collective-permute-done | bytes 524320 | tf_op jit(solution)/shard_map/ppermute | solution.py:109
  177.1 0.6 fusion.9
  177.7 1.8 multiply_convert_fusion
  179.6 1.6 collective-permute-start.22
  181.2 0.9 reverse_select_fusion.2
  182.1 5.4 %collective-permute-done.22 = bf16[384,512]{0,1:T(8,128)(2,1)S(1)} collective-permute-done((bf16[384,512]{0,1:T(8,128)(2,1)S(1)}, bf16[384,512]{0,1:T(8,128)(2,1)S(1)}, u32[]{:S(2)}, u32[]{:S(2)}) %collective-permute-start.22) | collective-permute-done | bytes 393248 | tf_op jit(solution)/shard_map/ppermute | solution.py:56
  187.7 1.2 copy.26
  (46 shorter events, 4.2 us)
Async XLA Ops:
  1.8 8.8 %collective-permute-start = (bf16[64,768]{1,0:T(8,128)(2,1)S(1)}, bf16[64,768]{1,0:T(8,128)(2,1)S(1)}, u32[]{:S(2)}, u32[]{:S(2)}) collective-permute-start(bf16[64,768]{1,0:T(8,128)(2,1)S(1)} %get-tuple-element.25), channel_id=1, source_target_pairs={{0,8},{4,12},{8,16},{12,20},{16,24},{20,28},{24,0},{28,4},{1,9},{5... | collective-permute-start | bytes 294920 | tf_op jit(solution)/shard_map/ppermute | solution.py:67
  4.9 9.2 %collective-permute-start.1 = (bf16[64,768]{1,0:T(8,128)(2,1)S(1)}, bf16[64,768]{1,0:T(8,128)(2,1)S(1)}, u32[]{:S(2)}, u32[]{:S(2)}) collective-permute-start(bf16[64,768]{1,0:T(8,128)(2,1)S(1)} %get-tuple-element.27), channel_id=1, source_target_pairs={{0,16},{4,20},{8,24},{12,28},{16,0},{20,4},{24,8},{28,12},{1,17},{... | collective-permute-start | bytes 294920 | tf_op jit(solution)/shard_map/ppermute | solution.py:67
  7.5 6.6 %collective-permute-start.2 = (bf16[64,768]{1,0:T(8,128)(2,1)S(1)}, bf16[64,768]{1,0:T(8,128)(2,1)S(1)}, u32[]{:S(2)}, u32[]{:S(2)}) collective-permute-start(bf16[64,768]{1,0:T(8,128)(2,1)S(1)} %get-tuple-element.26), channel_id=1, source_target_pairs={{0,24},{4,28},{8,0},{12,4},{16,8},{20,12},{24,16},{28,20},{1,25},{... | collective-permute-start | bytes 294920 | tf_op jit(solution)/shard_map/ppermute | solution.py:67
  14.2 11.0 %collective-permute-start.3 = (bf16[4,64,768]{2,1,0:T(8,128)(2,1)S(1)}, bf16[4,64,768]{2,1,0:T(8,128)(2,1)S(1)}, u32[]{:S(2)}, u32[]{:S(2)}) collective-permute-start(bf16[4,64,768]{2,1,0:T(8,128)(2,1)S(1)} %get-tuple-element.23), channel_id=1, source_target_pairs={{0,2},{1,3},{2,0},{3,1},{4,6},{5,7},{6,4},{7,5},{8,10},{9,11},{10,... | collective-permute-start | bytes 1179656 | tf_op jit(solution)/shard_map/ppermute | solution.py:59
  15.8 10.6 %collective-permute-start.4 = (bf16[4,64,768]{2,1,0:T(8,128)(2,1)S(1)}, bf16[4,64,768]{2,1,0:T(8,128)(2,1)S(1)}, u32[]{:S(2)}, u32[]{:S(2)}) collective-permute-start(bf16[4,64,768]{2,1,0:T(8,128)(2,1)S(1)} %get-tuple-element.23), channel_id=1, source_target_pairs={{0,4},{4,0},{8,12},{12,8},{16,20},{20,16},{24,28},{28,24},{1,5},{5... | collective-permute-start | bytes 1179656 | tf_op jit(solution)/shard_map/ppermute | solution.py:56
  26.4 7.8 %collective-permute-start.5 = (bf16[4,64,768]{2,1,0:T(8,128)(2,1)S(1)}, bf16[4,64,768]{2,1,0:T(8,128)(2,1)S(1)}, u32[]{:S(2)}, u32[]{:S(2)}) collective-permute-start(bf16[4,64,768]{2,1,0:T(8,128)(2,1)S(1)} %broadcast_select_fusion.4), channel_id=1, source_target_pairs={{0,4},{1,3},{2,6},{3,1},{4,0},{5,7},{6,2},{7,5},{8,12},{9,11},{10,... | collective-permute-start | bytes 1179656 | tf_op jit(solution)/shard_map/ppermute | solution.py:98
  34.3 1.6 copy-start.6
  34.4 1.6 copy-start.4
  35.9 12.0 %collective-permute-start.6 = (bf16[4,2,2,64,768]{4,3,2,1,0:T(8,128)(2,1)}, bf16[4,2,2,64,768]{4,3,2,1,0:T(8,128)(2,1)}, u32[]{:S(2)}, u32[]{:S(2)}) collective-permute-start(bf16[4,2,2,64,768]{4,3,2,1,0:T(8,128)(2,1)} %get-tuple-element.10), channel_id=1, source_target_pairs={{0,1},{1,0},{2,3},{3,2},{4,5},{5,4},{6,7},{7,6},{8,9},{9,8},{10,11... | collective-permute-start | bytes 4718600 | tf_op jit(solution)/shard_map/ppermute | solution.py:59
  36.2 11.6 %collective-permute-start.7 = (bf16[512,384]{1,0:T(8,128)(2,1)S(1)}, bf16[512,384]{1,0:T(8,128)(2,1)S(1)}, u32[]{:S(2)}, u32[]{:S(2)}) collective-permute-start(bf16[512,384]{1,0:T(8,128)(2,1)S(1)} %constant_dynamic-slice_fusion.3), channel_id=1, source_target_pairs={{0,4},{4,0},{8,12},{12,8},{16,20},{20,16},{24,28},{28,24},{1,5},{5... | collective-permute-start | bytes 1179656 | tf_op jit(solution)/shard_map/ppermute | solution.py:56
  49.6 31.0 %copy-start.2 = (bf16[1,2,2,2,64,768]{5,4,3,2,1,0:T(8,128)(2,1)}, bf16[1,2,2,2,64,768]{5,4,3,2,1,0:T(8,128)(2,1)S(1)}, u32[]{:S(2)}) copy-start(bf16[1,2,2,2,64,768]{5,4,3,2,1,0:T(8,128)(2,1)S(1)} %get-tuple-element.6) | copy-start | bytes 2359300
  49.6 70.6 %copy-start = (bf16[1,2,2,2,64,768]{5,4,3,2,1,0:T(8,128)(2,1)}, bf16[1,2,2,2,64,768]{5,4,3,2,1,0:T(8,128)(2,1)S(1)}, u32[]{:S(2)}) copy-start(bf16[1,2,2,2,64,768]{5,4,3,2,1,0:T(8,128)(2,1)S(1)} %get-tuple-element.7) | copy-start | bytes 2359300
  50.2 15.6 %collective-permute-start.8 = (bf16[512,512]{0,1:T(8,128)(2,1)S(1)}, bf16[512,512]{0,1:T(8,128)(2,1)S(1)}, u32[]{:S(2)}, u32[]{:S(2)}) collective-permute-start(bf16[512,512]{0,1:T(8,128)(2,1)S(1)} %get-tuple-element.28), channel_id=1, source_target_pairs={{0,8},{4,12},{1,9},{5,13},{2,10},{6,14},{3,11},{7,15}} | collective-permute-start | bytes 1572872 | tf_op jit(solution)/shard_map/ppermute | solution.py:134
  66.1 14.6 %collective-permute-start.9 = (bf16[512,512]{0,1:T(8,128)(2,1)S(1)}, bf16[512,512]{0,1:T(8,128)(2,1)S(1)}, u32[]{:S(2)}, u32[]{:S(2)}) collective-permute-start(bf16[512,512]{0,1:T(8,128)(2,1)S(1)} %add_convert_fusion.3), channel_id=1, source_target_pairs={{0,8},{4,12},{8,16},{12,20},{1,9},{5,13},{9,17},{13,21},{2,10},{6,... | collective-permute-start | bytes 1572872 | tf_op jit(solution)/shard_map/ppermute | solution.py:134
  81.3 0.7 collective-permute-start.11
  82.2 5.7 %collective-permute-start.12 = (bf16[512,512]{0,1:T(8,128)(2,1)S(1)}, bf16[512,512]{0,1:T(8,128)(2,1)S(1)}, u32[]{:S(2)}, u32[]{:S(2)}) collective-permute-start(bf16[512,512]{0,1:T(8,128)(2,1)S(1)} %add_convert_fusion.1), channel_id=1, source_target_pairs={{16,8},{20,12},{24,16},{28,20},{17,9},{21,13},{25,17},{29,21},{18,... | collective-permute-start | bytes 1572872 | tf_op jit(solution)/shard_map/ppermute | solution.py:137
  82.9 14.2 %collective-permute-start.10 = (bf16[512,512]{0,1:T(8,128)(2,1)S(1)}, bf16[512,512]{0,1:T(8,128)(2,1)S(1)}, u32[]{:S(2)}, u32[]{:S(2)}) collective-permute-start(bf16[512,512]{0,1:T(8,128)(2,1)S(1)} %get-tuple-element.16), channel_id=1, source_target_pairs={{0,8},{4,12},{8,16},{12,20},{16,24},{20,28},{1,9},{5,13},{9,17},{1... | collective-permute-start | bytes 1572872 | tf_op jit(solution)/shard_map/ppermute | solution.py:134
  88.1 32.1 %collective-permute-start.13 = (bf16[512,512]{0,1:T(8,128)(2,1)S(1)}, bf16[512,512]{0,1:T(8,128)(2,1)S(1)}, u32[]{:S(2)}, u32[]{:S(2)}) collective-permute-start(bf16[512,512]{0,1:T(8,128)(2,1)S(1)} %add_convert_fusion), channel_id=1, source_target_pairs={{8,0},{12,4},{16,8},{20,12},{24,16},{28,20},{9,1},{13,5},{17,9},{2... | collective-permute-start | bytes 1572872 | tf_op jit(solution)/shard_map/ppermute | solution.py:137
  120.9 8.1 %collective-permute-start.14 = (bf16[256,512]{0,1:T(8,128)(2,1)S(1)}, bf16[256,512]{0,1:T(8,128)(2,1)S(1)}, u32[]{:S(2)}, u32[]{:S(2)}) collective-permute-start(bf16[256,512]{0,1:T(8,128)(2,1)S(1)} %slice.39), channel_id=1, source_target_pairs={{0,4},{4,0},{8,12},{12,8},{16,20},{20,16},{24,28},{28,24},{1,5},{5... | collective-permute-start | bytes 786440 | tf_op jit(solution)/shard_map/ppermute | solution.py:56
  122.5 6.9 %copy-start.5 = (bf16[256,1024]{1,0:T(8,128)(2,1)S(1)}, bf16[256,1024]{1,0:T(8,128)(2,1)}, u32[]{:S(2)}) copy-start(bf16[256,1024]{1,0:T(8,128)(2,1)} %param.5) | copy-start | bytes 1572868
  129.6 37.5 %copy-start.1 = (bf16[1,2,2,2,64,768]{5,4,3,2,1,0:T(8,128)(2,1)S(1)}, bf16[1,2,2,2,64,768]{5,4,3,2,1,0:T(8,128)(2,1)}, u32[]{:S(2)}) copy-start(bf16[1,2,2,2,64,768]{5,4,3,2,1,0:T(8,128)(2,1)} %copy-done) | copy-start | bytes 2359300
  129.8 6.4 %collective-permute-start.15 = (bf16[256,512]{1,0:T(8,128)(2,1)S(1)}, bf16[256,512]{1,0:T(8,128)(2,1)S(1)}, u32[]{:S(2)}, u32[]{:S(2)}) collective-permute-start(bf16[256,512]{1,0:T(8,128)(2,1)S(1)} %get-tuple-element.21), channel_id=1, source_target_pairs={{0,4},{4,0},{8,12},{12,8},{16,20},{20,16},{24,28},{28,24},{1,5},{5... | collective-permute-start | bytes 786440 | tf_op jit(solution)/shard_map/ppermute | solution.py:56
  136.3 13.9 %collective-permute-start.17 = (bf16[512,512]{1,0:T(8,128)(2,1)S(1)}, bf16[512,512]{1,0:T(8,128)(2,1)}, u32[]{:S(2)}, u32[]{:S(2)}) collective-permute-start(bf16[512,512]{1,0:T(8,128)(2,1)S(1)} %pad_maximum_fusion.5), channel_id=1, source_target_pairs={{8,0},{12,4},{16,8},{20,12},{24,16},{28,20},{9,1},{13,5},{17,9},{2... | collective-permute-start | bytes 1572872 | tf_op jit(solution)/shard_map/ppermute | solution.py:109
  137.6 13.8 %collective-permute-start.16 = (bf16[512,512]{1,0:T(8,128)(2,1)S(1)}, bf16[512,512]{1,0:T(8,128)(2,1)}, u32[]{:S(2)}, u32[]{:S(2)}) collective-permute-start(bf16[512,512]{1,0:T(8,128)(2,1)S(1)} %pad_maximum_fusion.5), channel_id=1, source_target_pairs={{0,8},{4,12},{8,16},{12,20},{16,24},{20,28},{1,9},{5,13},{9,17},{1... | collective-permute-start | bytes 1572872 | tf_op jit(solution)/shard_map/ppermute | solution.py:108
  150.2 15.6 %collective-permute-start.18 = (bf16[512,512]{1,0:T(8,128)(2,1)}, bf16[512,512]{1,0:T(8,128)(2,1)}, u32[]{:S(2)}, u32[]{:S(2)}) collective-permute-start(bf16[512,512]{1,0:T(8,128)(2,1)} %collective-permute-done.17), channel_id=1, source_target_pairs={{8,0},{12,4},{16,8},{20,12},{9,1},{13,5},{17,9},{21,13},{10,2},{14... | collective-permute-start | bytes 1572872 | tf_op jit(solution)/shard_map/ppermute | solution.py:109
  151.5 16.3 %collective-permute-start.20 = (bf16[512,512]{1,0:T(8,128)(2,1)}, bf16[512,512]{1,0:T(8,128)(2,1)}, u32[]{:S(2)}, u32[]{:S(2)}) collective-permute-start(bf16[512,512]{1,0:T(8,128)(2,1)} %collective-permute-done.16), channel_id=1, source_target_pairs={{8,16},{12,20},{16,24},{20,28},{9,17},{13,21},{17,25},{21,29},{10,... | collective-permute-start | bytes 1572872 | tf_op jit(solution)/shard_map/ppermute | solution.py:108
  165.8 11.3 %collective-permute-start.19 = (bf16[512,512]{1,0:T(8,128)(2,1)}, bf16[512,512]{1,0:T(8,128)(2,1)S(1)}, u32[]{:S(2)}, u32[]{:S(2)}) collective-permute-start(bf16[512,512]{1,0:T(8,128)(2,1)} %collective-permute-done.18), channel_id=1, source_target_pairs={{8,0},{12,4},{9,1},{13,5},{10,2},{14,6},{11,3},{15,7}} | collective-permute-start | bytes 1572872 | tf_op jit(solution)/shard_map/ppermute | solution.py:109
  167.7 10.0 %collective-permute-start.21 = (bf16[512,512]{1,0:T(8,128)(2,1)}, bf16[512,512]{1,0:T(8,128)(2,1)S(1)}, u32[]{:S(2)}, u32[]{:S(2)}) collective-permute-start(bf16[512,512]{1,0:T(8,128)(2,1)} %collective-permute-done.20), channel_id=1, source_target_pairs={{16,24},{20,28},{17,25},{21,29},{18,26},{22,30},{19,27},{23,31}} | collective-permute-start | bytes 1572872 | tf_op jit(solution)/shard_map/ppermute | solution.py:108
  170.1 7.6 %copy-start.3 = (bf16[1,2,2,2,64,768]{5,4,3,2,1,0:T(8,128)(2,1)S(1)}, bf16[1,2,2,2,64,768]{5,4,3,2,1,0:T(8,128)(2,1)}, u32[]{:S(2)}) copy-start(bf16[1,2,2,2,64,768]{5,4,3,2,1,0:T(8,128)(2,1)} %copy-done.2) | copy-start | bytes 2359300
  179.6 7.8 %collective-permute-start.22 = (bf16[384,512]{0,1:T(8,128)(2,1)S(1)}, bf16[384,512]{0,1:T(8,128)(2,1)S(1)}, u32[]{:S(2)}, u32[]{:S(2)}) collective-permute-start(bf16[384,512]{0,1:T(8,128)(2,1)S(1)} %constant_dynamic-slice_fusion), channel_id=1, source_target_pairs={{0,4},{4,0},{8,12},{12,8},{16,20},{20,16},{24,28},{28,24},{1,5},{5... | collective-permute-start | bytes 1179656 | tf_op jit(solution)/shard_map/ppermute | solution.py:56

commit v2 on v1

--- a/solution.py
+++ b/solution.py
@@ -87,6 +87,7 @@
     weight_other = swap_x(lax.dynamic_slice_in_dim(weight, (1 - side) * half, half, 0))
     weight_slab = halves(weight_own, weight_other, side, 1)
 
+    own, attn_layer, weight_slab = lax.optimization_barrier((own, attn_layer, weight_slab))
     top = n_mp // 2
     via_x = swap_x(own)
     via_mp = swap_mp(own, top)
@@ -107,6 +108,25 @@
     for r in range(1, layers):
         up.append(lax.ppermute(up[-1], "dp", layer_moves(1, lambda z: z >= r - 1)))
         down.append(lax.ppermute(down[-1], "dp", layer_moves(-1, lambda z: z <= layers - r)))
+
+    def terms(r):
+        return lax.dot_general(
+            columns[r], weight_slab, (((1,), (1,)), ((), ())), preferred_element_type=jnp.float32
+        )
+
+    parts = [terms(r) for r in range(layers)]
+    carried = jnp.bfloat16 if layers <= 4 else jnp.float32
+    from_below = from_above = None
+    for k in range(1, layers):
+        send_up, send_down = parts[k], parts[layers - k]
+        if k > 1:
+            send_up = send_up + from_below.astype(jnp.float32)
+            send_down = send_down + from_above.astype(jnp.float32)
+        send_up, send_down, up[k], down[k] = lax.optimization_barrier(
+            (send_up.astype(carried), send_down.astype(carried), up[k], down[k])
+        )
+        from_below = lax.ppermute(send_up, "dp", layer_moves(1, lambda z: z <= k - 1))
+        from_above = lax.ppermute(send_down, "dp", layer_moves(-1, lambda z: z >= layers - k))
     total = None
     for r in range(layers):
         rows_r = attn_layer if r == 0 else jnp.where(layer >= r, up[r], down[layers - r])
@@ -119,24 +139,6 @@
     gw_other = swap_x(lax.dynamic_slice_in_dim(gw, (1 - side) * own_features, own_features, 0))
     grad_weight_t = halves(gw_own, gw_other, side, 1)
 
-    def terms(r):
-        return lax.dot_general(
-            columns[r], weight_slab, (((1,), (1,)), ((), ())), preferred_element_type=jnp.float32
-        )
-
-    parts = [terms(r) for r in range(layers)]
-    from_below = from_above = None
-    for k in range(1, layers):
-        send_up, send_down = parts[k], parts[layers - k]
-        if k > 1:
-            send_up = send_up + from_below.astype(jnp.float32)
-            send_down = send_down + from_above.astype(jnp.float32)
-        from_below = lax.ppermute(
-            send_up.astype(jnp.bfloat16), "dp", layer_moves(1, lambda z: z <= k - 1)
-        )
-        from_above = lax.ppermute(
-            send_down.astype(jnp.bfloat16), "dp", layer_moves(-1, lambda z: z >= layers - k)
-        )
     ga = parts[0] + from_below.astype(jnp.float32) + from_above.astype(jnp.float32)
     ga = ga.astype(jnp.bfloat16)
     ga_other = swap_x(ga[group_rows:])

time: 192 us -> 126 us (0.66); the launches traced: 189 us -> 126 us
  waiting for transfers between devices: 126 us -> 58.6 us
  matrix products: 7.18 us -> 10.8 us
  starting transfers between devices: 46 us -> 48.1 us
    ppermute x6, waiting for transfers between devices: 51.4 us -> 15.2 us  [the longest x3 12.8 us: body(): lax.ppermute(send_up, 'dp', layer_moves(1, lambda z: z <= k - 1))]
    ppermute x5, waiting for transfers between devices: 28.1 us -> 6.41 us  [swap_x(): return lax.ppermute(piece, 'dp', across)]
    ppermute x3, waiting for transfers between devices: 26.9 us -> 6.52 us  [body(): lax.ppermute(down[-1], 'dp', layer_moves(-1, lambda z: z <= layers - r))]
    ppermute x3, waiting for transfers between devices: 0.01 us -> 9.73 us  [body(): up.append(lax.ppermute(up[-1], 'dp', layer_moves(1, lambda z: z >= r - 1)))]
    ppermute x6, starting transfers between devices: 16.7 us -> 21.7 us  [the longest x3 18 us: body(): lax.ppermute(send_up, 'dp', layer_moves(1, lambda z: z <= k - 1))]
    dot_general x4, matrix products: 2.44 us -> 6.01 us  [terms(): lax.dot_general(columns[r], weight_slab, (((1,), (1,)), ((), ())), prefer...]
    ppermute x3, waiting for transfers between devices: 5.27 us -> 7.34 us  [body(): lax.ppermute(piece, 'dp', [(z * PAIR + x, (z + r) % layers * PAIR + x) fo...]
    ppermute x3, starting transfers between devices: 7.01 us -> 5.07 us  [body(): lax.ppermute(piece, 'dp', [(z * PAIR + x, (z + r) % layers * PAIR + x) fo...]
  transfers between devices with their start and end apart: 23 -> 23, of which waited for: 16 -> 15; matrix products, arithmetic and copies ran while one was open for 3% -> 11% of each run, Pallas kernels for 0% -> 0%
where the time goes in v2:
time: 126 us
  waiting for transfers between devices  58.6 us (47%)
  starting transfers between devices  48.1 us (38%)
  matrix products  10.8 us (9%)
  other arithmetic  5.57 us (4%)
  local copies, waits for them, and re-layouts  1.63 us (1%)
    ppermute x3, starting transfers between devices, body(): lax.ppermute(send_up, 'dp', layer_moves(1, lambda z: z <= k - 1))  18 us
    ppermute x3, waiting for transfers between devices, body(): lax.ppermute(send_up, 'dp', layer_moves(1, lambda z: z <= k - 1))  12.8 us
    ppermute x3, waiting for transfers between devices, body(): up.append(lax.ppermute(up[-1], 'dp', layer_moves(1, lambda z: z >= r - 1)))  9.73 us
    ppermute x5, starting transfers between devices, swap_x(): return lax.ppermute(piece, 'dp', across)  7.63 us
    ppermute x3, waiting for transfers between devices, body(): lax.ppermute(piece, 'dp', [(z * PAIR + x, (z + r) % layers * PAIR + x) fo...  7.34 us
    ppermute x2, waiting for transfers between devices, swap_mp(): return lax.ppermute(piece, 'mp', [(i, i ^ bit) for i in range(n_mp)])  7.04 us
    ppermute x3, waiting for transfers between devices, body(): lax.ppermute(down[-1], 'dp', layer_moves(-1, lambda z: z <= layers - r))  6.52 us
    ppermute x3, starting transfers between devices, body(): up.append(lax.ppermute(up[-1], 'dp', layer_moves(1, lambda z: z >= r - 1)))  6.42 us
  transfers between devices with their start and end apart: 23, of which 15 were waited for; matrix products, arithmetic and copies ran while one was open for 11% of the time, Pallas kernels for 0%

profile of v2, /device:TPU:0, one launch (start us, length us, event | category | flops | bytes accessed | tf_op | source)
XLA Modules:
  0.0 125.9 jit_solution(16045176886810691548)
XLA Ops:
  0.7 1.5 %reverse_select_fusion.3 = bf16[2,2,64,1024]{3,2,1,0:T(8,128)(2,1)S(1)} fusion(bf16[2,2,64,1024]{3,2,1,0:T(8,128)(2,1)} %bitcast.61, pred[]{:T(512)S(6)} %eq.27), kind=kLoop, calls=%fused_computation.26 | loop fusion | flops 262144 | bytes 1048577 | tf_op jit(solution)/shard_map/jit(_where)/select_n | solution.py:21
  2.4 3.0 %collective-permute-start.3 = (bf16[256,512]{1,0:T(8,128)(2,1)S(1)}, bf16[256,512]{1,0:T(8,128)(2,1)}, u32[]{:S(2)}, u32[]{:S(2)}) collective-permute-start(bf16[256,512]{1,0:T(8,128)(2,1)S(1)} %get-tuple-element.51), channel_id=1, source_target_pairs={{0,4},{4,0},{8,12},{12,8},{16,20},{20,16},{24,28},{28,24},{1,5},{5... | collective-permute-start | bytes 786440 | tf_op jit(solution)/shard_map/ppermute | solution.py:56
  5.8 4.1 %collective-permute-start.2 = (bf16[64,768]{1,0:T(8,128)(2,1)S(1)}, bf16[64,768]{1,0:T(8,128)(2,1)S(1)}, u32[]{:S(2)}, u32[]{:S(2)}) collective-permute-start(bf16[64,768]{1,0:T(8,128)(2,1)S(1)} %get-tuple-element.54), channel_id=1, source_target_pairs={{0,24},{4,28},{8,0},{12,4},{16,8},{20,12},{24,16},{28,20},{1,25},{... | collective-permute-start | bytes 294920 | tf_op jit(solution)/shard_map/ppermute | solution.py:67
  9.9 1.0 collective-permute-start
  10.9 2.2 %collective-permute-done.2 = bf16[64,768]{1,0:T(8,128)(2,1)S(1)} collective-permute-done((bf16[64,768]{1,0:T(8,128)(2,1)S(1)}, bf16[64,768]{1,0:T(8,128)(2,1)S(1)}, u32[]{:S(2)}, u32[]{:S(2)}) %collective-permute-start.2) | collective-permute-done | bytes 98336 | tf_op jit(solution)/shard_map/ppermute | solution.py:67
  13.1 5.1 %collective-permute-done.1 = bf16[64,768]{1,0:T(8,128)(2,1)S(1)} collective-permute-done((bf16[64,768]{1,0:T(8,128)(2,1)S(1)}, bf16[64,768]{1,0:T(8,128)(2,1)S(1)}, u32[]{:S(2)}, u32[]{:S(2)}) %collective-permute-start.1) | collective-permute-done | bytes 98336 | tf_op jit(solution)/shard_map/ppermute | solution.py:67
  18.3 1.0 pad_maximum_fusion.4
  19.3 0.8 collective-permute-done.4
  20.4 1.8 %collective-permute-start.5 = (bf16[4,64,768]{2,1,0:T(8,128)(2,1)S(1)}, bf16[4,64,768]{2,1,0:T(8,128)(2,1)S(1)}, u32[]{:S(2)}, u32[]{:S(2)}) collective-permute-start(bf16[4,64,768]{2,1,0:T(8,128)(2,1)S(1)} %pad_maximum_fusion.6), channel_id=1, source_target_pairs={{0,2},{1,3},{2,0},{3,1},{4,6},{5,7},{6,4},{7,5},{8,10},{9,11},{10,... | collective-permute-start | bytes 1179656 | tf_op jit(solution)/shard_map/ppermute | solution.py:59
  22.2 1.5 %collective-permute-start.6 = (bf16[4,64,768]{2,1,0:T(8,128)(2,1)S(1)}, bf16[4,64,768]{2,1,0:T(8,128)(2,1)S(1)}, u32[]{:S(2)}, u32[]{:S(2)}) collective-permute-start(bf16[4,64,768]{2,1,0:T(8,128)(2,1)S(1)} %pad_maximum_fusion.6), channel_id=1, source_target_pairs={{0,4},{4,0},{8,12},{12,8},{16,20},{20,16},{24,28},{28,24},{1,5},{5... | collective-permute-start | bytes 1179656 | tf_op jit(solution)/shard_map/ppermute | solution.py:56
  23.7 7.0 %collective-permute-done.5 = bf16[4,64,768]{2,1,0:T(8,128)(2,1)S(1)} collective-permute-done((bf16[4,64,768]{2,1,0:T(8,128)(2,1)S(1)}, bf16[4,64,768]{2,1,0:T(8,128)(2,1)S(1)}, u32[]{:S(2)}, u32[]{:S(2)}) %collective-permute-start.5) | collective-permute-done | bytes 393248 | tf_op jit(solution)/shard_map/ppermute | solution.py:59
  30.7 1.2 collective-permute-done.6
  31.9 1.5 %collective-permute-start.7 = (bf16[4,64,768]{2,1,0:T(8,128)(2,1)S(1)}, bf16[4,64,768]{2,1,0:T(8,128)(2,1)S(1)}, u32[]{:S(2)}, u32[]{:S(2)}) collective-permute-start(bf16[4,64,768]{2,1,0:T(8,128)(2,1)S(1)} %broadcast_select_fusion.2), channel_id=1, source_target_pairs={{0,4},{1,3},{2,6},{3,1},{4,0},{5,7},{6,2},{7,5},{8,12},{9,11},{10,... | collective-permute-start | bytes 1179656 | tf_op jit(solution)/shard_map/ppermute | solution.py:99
  33.5 6.3 %collective-permute-done.7 = bf16[4,64,768]{2,1,0:T(8,128)(2,1)S(1)} collective-permute-done((bf16[4,64,768]{2,1,0:T(8,128)(2,1)S(1)}, bf16[4,64,768]{2,1,0:T(8,128)(2,1)S(1)}, u32[]{:S(2)}, u32[]{:S(2)}) %collective-permute-start.7) | collective-permute-done | bytes 393248 | tf_op jit(solution)/shard_map/ppermute | solution.py:99
  40.2 4.3 %collective-permute-start.9 = (bf16[512,512]{1,0:T(8,128)(2,1)S(1)}, bf16[512,512]{1,0:T(8,128)(2,1)}, u32[]{:S(2)}, u32[]{:S(2)}) collective-permute-start(bf16[512,512]{1,0:T(8,128)(2,1)S(1)} %pad_maximum_fusion.4), channel_id=1, source_target_pairs={{0,8},{4,12},{8,16},{12,20},{16,24},{20,28},{1,9},{5,13},{9,17},{1... | collective-permute-start | bytes 1572872 | tf_op jit(solution)/shard_map/ppermute | solution.py:109
  44.5 1.3 %collective-permute-start.10 = (bf16[512,512]{1,0:T(8,128)(2,1)S(1)}, bf16[512,512]{1,0:T(8,128)(2,1)}, u32[]{:S(2)}, u32[]{:S(2)}) collective-permute-start(bf16[512,512]{1,0:T(8,128)(2,1)S(1)} %pad_maximum_fusion.4), channel_id=1, source_target_pairs={{8,0},{12,4},{16,8},{20,12},{24,16},{28,20},{9,1},{13,5},{17,9},{2... | collective-permute-start | bytes 1572872 | tf_op jit(solution)/shard_map/ppermute | solution.py:110
  45.7 9.7 %collective-permute-done.9 = bf16[512,512]{1,0:T(8,128)(2,1)} collective-permute-done((bf16[512,512]{1,0:T(8,128)(2,1)S(1)}, bf16[512,512]{1,0:T(8,128)(2,1)}, u32[]{:S(2)}, u32[]{:S(2)}) %collective-permute-start.9) | collective-permute-done | bytes 524320 | tf_op jit(solution)/shard_map/ppermute | solution.py:109
  55.5 1.4 %collective-permute-start.13 = (bf16[512,512]{1,0:T(8,128)(2,1)}, bf16[512,512]{1,0:T(8,128)(2,1)}, u32[]{:S(2)}, u32[]{:S(2)}) collective-permute-start(bf16[512,512]{1,0:T(8,128)(2,1)} %collective-permute-done.9), channel_id=1, source_target_pairs={{8,16},{12,20},{16,24},{20,28},{9,17},{13,21},{17,25},{21,29},{10,... | collective-permute-start | bytes 1572872 | tf_op jit(solution)/shard_map/ppermute | solution.py:109
  56.9 3.6 %collective-permute-done.10 = bf16[512,512]{1,0:T(8,128)(2,1)} collective-permute-done((bf16[512,512]{1,0:T(8,128)(2,1)S(1)}, bf16[512,512]{1,0:T(8,128)(2,1)}, u32[]{:S(2)}, u32[]{:S(2)}) %collective-permute-start.10) | collective-permute-done | bytes 524320 | tf_op jit(solution)/shard_map/ppermute | solution.py:110
  60.5 1.3 %collective-permute-start.14 = (bf16[512,512]{1,0:T(8,128)(2,1)}, bf16[512,512]{1,0:T(8,128)(2,1)}, u32[]{:S(2)}, u32[]{:S(2)}) collective-permute-start(bf16[512,512]{1,0:T(8,128)(2,1)} %collective-permute-done.10), channel_id=1, source_target_pairs={{8,0},{12,4},{16,8},{20,12},{9,1},{13,5},{17,9},{21,13},{10,2},{14... | collective-permute-start | bytes 1572872 | tf_op jit(solution)/shard_map/ppermute | solution.py:110
  61.8 0.3 fusion.2
  62.1 1.8 %fusion.14 = (bf16[512,512]{0,1:T(8,128)(2,1)}, f32[512,512]{0,1:T(8,128)}) fusion(bf16[512,768]{1,0:T(8,128)(2,1)S(1)} %bitcast.53, bf16[512,768]{1,0:T(8,128)(2,1)S(1)} %pad_maximum_fusion.2), kind=kOutput, calls=%fused_computation.55 | convolution fusion | flops 402915328 | bytes 3145728 | tf_op jit(solution)/shard_map/dot_general | solution.py:113
  63.8 1.7 %fusion.13 = (bf16[512,512]{0,1:T(8,128)(2,1)}, f32[512,512]{0,1:T(8,128)}) fusion(bf16[512,768]{1,0:T(8,128)(2,1)S(1)} %bitcast.51, bf16[512,768]{1,0:T(8,128)(2,1)S(1)} %pad_maximum_fusion.2), kind=kOutput, calls=%fused_computation.54 | convolution fusion | flops 402915328 | bytes 3145728 | tf_op jit(solution)/shard_map/dot_general | solution.py:113
  65.6 1.4 %collective-permute-start.12 = (bf16[512,512]{0,1:T(8,128)(2,1)}, bf16[512,512]{0,1:T(8,128)(2,1)}, u32[]{:S(2)}, u32[]{:S(2)}) collective-permute-start(bf16[512,512]{0,1:T(8,128)(2,1)} %get-tuple-element.21), channel_id=1, source_target_pairs={{24,16},{28,20},{25,17},{29,21},{26,18},{30,22},{27,19},{31,23}} | collective-permute-start | bytes 1572872 | tf_op jit(solution)/shard_map/ppermute | solution.py:129
  67.0 5.4 %collective-permute-start.11 = (bf16[512,512]{0,1:T(8,128)(2,1)}, bf16[512,512]{0,1:T(8,128)(2,1)}, u32[]{:S(2)}, u32[]{:S(2)}) collective-permute-start(bf16[512,512]{0,1:T(8,128)(2,1)} %get-tuple-element.20), channel_id=1, source_target_pairs={{0,8},{4,12},{1,9},{5,13},{2,10},{6,14},{3,11},{7,15}} | collective-permute-start | bytes 1572872 | tf_op jit(solution)/shard_map/ppermute | solution.py:128
  72.4 0.7 collective-permute-start.17
  73.1 3.0 %collective-permute-done.14 = bf16[512,512]{1,0:T(8,128)(2,1)} collective-permute-done((bf16[512,512]{1,0:T(8,128)(2,1)}, bf16[512,512]{1,0:T(8,128)(2,1)}, u32[]{:S(2)}, u32[]{:S(2)}) %collective-permute-start.14) | collective-permute-done | bytes 524320 | tf_op jit(solution)/shard_map/ppermute | solution.py:110
  76.0 1.3 %collective-permute-start.18 = (bf16[512,512]{1,0:T(8,128)(2,1)}, bf16[512,512]{1,0:T(8,128)(2,1)S(1)}, u32[]{:S(2)}, u32[]{:S(2)}) collective-permute-start(bf16[512,512]{1,0:T(8,128)(2,1)} %collective-permute-done.14), channel_id=1, source_target_pairs={{8,0},{12,4},{9,1},{13,5},{10,2},{14,6},{11,3},{15,7}} | collective-permute-start | bytes 1572872 | tf_op jit(solution)/shard_map/ppermute | solution.py:110
  77.3 5.1 %collective-permute-done.11 = bf16[512,512]{0,1:T(8,128)(2,1)} collective-permute-done((bf16[512,512]{0,1:T(8,128)(2,1)}, bf16[512,512]{0,1:T(8,128)(2,1)}, u32[]{:S(2)}, u32[]{:S(2)}) %collective-permute-start.11) | collective-permute-done | bytes 524320 | tf_op jit(solution)/shard_map/ppermute | solution.py:128
  82.5 1.9 %add_convert_fusion.3 = (bf16[512,512]{0,1:T(8,128)(2,1)S(1)}, bf16[512,512]{0,1:T(8,128)(2,1)S(1)}) fusion(bf16[512,512]{0,1:T(8,128)(2,1)} %collective-permute-done.12, bf16[512,512]{0,1:T(8,128)(2,1)} %collective-permute-done.11, bf16[512,768]{1,0:T(8,128)(2,1)S(1)} %bitcast.47, bf16[512,768]{1,0:T(8,128)(2,1)S(1)} %pad_maximum_fusion.2), kind=kOutput, calls=%fused_computation.13 | convolution fusion | flops 404226048 | bytes 3670016 | tf_op jit(solution)/shard_map/dot_general | solution.py:113
  84.4 4.4 %collective-permute-start.15 = (bf16[512,512]{0,1:T(8,128)(2,1)S(1)}, bf16[512,512]{0,1:T(8,128)(2,1)S(1)}, u32[]{:S(2)}, u32[]{:S(2)}) collective-permute-start(bf16[512,512]{0,1:T(8,128)(2,1)S(1)} %get-tuple-element.22), channel_id=1, source_target_pairs={{0,8},{4,12},{8,16},{12,20},{1,9},{5,13},{9,17},{13,21},{2,10},{6,... | collective-permute-start | bytes 1572872 | tf_op jit(solution)/shard_map/ppermute | solution.py:128
  88.8 0.6 fusion.16
  89.5 0.8 collective-permute-start.16
  90.3 1.7 %fusion.5 = f32[768,512]{0,1:T(8,128)S(1)} fusion(bf16[512,768]{1,0:T(8,128)(2,1)S(1)} %bitcast.48, bf16[512,512]{1,0:T(8,128)(2,1)} %collective-permute-done.13, bf16[512,512]{1,0:T(8,128)(2,1)} %collective-permute-done.14, pred[]{:T(512)S(6)} %ge.10), kind=kOutput, calls=%fused_computation.30 | convolution fusion | flops 402915328 | bytes 3407873 | tf_op jit(solution)/shard_map/dot_general | solution.py:133
  92.0 6.4 %collective-permute-done.15 = bf16[512,512]{0,1:T(8,128)(2,1)S(1)} collective-permute-done((bf16[512,512]{0,1:T(8,128)(2,1)S(1)}, bf16[512,512]{0,1:T(8,128)(2,1)S(1)}, u32[]{:S(2)}, u32[]{:S(2)}) %collective-permute-start.15) | collective-permute-done | bytes 524320 | tf_op jit(solution)/shard_map/ppermute | solution.py:128
  98.8 1.4 %collective-permute-start.20 = (bf16[512,512]{0,1:T(8,128)(2,1)S(1)}, bf16[512,512]{0,1:T(8,128)(2,1)S(1)}, u32[]{:S(2)}, u32[]{:S(2)}) collective-permute-start(bf16[512,512]{0,1:T(8,128)(2,1)S(1)} %add_convert_fusion.1), channel_id=1, source_target_pairs={{8,0},{12,4},{16,8},{20,12},{24,16},{28,20},{9,1},{13,5},{17,9},{2... | collective-permute-start | bytes 1572872 | tf_op jit(solution)/shard_map/ppermute | solution.py:129
  100.3 8.3 %collective-permute-start.19 = (bf16[512,512]{0,1:T(8,128)(2,1)S(1)}, bf16[512,512]{0,1:T(8,128)(2,1)S(1)}, u32[]{:S(2)}, u32[]{:S(2)}) collective-permute-start(bf16[512,512]{0,1:T(8,128)(2,1)S(1)} %add_convert_fusion.2), channel_id=1, source_target_pairs={{0,8},{4,12},{8,16},{12,20},{16,24},{20,28},{1,9},{5,13},{9,17},{1... | collective-permute-start | bytes 1572872 | tf_op jit(solution)/shard_map/ppermute | solution.py:128
  108.5 0.7 fusion.7
  109.2 1.8 %multiply_convert_fusion = bf16[768,512]{0,1:T(8,128)(2,1)S(1)} fusion(f32[768,512]{0,1:T(8,128)S(1)} %fusion.5, f32[768,512]{0,1:T(8,128)S(1)} %fusion.16, f32[768,512]{0,1:T(8,128)S(1)} %fusion.7, bf16[512,768]{1,0:T(8,128)(2,1)S(1)} %bitcast.54, bf16[512,512]{1,0:T(8,128)(2,1)S(1)} %collective-permute-done.17, ...), kind=kOutput, calls=%fused_computation.9 | convolution fusion | flops 404881408 | bytes 7340033 | tf_op jit(solution)/shard_map/dot_general | solution.py:133
  111.1 1.5 %collective-permute-start.22 = (bf16[384,512]{0,1:T(8,128)(2,1)S(1)}, bf16[384,512]{0,1:T(8,128)(2,1)S(1)}, u32[]{:S(2)}, u32[]{:S(2)}) collective-permute-start(bf16[384,512]{0,1:T(8,128)(2,1)S(1)} %constant_dynamic-slice_fusion), channel_id=1, source_target_pairs={{0,4},{4,0},{8,12},{12,8},{16,20},{20,16},{24,28},{28,24},{1,5},{5... | collective-permute-start | bytes 1179656 | tf_op jit(solution)/shard_map/ppermute | solution.py:56
  112.6 0.6 fusion.15
  113.2 2.5 %collective-permute-done.20 = bf16[512,512]{0,1:T(8,128)(2,1)S(1)} collective-permute-done((bf16[512,512]{0,1:T(8,128)(2,1)S(1)}, bf16[512,512]{0,1:T(8,128)(2,1)S(1)}, u32[]{:S(2)}, u32[]{:S(2)}) %collective-permute-start.20) | collective-permute-done | bytes 524320 | tf_op jit(solution)/shard_map/ppermute | solution.py:129
  115.7 1.2 collective-permute-done.19
  117.1 1.5 %collective-permute-start.21 = (bf16[256,512]{0,1:T(8,128)(2,1)S(1)}, bf16[256,512]{0,1:T(8,128)(2,1)S(1)}, u32[]{:S(2)}, u32[]{:S(2)}) collective-permute-start(bf16[256,512]{0,1:T(8,128)(2,1)S(1)} %slice.39), channel_id=1, source_target_pairs={{0,4},{4,0},{8,12},{12,8},{16,20},{20,16},{24,28},{28,24},{1,5},{5... | collective-permute-start | bytes 786440 | tf_op jit(solution)/shard_map/ppermute | solution.py:56
  118.6 3.1 %collective-permute-done.22 = bf16[384,512]{0,1:T(8,128)(2,1)S(1)} collective-permute-done((bf16[384,512]{0,1:T(8,128)(2,1)S(1)}, bf16[384,512]{0,1:T(8,128)(2,1)S(1)}, u32[]{:S(2)}, u32[]{:S(2)}) %collective-permute-start.22) | collective-permute-done | bytes 393248 | tf_op jit(solution)/shard_map/ppermute | solution.py:56
  122.0 1.2 copy.26
  123.2 1.4 %collective-permute-done.21 = bf16[256,512]{0,1:T(8,128)(2,1)S(1)} collective-permute-done((bf16[256,512]{0,1:T(8,128)(2,1)S(1)}, bf16[256,512]{0,1:T(8,128)(2,1)S(1)}, u32[]{:S(2)}, u32[]{:S(2)}) %collective-permute-start.21) | collective-permute-done | bytes 262176 | tf_op jit(solution)/shard_map/ppermute | solution.py:56
  124.9 0.9 reverse_select_fusion
  (52 shorter events, 2.6 us)
Async XLA Ops:
  0.7 4.7 %copy-start.8 = (bf16[32,384]{1,0:T(8,128)(2,1)S(1)}, bf16[32,384]{1,0:T(8,128)(2,1)}, u32[]{:S(2)}) copy-start(bf16[32,384]{1,0:T(8,128)(2,1)} %param.7) | copy-start | bytes 73732
  0.7 4.7 %copy-start.6 = (bf16[1024,384]{1,0:T(8,128)(2,1)S(1)}, bf16[1024,384]{1,0:T(8,128)(2,1)}, u32[]{:S(2)}) copy-start(bf16[1024,384]{1,0:T(8,128)(2,1)} %param.6) | copy-start | bytes 2359300
  2.3 3.4 %copy-start.7 = (bf16[64,3072]{1,0:T(8,128)(2,1)S(1)}, bf16[64,3072]{1,0:T(8,128)(2,1)}, u32[]{:S(2)}) copy-start(bf16[64,3072]{1,0:T(8,128)(2,1)} %param.4) | copy-start | bytes 1179652
  2.4 15.9 %collective-permute-start.3 = (bf16[256,512]{1,0:T(8,128)(2,1)S(1)}, bf16[256,512]{1,0:T(8,128)(2,1)}, u32[]{:S(2)}, u32[]{:S(2)}) collective-permute-start(bf16[256,512]{1,0:T(8,128)(2,1)S(1)} %get-tuple-element.51), channel_id=1, source_target_pairs={{0,4},{4,0},{8,12},{12,8},{16,20},{20,16},{24,28},{28,24},{1,5},{5... | collective-permute-start | bytes 786440 | tf_op jit(solution)/shard_map/ppermute | solution.py:56
  5.6 14.5 %collective-permute-start.4 = (bf16[512,384]{1,0:T(8,128)(2,1)S(1)}, bf16[512,384]{1,0:T(8,128)(2,1)S(1)}, u32[]{:S(2)}, u32[]{:S(2)}) collective-permute-start(bf16[512,384]{1,0:T(8,128)(2,1)S(1)} %constant_dynamic-slice_fusion.1), channel_id=1, source_target_pairs={{0,4},{4,0},{8,12},{12,8},{16,20},{20,16},{24,28},{28,24},{1,5},{5... | collective-permute-start | bytes 1179656 | tf_op jit(solution)/shard_map/ppermute | solution.py:56
  5.8 7.3 %collective-permute-start.2 = (bf16[64,768]{1,0:T(8,128)(2,1)S(1)}, bf16[64,768]{1,0:T(8,128)(2,1)S(1)}, u32[]{:S(2)}, u32[]{:S(2)}) collective-permute-start(bf16[64,768]{1,0:T(8,128)(2,1)S(1)} %get-tuple-element.54), channel_id=1, source_target_pairs={{0,24},{4,28},{8,0},{12,4},{16,8},{20,12},{24,16},{28,20},{1,25},{... | collective-permute-start | bytes 294920 | tf_op jit(solution)/shard_map/ppermute | solution.py:67
  9.9 8.3 %collective-permute-start.1 = (bf16[64,768]{1,0:T(8,128)(2,1)S(1)}, bf16[64,768]{1,0:T(8,128)(2,1)S(1)}, u32[]{:S(2)}, u32[]{:S(2)}) collective-permute-start(bf16[64,768]{1,0:T(8,128)(2,1)S(1)} %get-tuple-element.55), channel_id=1, source_target_pairs={{0,16},{4,20},{8,24},{12,28},{16,0},{20,4},{24,8},{28,12},{1,17},{... | collective-permute-start | bytes 294920 | tf_op jit(solution)/shard_map/ppermute | solution.py:67
  9.9 8.3 %collective-permute-start = (bf16[64,768]{1,0:T(8,128)(2,1)S(1)}, bf16[64,768]{1,0:T(8,128)(2,1)S(1)}, u32[]{:S(2)}, u32[]{:S(2)}) collective-permute-start(bf16[64,768]{1,0:T(8,128)(2,1)S(1)} %get-tuple-element.53), channel_id=1, source_target_pairs={{0,8},{4,12},{8,16},{12,20},{16,24},{20,28},{24,0},{28,4},{1,9},{5... | collective-permute-start | bytes 294920 | tf_op jit(solution)/shard_map/ppermute | solution.py:67
  19.3 25.2 %copy-start.4 = (bf16[512,512]{1,0:T(8,128)(2,1)}, bf16[512,512]{1,0:T(8,128)(2,1)S(1)}, u32[]{:S(2)}) copy-start(bf16[512,512]{1,0:T(8,128)(2,1)S(1)} %pad_maximum_fusion.4) | copy-start | bytes 1572868
  20.4 10.4 %collective-permute-start.5 = (bf16[4,64,768]{2,1,0:T(8,128)(2,1)S(1)}, bf16[4,64,768]{2,1,0:T(8,128)(2,1)S(1)}, u32[]{:S(2)}, u32[]{:S(2)}) collective-permute-start(bf16[4,64,768]{2,1,0:T(8,128)(2,1)S(1)} %pad_maximum_fusion.6), channel_id=1, source_target_pairs={{0,2},{1,3},{2,0},{3,1},{4,6},{5,7},{6,4},{7,5},{8,10},{9,11},{10,... | collective-permute-start | bytes 1179656 | tf_op jit(solution)/shard_map/ppermute | solution.py:59
  22.2 9.7 %collective-permute-start.6 = (bf16[4,64,768]{2,1,0:T(8,128)(2,1)S(1)}, bf16[4,64,768]{2,1,0:T(8,128)(2,1)S(1)}, u32[]{:S(2)}, u32[]{:S(2)}) collective-permute-start(bf16[4,64,768]{2,1,0:T(8,128)(2,1)S(1)} %pad_maximum_fusion.6), channel_id=1, source_target_pairs={{0,4},{4,0},{8,12},{12,8},{16,20},{20,16},{24,28},{28,24},{1,5},{5... | collective-permute-start | bytes 1179656 | tf_op jit(solution)/shard_map/ppermute | solution.py:56
  31.9 7.8 %collective-permute-start.7 = (bf16[4,64,768]{2,1,0:T(8,128)(2,1)S(1)}, bf16[4,64,768]{2,1,0:T(8,128)(2,1)S(1)}, u32[]{:S(2)}, u32[]{:S(2)}) collective-permute-start(bf16[4,64,768]{2,1,0:T(8,128)(2,1)S(1)} %broadcast_select_fusion.2), channel_id=1, source_target_pairs={{0,4},{1,3},{2,6},{3,1},{4,0},{5,7},{6,2},{7,5},{8,12},{9,11},{10,... | collective-permute-start | bytes 1179656 | tf_op jit(solution)/shard_map/ppermute | solution.py:99
  40.1 21.7 %collective-permute-start.8 = (bf16[4,2,2,64,768]{4,3,2,1,0:T(8,128)(2,1)S(1)}, bf16[4,2,2,64,768]{4,3,2,1,0:T(8,128)(2,1)S(1)}, u32[]{:S(2)}, u32[]{:S(2)}) collective-permute-start(bf16[4,2,2,64,768]{4,3,2,1,0:T(8,128)(2,1)S(1)} %get-tuple-element.40), channel_id=1, source_target_pairs={{0,1},{1,0},{2,3},{3,2},{4,5},{5,4},{6,7},{7,6},{8,9},{9,8},{10,11... | collective-permute-start | bytes 4718600 | tf_op jit(solution)/shard_map/ppermute | solution.py:59
  40.2 15.3 %collective-permute-start.9 = (bf16[512,512]{1,0:T(8,128)(2,1)S(1)}, bf16[512,512]{1,0:T(8,128)(2,1)}, u32[]{:S(2)}, u32[]{:S(2)}) collective-permute-start(bf16[512,512]{1,0:T(8,128)(2,1)S(1)} %pad_maximum_fusion.4), channel_id=1, source_target_pairs={{0,8},{4,12},{8,16},{12,20},{16,24},{20,28},{1,9},{5,13},{9,17},{1... | collective-permute-start | bytes 1572872 | tf_op jit(solution)/shard_map/ppermute | solution.py:109
  44.5 16.0 %collective-permute-start.10 = (bf16[512,512]{1,0:T(8,128)(2,1)S(1)}, bf16[512,512]{1,0:T(8,128)(2,1)}, u32[]{:S(2)}, u32[]{:S(2)}) collective-permute-start(bf16[512,512]{1,0:T(8,128)(2,1)S(1)} %pad_maximum_fusion.4), channel_id=1, source_target_pairs={{8,0},{12,4},{16,8},{20,12},{24,16},{28,20},{9,1},{13,5},{17,9},{2... | collective-permute-start | bytes 1572872 | tf_op jit(solution)/shard_map/ppermute | solution.py:110
  55.5 16.9 %collective-permute-start.13 = (bf16[512,512]{1,0:T(8,128)(2,1)}, bf16[512,512]{1,0:T(8,128)(2,1)}, u32[]{:S(2)}, u32[]{:S(2)}) collective-permute-start(bf16[512,512]{1,0:T(8,128)(2,1)} %collective-permute-done.9), channel_id=1, source_target_pairs={{8,16},{12,20},{16,24},{20,28},{9,17},{13,21},{17,25},{21,29},{10,... | collective-permute-start | bytes 1572872 | tf_op jit(solution)/shard_map/ppermute | solution.py:109
  60.5 15.6 %collective-permute-start.14 = (bf16[512,512]{1,0:T(8,128)(2,1)}, bf16[512,512]{1,0:T(8,128)(2,1)}, u32[]{:S(2)}, u32[]{:S(2)}) collective-permute-start(bf16[512,512]{1,0:T(8,128)(2,1)} %collective-permute-done.10), channel_id=1, source_target_pairs={{8,0},{12,4},{16,8},{20,12},{9,1},{13,5},{17,9},{21,13},{10,2},{14... | collective-permute-start | bytes 1572872 | tf_op jit(solution)/shard_map/ppermute | solution.py:110
  62.1 1.8 %copy-start = (bf16[1,2,2,2,64,768]{5,4,3,2,1,0:T(8,128)(2,1)}, bf16[1,2,2,2,64,768]{5,4,3,2,1,0:T(8,128)(2,1)S(1)}, u32[]{:S(2)}) copy-start(bf16[1,2,2,2,64,768]{5,4,3,2,1,0:T(8,128)(2,1)S(1)} %get-tuple-element.37) | copy-start | bytes 2359300
  65.6 11.7 %collective-permute-start.12 = (bf16[512,512]{0,1:T(8,128)(2,1)}, bf16[512,512]{0,1:T(8,128)(2,1)}, u32[]{:S(2)}, u32[]{:S(2)}) collective-permute-start(bf16[512,512]{0,1:T(8,128)(2,1)} %get-tuple-element.21), channel_id=1, source_target_pairs={{24,16},{28,20},{25,17},{29,21},{26,18},{30,22},{27,19},{31,23}} | collective-permute-start | bytes 1572872 | tf_op jit(solution)/shard_map/ppermute | solution.py:129
  67.0 15.4 %collective-permute-start.11 = (bf16[512,512]{0,1:T(8,128)(2,1)}, bf16[512,512]{0,1:T(8,128)(2,1)}, u32[]{:S(2)}, u32[]{:S(2)}) collective-permute-start(bf16[512,512]{0,1:T(8,128)(2,1)} %get-tuple-element.20), channel_id=1, source_target_pairs={{0,8},{4,12},{1,9},{5,13},{2,10},{6,14},{3,11},{7,15}} | collective-permute-start | bytes 1572872 | tf_op jit(solution)/shard_map/ppermute | solution.py:128
  72.4 26.4 %collective-permute-start.17 = (bf16[512,512]{1,0:T(8,128)(2,1)}, bf16[512,512]{1,0:T(8,128)(2,1)S(1)}, u32[]{:S(2)}, u32[]{:S(2)}) collective-permute-start(bf16[512,512]{1,0:T(8,128)(2,1)} %collective-permute-done.13), channel_id=1, source_target_pairs={{16,24},{20,28},{17,25},{21,29},{18,26},{22,30},{19,27},{23,31}} | collective-permute-start | bytes 1572872 | tf_op jit(solution)/shard_map/ppermute | solution.py:109
  76.0 22.8 %collective-permute-start.18 = (bf16[512,512]{1,0:T(8,128)(2,1)}, bf16[512,512]{1,0:T(8,128)(2,1)S(1)}, u32[]{:S(2)}, u32[]{:S(2)}) collective-permute-start(bf16[512,512]{1,0:T(8,128)(2,1)} %collective-permute-done.14), channel_id=1, source_target_pairs={{8,0},{12,4},{9,1},{13,5},{10,2},{14,6},{11,3},{15,7}} | collective-permute-start | bytes 1572872 | tf_op jit(solution)/shard_map/ppermute | solution.py:110
  82.5 6.3 %copy-start.5 = (bf16[512,512]{1,0:T(8,128)(2,1)S(1)}, bf16[512,512]{1,0:T(8,128)(2,1)}, u32[]{:S(2)}) copy-start(bf16[512,512]{1,0:T(8,128)(2,1)} %copy-done.4) | copy-start | bytes 1572868
  84.4 14.1 %collective-permute-start.15 = (bf16[512,512]{0,1:T(8,128)(2,1)S(1)}, bf16[512,512]{0,1:T(8,128)(2,1)S(1)}, u32[]{:S(2)}, u32[]{:S(2)}) collective-permute-start(bf16[512,512]{0,1:T(8,128)(2,1)S(1)} %get-tuple-element.22), channel_id=1, source_target_pairs={{0,8},{4,12},{8,16},{12,20},{1,9},{5,13},{9,17},{13,21},{2,10},{6,... | collective-permute-start | bytes 1572872 | tf_op jit(solution)/shard_map/ppermute | solution.py:128
  89.5 9.0 %copy-start.3 = (f32[512,512]{0,1:T(8,128)S(1)}, f32[512,512]{0,1:T(8,128)}, u32[]{:S(2)}) copy-start(f32[512,512]{0,1:T(8,128)} %get-tuple-element.59) | copy-start | bytes 3145732
  89.5 9.2 %collective-permute-start.16 = (bf16[512,512]{0,1:T(8,128)(2,1)S(1)}, bf16[512,512]{0,1:T(8,128)(2,1)S(1)}, u32[]{:S(2)}, u32[]{:S(2)}) collective-permute-start(bf16[512,512]{0,1:T(8,128)(2,1)S(1)} %get-tuple-element.23), channel_id=1, source_target_pairs={{16,8},{20,12},{24,16},{28,20},{17,9},{21,13},{25,17},{29,21},{18,... | collective-permute-start | bytes 1572872 | tf_op jit(solution)/shard_map/ppermute | solution.py:129
  92.0 6.6 %copy-start.2 = (f32[512,512]{0,1:T(8,128)S(1)}, f32[512,512]{0,1:T(8,128)}, u32[]{:S(2)}) copy-start(f32[512,512]{0,1:T(8,128)} %get-tuple-element.57) | copy-start | bytes 3145732
  98.8 10.4 %copy-start.1 = (bf16[1,2,2,2,64,768]{5,4,3,2,1,0:T(8,128)(2,1)S(1)}, bf16[1,2,2,2,64,768]{5,4,3,2,1,0:T(8,128)(2,1)}, u32[]{:S(2)}) copy-start(bf16[1,2,2,2,64,768]{5,4,3,2,1,0:T(8,128)(2,1)} %copy-done) | copy-start | bytes 2359300
  98.8 16.8 %collective-permute-start.20 = (bf16[512,512]{0,1:T(8,128)(2,1)S(1)}, bf16[512,512]{0,1:T(8,128)(2,1)S(1)}, u32[]{:S(2)}, u32[]{:S(2)}) collective-permute-start(bf16[512,512]{0,1:T(8,128)(2,1)S(1)} %add_convert_fusion.1), channel_id=1, source_target_pairs={{8,0},{12,4},{16,8},{20,12},{24,16},{28,20},{9,1},{13,5},{17,9},{2... | collective-permute-start | bytes 1572872 | tf_op jit(solution)/shard_map/ppermute | solution.py:129
  100.3 16.6 %collective-permute-start.19 = (bf16[512,512]{0,1:T(8,128)(2,1)S(1)}, bf16[512,512]{0,1:T(8,128)(2,1)S(1)}, u32[]{:S(2)}, u32[]{:S(2)}) collective-permute-start(bf16[512,512]{0,1:T(8,128)(2,1)S(1)} %add_convert_fusion.2), channel_id=1, source_target_pairs={{0,8},{4,12},{8,16},{12,20},{16,24},{20,28},{1,9},{5,13},{9,17},{1... | collective-permute-start | bytes 1572872 | tf_op jit(solution)/shard_map/ppermute | solution.py:128
  111.1 10.7 %collective-permute-start.22 = (bf16[384,512]{0,1:T(8,128)(2,1)S(1)}, bf16[384,512]{0,1:T(8,128)(2,1)S(1)}, u32[]{:S(2)}, u32[]{:S(2)}) collective-permute-start(bf16[384,512]{0,1:T(8,128)(2,1)S(1)} %constant_dynamic-slice_fusion), channel_id=1, source_target_pairs={{0,4},{4,0},{8,12},{12,8},{16,20},{20,16},{24,28},{28,24},{1,5},{5... | collective-permute-start | bytes 1179656 | tf_op jit(solution)/shard_map/ppermute | solution.py:56
  117.1 7.4 %collective-permute-start.21 = (bf16[256,512]{0,1:T(8,128)(2,1)S(1)}, bf16[256,512]{0,1:T(8,128)(2,1)S(1)}, u32[]{:S(2)}, u32[]{:S(2)}) collective-permute-start(bf16[256,512]{0,1:T(8,128)(2,1)S(1)} %slice.39), channel_id=1, source_target_pairs={{0,4},{4,0},{8,12},{12,8},{16,20},{20,16},{24,28},{28,24},{1,5},{5... | collective-permute-start | bytes 786440 | tf_op jit(solution)/shard_map/ppermute | solution.py:56

commit v3 on v0

v3 whole, which is shorter than its diff:
```python
import math

import jax
import jax.numpy as jnp
from jax import lax
from jax.sharding import PartitionSpec as P

BLOCK = 32
PAIR = 2
LINE = 4
STREAMS = 2


def dequantize(codes_part, scales_part):
    expanded = jnp.repeat(scales_part.astype(jnp.float32), BLOCK, axis=0)
    return (codes_part.astype(jnp.float32) * expanded).astype(jnp.bfloat16)


def halves(own, other, side, axis):
    first = jnp.where(side == 0, own, other)
    second = jnp.where(side == 0, other, own)
    return jnp.concatenate([first, second], axis)


def pair(own, other, side, axis):
    return halves(jnp.expand_dims(own, axis), jnp.expand_dims(other, axis), side, axis)


def together(*arrays):
    return lax.optimization_barrier(arrays)


def by_feature(rows, weight):
    return lax.dot_general(
        rows, weight, (((1,), (1,)), ((), ())), preferred_element_type=jnp.float32
    )


def by_token(columns, rows):
    return lax.dot_general(
        columns, rows, (((0,), (0,)), ((), ())), preferred_element_type=jnp.float32
    )


def body(grad_out, attn_out, weight_codes, block_scales):
    n_dp, n_mp = lax.axis_size("dp"), lax.axis_size("mp")
    layers = n_dp // PAIR
    bits = n_mp.bit_length() - 1
    group_rows, heads = attn_out.shape
    own_features = weight_codes.shape[1]
    half = heads // PAIR
    layer_rows, layer_features = PAIR * group_rows, PAIR * own_features
    scaling = 1.0 / math.sqrt(group_rows * n_dp)

    dp, mp = lax.axis_index("dp"), lax.axis_index("mp")
    layer, side = dp // PAIR, dp % PAIR
    middle = (layer > 0) & (layer < layers - 1)

    def swap_x(piece):
        return lax.ppermute(piece, "dp", [(i, i ^ 1) for i in range(n_dp)])

    def swap_mp(piece, bit):
        return lax.ppermute(piece, "mp", [(i, i ^ bit) for i in range(n_mp)])

    def move_layers(piece, to):
        moves = [(i, to(i // PAIR) * PAIR + i % PAIR) for i in range(n_dp)]
        return lax.ppermute(piece, "dp", moves)

    def outer(piece):
        return move_layers(piece, lambda z: z ^ 1)

    between = []
    for i in range(n_dp):
        z, x = i // PAIR, i % PAIR
        for j in range(n_mp):
            if z in (0, layers - 1):
                there = i, j ^ 1
            else:
                there = (((z - 1) ^ 1) + 1) * PAIR + x, j
            between.append((i * n_mp + j, there[0] * n_mp + there[1]))

    def inner(piece):
        return lax.ppermute(piece, ("dp", "mp"), between)

    slots = []
    for s in range(layers):
        piece = lax.dynamic_slice_in_dim(
            grad_out, (layer ^ s) * layer_features, layer_features, 1
        )
        slots.append(move_layers(piece, lambda z: z ^ s) if s else piece)
    own = jnp.stack(slots)

    width = half // STREAMS
    attn = []
    for k in range(STREAMS):
        keep = lax.dynamic_slice_in_dim(attn_out, side * half + k * width, width, 1)
        send = lax.dynamic_slice_in_dim(attn_out, (1 - side) * half + k * width, width, 1)
        attn.append([keep, swap_x(send)])
    weight = dequantize(weight_codes, block_scales)
    weight_own = lax.dynamic_slice_in_dim(weight, side * half, half, 0)
    weight_send = lax.dynamic_slice_in_dim(weight, (1 - side) * half, half, 0)

    top = n_mp // 2
    weight_other = swap_x(weight_send)
    own, attn[0][1], attn[-1][1], weight_other = together(
        own, attn[0][1], attn[-1][1], weight_other
    )
    via_x, via_mp = swap_x(own), swap_mp(own, top)
    attn = [jnp.concatenate(parts, 0) for parts in attn]
    if layers == LINE:
        attn_1 = [outer(a) for a in attn]
        attn_in = [inner(a) for a in attn]
    if layers == LINE:
        via_x, via_mp, attn_1[0], attn_in[0] = together(via_x, via_mp, attn_1[0], attn_in[0])
    mixed = []
    for i in range(n_dp):
        for j in range(n_mp):
            there = ((i ^ 1), j) if j % 2 == 0 else (i, j ^ top)
            mixed.append((i * n_mp + j, there[0] * n_mp + there[1]))
    far = lax.ppermute(jnp.where(mp % 2 == 0, via_mp, via_x), ("dp", "mp"), mixed)
    near = pair(own, via_mp, mp // top, 1)
    away = pair(via_x, far, mp // top, 1)
    held = jnp.stack([near, away], 1)
    if layers == LINE:
        held, attn_1, attn_in = together(held, attn_1, attn_in)
    for k in range(1, bits):
        bit = top >> k
        held = pair(held, swap_mp(held, bit), (mp // bit) % 2, 2 + k)
    cols = held.reshape(layers, layer_rows, layer_features)
    weight_slab = halves(weight_own, weight_other, side, 1)

    def terms(k):
        stream = weight_slab[k * width : (k + 1) * width]
        return by_feature(cols.reshape(-1, layer_features), stream)

    gws, gas = [], []
    if layers == LINE:
        streams = range(STREAMS)
        part = [terms(k).reshape(layers, layer_rows, width) for k in streams]
        outer_2, inner_2, outer_3, inner_3 = [], [], [], []
        for k in streams:
            send = jnp.where(middle, attn_in[k], part[k][3].astype(jnp.bfloat16))
            outer_2.append(outer(send))
            inner_2.append(inner(attn_1[k]))
        for k in streams:
            send_outer = jnp.where(middle, inner_2[k], part[k][2].astype(jnp.bfloat16))
            send_inner = (part[k][2] + outer_2[k].astype(jnp.float32)).astype(jnp.bfloat16)
            send_outer, send_inner = together(send_outer, send_inner)
            outer_3.append(outer(send_outer))
            inner_3.append(inner(send_inner))
        for k in streams:
            send_inner = (part[k][3] + outer_3[k].astype(jnp.float32)).astype(jnp.bfloat16)
            send_outer = part[k][1] + jnp.where(middle, inner_3[k].astype(jnp.float32), 0.0)
            send_outer, send_inner = together(send_outer.astype(jnp.bfloat16), send_inner)
            outer_4, inner_4 = outer(send_outer), inner(send_inner)
            ga = part[k][0] + outer_4.astype(jnp.float32)
            gas.append(ga + jnp.where(middle, inner_4.astype(jnp.float32), 0.0))

            attn_2 = jnp.where(middle, inner_2[k], outer_2[k])
            attn_3 = jnp.where(middle, attn_in[k], outer_3[k])
            total = by_token(cols[0], attn[k]) + by_token(cols[1], attn_1[k])
            gws.append(total + by_token(cols[2], attn_2) + by_token(cols[3], attn_3))
    else:
        lines = [[z * PAIR + x for z in range(layers)] for x in range(PAIR)]
        cols = cols[jnp.arange(layers) ^ layer].reshape(-1, layer_features)
        for k in range(STREAMS):
            attn_all = lax.all_gather(
                attn[k], "dp", axis=0, tiled=True, axis_index_groups=lines
            )
            gws.append(by_token(cols, attn_all))
            gas.append(
                lax.psum_scatter(
                    terms(k), "dp", scatter_dimension=0, tiled=True, axis_index_groups=lines
                )
            )

    gw_own, gw_other, ga_own, ga_other = [], [], [], []
    for k in range(STREAMS):
        gw = (scaling * gws[k]).astype(jnp.bfloat16)
        send = lax.dynamic_slice_in_dim(gw, (1 - side) * own_features, own_features, 0)
        gw_own.append(lax.dynamic_slice_in_dim(gw, side * own_features, own_features, 0))
        gw_other.append(swap_x(send))
        ga = gas[k].astype(jnp.bfloat16)
        ga_own.append(ga[:group_rows])
        ga_other.append(swap_x(ga[group_rows:]))
    beside = lambda parts: jnp.concatenate(parts, 1)
    grad_weight_t = halves(beside(gw_own), beside(gw_other), side, 1)
    grad_attn = halves(beside(ga_own), beside(ga_other), side, 1)
    return grad_attn, grad_weight_t


def solution(mesh):
    placed = (P(("dp", "mp"), None), P("dp", "mp"), P("mp", "dp"), P("mp", "dp"))
    return jax.shard_map(
        body, mesh=mesh, in_specs=placed, out_specs=(P("dp", "mp"), P("dp", "mp")), check_vma=False
    )
```

time: 355 us -> 99.9 us (0.28)
  waiting for transfers between devices: 291 us -> 43.4 us
  starting transfers between devices: 0.11 us -> 35.2 us
  blocking collectives: 32.3 us -> 0 us
  between operations: 13.8 us -> 1.11 us
  matrix products: 9.6 us -> 5.03 us
    reduce_scatter x1 -> x0, waiting for transfers between devices: 202 us -> none  [body(): lax.psum_scatter(scaling * lax.dot_general(whole_rows, attn_out, by_token...]
    all_gather x2 -> x0, waiting for transfers between devices: 87.6 us -> none  [the longest x1 64.4 us: body(): lax.all_gather(weight_codes, 'dp', axis=1, tiled=True)]
    ppermute x0 -> x30, waiting for transfers between devices: none -> 43.4 us  [the longest x11 23.6 us: move_layers(): return lax.ppermute(piece, 'dp', moves)]
    ppermute x0 -> x30, starting transfers between devices: none -> 35.2 us  [the longest x11 23.9 us: move_layers(): return lax.ppermute(piece, 'dp', moves)]
    all_gather x1 -> x0, blocking collectives: 32.3 us -> none  [body(): lax.all_gather(block_scales, 'dp', axis=1, tiled=True)]
    select_n x0 -> x8, other arithmetic: none -> 6.09 us  [the longest x5 4.73 us: halves(): first = jnp.where(side == 0, own, other)]
    dot_general x2 -> x10, matrix products: 9.6 us -> 5.03 us  [the longest x8 3.02 us: by_token(): lax.dot_general(columns, rows, (((0,), (0,)), ((), ())), preferred_elemen...]
  transfers between devices with their start and end apart: 3 -> 30, of which waited for: 3 -> 16; matrix products, arithmetic and copies ran while one was open for 4% -> 13% of each run, Pallas kernels for 0% -> 0%
where the time goes in v3:
time: 99.9 us; the launch traced here: 99.5 us
  waiting for transfers between devices  43.4 us (43%)
  starting transfers between devices  35.2 us (35%)
  other arithmetic  9.99 us (10%)
  matrix products  5.03 us (5%)
  local copies, waits for them, and re-layouts  4.71 us (5%)
  between operations  1.11 us (1%)
    ppermute x11, starting transfers between devices, move_layers(): return lax.ppermute(piece, 'dp', moves)  23.9 us
    ppermute x11, waiting for transfers between devices, move_layers(): return lax.ppermute(piece, 'dp', moves)  23.6 us
    ppermute x8, waiting for transfers between devices, swap_x(): return lax.ppermute(piece, 'dp', [(i, i ^ 1) for i in range(n_dp)])  11.5 us
    ppermute x8, starting transfers between devices, swap_x(): return lax.ppermute(piece, 'dp', [(i, i ^ 1) for i in range(n_dp)])  8.45 us
    ppermute x1, waiting for transfers between devices, body(): lax.ppermute(jnp.where(mp % 2 == 0, via_mp, via_x), ('dp', 'mp'), mixed)  5.78 us
    select_n x5, other arithmetic, halves(): first = jnp.where(side == 0, own, other)  4.73 us
    unnamed x30, local copies, waits for them, and re-layouts  4.38 us
    dot_general x8, matrix products, by_token(): lax.dot_general(columns, rows, (((0,), (0,)), ((), ())), preferred_elemen...  3.02 us
  transfers between devices with their start and end apart: 30, of which 16 were waited for; matrix products, arithmetic and copies ran while one was open for 13% of the time, Pallas kernels for 0%

profile of v3, /device:TPU:0, one launch (start us, length us, event | category | flops | bytes accessed | tf_op | source)
XLA Modules:
  0.0 99.5 jit_solution(8136504708681542897)
XLA Ops:
  0.7 0.8 convert_element_type.82
  1.5 1.3 %fusion = bf16[1024,384]{1,0:T(8,128)(2,1)S(1)} fusion(bf16[1024,384]{1,0:T(8,128)(2,1)} %param.6, f32[32,384]{1,0:T(8,128)S(1)} %convert_element_type.82), kind=kLoop, calls=%fused_computation.11 | loop fusion | flops 1179648 | bytes 1622016 | tf_op jit(solution)/shard_map/convert_element_type | solution.py:16
  2.8 3.0 %collective-permute-start.5 = (bf16[512,384]{1,0:T(8,128)(2,1)S(1)}, bf16[512,384]{1,0:T(8,128)(2,1)S(1)}, u32[]{:S(2)}, u32[]{:S(2)}) collective-permute-start(bf16[512,384]{1,0:T(8,128)(2,1)S(1)} %constant_dynamic-slice_fusion.6), channel_id=1, source_target_pairs={{0,4},{4,0},{8,12},{12,8},{16,20},{20,16},{24,28},{28,24},{1,5},{5... | collective-permute-start | bytes 1179656 | tf_op jit(solution)/shard_map/ppermute | solution.py:60
  5.9 3.7 %collective-permute-start.2 = (bf16[64,768]{1,0:T(8,128)(2,1)S(1)}, bf16[64,768]{1,0:T(8,128)(2,1)S(1)}, u32[]{:S(2)}, u32[]{:S(2)}) collective-permute-start(bf16[64,768]{1,0:T(8,128)(2,1)S(1)} %get-tuple-element.83), channel_id=1, source_target_pairs={{0,24},{4,28},{8,16},{12,20},{16,8},{20,12},{24,0},{28,4},{1,25},{... | collective-permute-start | bytes 294920 | tf_op jit(solution)/shard_map/ppermute | solution.py:67
  9.5 0.8 collective-permute-start
  10.5 0.5 collective-permute-start.3
  11.1 2.4 %collective-permute-done.2 = bf16[64,768]{1,0:T(8,128)(2,1)S(1)} collective-permute-done((bf16[64,768]{1,0:T(8,128)(2,1)S(1)}, bf16[64,768]{1,0:T(8,128)(2,1)S(1)}, u32[]{:S(2)}, u32[]{:S(2)}) %collective-permute-start.2) | collective-permute-done | bytes 98336 | tf_op jit(solution)/shard_map/ppermute | solution.py:67
  13.6 4.0 %collective-permute-done.1 = bf16[64,768]{1,0:T(8,128)(2,1)S(1)} collective-permute-done((bf16[64,768]{1,0:T(8,128)(2,1)S(1)}, bf16[64,768]{1,0:T(8,128)(2,1)S(1)}, u32[]{:S(2)}, u32[]{:S(2)}) %collective-permute-start.1) | collective-permute-done | bytes 98336 | tf_op jit(solution)/shard_map/ppermute | solution.py:67
  17.6 1.0 %collective-permute-done.3 = bf16[256,256]{0,1:T(8,128)(2,1)S(1)} collective-permute-done((bf16[256,256]{0,1:T(8,128)(2,1)S(1)}, bf16[256,256]{0,1:T(8,128)(2,1)S(1)}, u32[]{:S(2)}, u32[]{:S(2)}) %collective-permute-start.3) | collective-permute-done | bytes 131104 | tf_op jit(solution)/shard_map/ppermute | solution.py:60
  18.6 2.0 %collective-permute-done.4 = bf16[256,256]{0,1:T(8,128)(2,1)S(1)} collective-permute-done((bf16[256,256]{0,1:T(8,128)(2,1)S(1)}, bf16[256,256]{0,1:T(8,128)(2,1)S(1)}, u32[]{:S(2)}, u32[]{:S(2)}) %collective-permute-start.4) | collective-permute-done | bytes 131104 | tf_op jit(solution)/shard_map/ppermute | solution.py:60
  20.6 1.7 %collective-permute-start.6 = (bf16[4,64,768]{2,1,0:T(8,128)(2,1)S(1)}, bf16[4,64,768]{2,1,0:T(8,128)(2,1)S(1)}, u32[]{:S(2)}, u32[]{:S(2)}) collective-permute-start(bf16[4,64,768]{2,1,0:T(8,128)(2,1)S(1)} %pad_maximum_fusion.6), channel_id=1, source_target_pairs={{0,4},{4,0},{8,12},{12,8},{16,20},{20,16},{24,28},{28,24},{1,5},{5... | collective-permute-start | bytes 1179656 | tf_op jit(solution)/shard_map/ppermute | solution.py:60
  22.3 1.5 %collective-permute-start.7 = (bf16[4,64,768]{2,1,0:T(8,128)(2,1)S(1)}, bf16[4,64,768]{2,1,0:T(8,128)(2,1)}, u32[]{:S(2)}, u32[]{:S(2)}) collective-permute-start(bf16[4,64,768]{2,1,0:T(8,128)(2,1)S(1)} %pad_maximum_fusion.6), channel_id=1, source_target_pairs={{0,2},{1,3},{2,0},{3,1},{4,6},{5,7},{6,4},{7,5},{8,10},{9,11},{10,... | collective-permute-start | bytes 1179656 | tf_op jit(solution)/shard_map/ppermute | solution.py:63
  24.0 1.6 %collective-permute-start.8 = (bf16[512,256]{0,1:T(8,128)(2,1)S(1)}, bf16[512,256]{0,1:T(8,128)(2,1)S(1)}, u32[]{:S(2)}, u32[]{:S(2)}) collective-permute-start(bf16[512,256]{0,1:T(8,128)(2,1)S(1)} %pad_maximum_fusion.8), channel_id=1, source_target_pairs={{0,8},{4,12},{8,0},{12,4},{16,24},{20,28},{24,16},{28,20},{1,9},{5... | collective-permute-start | bytes 786440 | tf_op jit(solution)/shard_map/ppermute | solution.py:67
  25.6 5.0 %collective-permute-done.8 = bf16[512,256]{0,1:T(8,128)(2,1)S(1)} collective-permute-done((bf16[512,256]{0,1:T(8,128)(2,1)S(1)}, bf16[512,256]{0,1:T(8,128)(2,1)S(1)}, u32[]{:S(2)}, u32[]{:S(2)}) %collective-permute-start.8) | collective-permute-done | bytes 262176 | tf_op jit(solution)/shard_map/ppermute | solution.py:67
  30.9 0.5 copy-done.7
  31.4 0.8 collective-permute-done.7
  32.1 1.8 %select_bitcast_fusion.5 = (bf16[4,1,64,768]{3,2,0,1:T(8,128)(2,1)S(1)}, bf16[4,1,64,768]{3,2,0,1:T(8,128)(2,1)S(1)}, bf16[4,64,768]{2,1,0:T(8,128)(2,1)}) fusion(bf16[4,64,768]{2,1,0:T(8,128)(2,1)S(1)} %pad_maximum_fusion.6, bf16[4,64,768]{2,1,0:T(8,128)(2,1)} %collective-permute-done.7, pred[]{:T(512)S(6)} %eq.12, ...), kind=kLoop, calls=%fused_computation.60 | loop fusion | flops 589824 | bytes 2359298 | tf_op jit(solution)/shard_map/jit(_where)/select_n | solution.py:20
  33.9 0.6 collective-permute-start.10
  34.7 1.6 %collective-permute-start.11 = (bf16[512,256]{0,1:T(8,128)(2,1)S(1)}, bf16[512,256]{0,1:T(8,128)(2,1)S(1)}, u32[]{:S(2)}, u32[]{:S(2)}) collective-permute-start(bf16[512,256]{0,1:T(8,128)(2,1)S(1)} %pad_maximum_fusion.9), channel_id=1, source_target_pairs={{0,8},{4,12},{8,0},{12,4},{16,24},{20,28},{24,16},{28,20},{1,9},{5... | collective-permute-start | bytes 786440 | tf_op jit(solution)/shard_map/ppermute | solution.py:67
  36.3 5.8 %collective-permute-done.10 = bf16[4,64,768]{2,1,0:T(8,128)(2,1)} collective-permute-done((bf16[4,64,768]{2,1,0:T(8,128)(2,1)}, bf16[4,64,768]{2,1,0:T(8,128)(2,1)}, u32[]{:S(2)}, u32[]{:S(2)}) %collective-permute-start.10) | collective-permute-done | bytes 393248 | tf_op jit(solution)/shard_map/ppermute | solution.py:120
  42.0 1.1 %select_bitcast_fusion.3 = (bf16[4,1,64,768]{3,2,1,0:T(8,128)(2,1)S(1)}, bf16[4,1,64,768]{3,2,1,0:T(8,128)(2,1)S(1)}) fusion(bf16[4,64,768]{2,1,0:T(8,128)(2,1)S(1)} %collective-permute-done.6, bf16[4,64,768]{2,1,0:T(8,128)(2,1)} %collective-permute-done.10, pred[]{:T(512)S(6)} %eq.12), kind=kLoop, calls=%fused_computation.58 | loop fusion | flops 393216 | bytes 1572865 | tf_op jit(solution)/shard_map/jit(_where)/select_n | solution.py:20
  43.3 0.7 copy-done.9
  44.0 1.1 %broadcast_select_fusion.2 = (bf16[512,384]{1,0:T(8,128)(2,1)S(1)}, bf16[512,384]{1,0:T(8,128)(2,1)S(1)}) fusion(bf16[512,384]{1,0:T(8,128)(2,1)} %copy-done.6, pred[]{:T(512)S(6)} %eq.10, bf16[1024,384]{1,0:T(8,128)(2,1)S(1)} %fusion, s32[]{:T(128)S(6)} %select_n.217), kind=kLoop, calls=%fused_computation.63 | loop fusion | flops 393216 | bytes 1572869 | tf_op jit(solution)/shard_map/jit(_where)/select_n | solution.py:21
  45.2 0.6 collective-permute-start.14
  45.8 1.7 %collective-permute-done.13 = bf16[4,2,2,64,768]{4,3,2,1,0:T(8,128)(2,1)} collective-permute-done((bf16[4,2,2,64,768]{4,3,2,1,0:T(8,128)(2,1)S(1)}, bf16[4,2,2,64,768]{4,3,2,1,0:T(8,128)(2,1)}, u32[]{:S(2)}, u32[]{:S(2)}) %collective-permute-start.13) | collective-permute-done | bytes 1572896 | tf_op jit(solution)/shard_map/ppermute | solution.py:63
  47.6 1.6 %select_bitcast_fusion.1 = (bf16[4,2,2,1,64,768]{5,4,3,2,1,0:T(8,128)(2,1)S(1)}, bf16[4,2,2,1,64,768]{5,4,3,2,1,0:T(8,128)(2,1)S(1)}) fusion(bf16[4,2,2,64,768]{4,3,2,1,0:T(8,128)(2,1)S(1)} %pad_maximum_fusion.1, bf16[4,2,2,64,768]{4,3,2,1,0:T(8,128)(2,1)} %collective-permute-done.13, pred[]{:T(512)S(6)} %eq.11), kind=kLoop, calls=%fused_computation.13 | loop fusion | flops 1572864 | bytes 6291457 | tf_op jit(solution)/shard_map/jit(_where)/select_n | solution.py:20
  49.5 1.0 %fusion.18 = f32[2048,256]{0,1:T(8,128)S(1)} fusion(bf16[2048,768]{1,0:T(8,128)(2,1)S(1)} %bitcast.48, bf16[512,384]{1,0:T(8,128)(2,1)S(1)} %get-tuple-element.63, bf16[512,384]{1,0:T(8,128)(2,1)S(1)} %get-tuple-element.62), kind=kOutput, calls=%fused_computation.51 | convolution fusion | flops 806092800 | bytes 6029312 | tf_op jit(solution)/shard_map/dot_general | solution.py:34
  50.5 1.0 %fusion.20 = f32[2048,256]{0,1:T(8,128)S(1)} fusion(bf16[2048,768]{1,0:T(8,128)(2,1)S(1)} %bitcast.49, bf16[512,384]{1,0:T(8,128)(2,1)S(1)} %get-tuple-element.62, bf16[512,384]{1,0:T(8,128)(2,1)S(1)} %get-tuple-element.63), kind=kOutput, calls=%fused_computation.53 | convolution fusion | flops 806092800 | bytes 6029312 | tf_op jit(solution)/shard_map/dot_general | solution.py:34
  51.9 0.6 copy-done.1
  52.6 3.7 %collective-permute-start.15 = (bf16[512,256]{0,1:T(8,128)(2,1)S(1)}, bf16[512,256]{0,1:T(8,128)(2,1)S(1)}, u32[]{:S(2)}, u32[]{:S(2)}) collective-permute-start(bf16[512,256]{0,1:T(8,128)(2,1)S(1)} %get-tuple-element.60), channel_id=1, source_target_pairs={{0,8},{4,12},{8,0},{12,4},{16,24},{20,28},{24,16},{28,20},{1,9},{5... | collective-permute-start | bytes 786440 | tf_op jit(solution)/shard_map/ppermute | solution.py:67
  57.2 5.3 %collective-permute-start.21 = (bf16[512,256]{0,1:T(8,128)(2,1)S(1)}, bf16[512,256]{0,1:T(8,128)(2,1)S(1)}, u32[]{:S(2)}, u32[]{:S(2)}) collective-permute-start(bf16[512,256]{0,1:T(8,128)(2,1)S(1)} %get-tuple-element.56), channel_id=1, source_target_pairs={{0,8},{4,12},{8,0},{12,4},{16,24},{20,28},{24,16},{28,20},{1,9},{5... | collective-permute-start | bytes 786440 | tf_op jit(solution)/shard_map/ppermute | solution.py:67
  63.0 1.0 %collective-permute-start.17 = (bf16[512,256]{0,1:T(8,128)(2,1)S(1)}, bf16[512,256]{0,1:T(8,128)(2,1)S(1)}, u32[]{:S(2)}, u32[]{:S(2)}) collective-permute-start(bf16[512,256]{0,1:T(8,128)(2,1)S(1)} %get-tuple-element.35), channel_id=1, source_target_pairs={{0,8},{4,12},{8,0},{12,4},{16,24},{20,28},{24,16},{28,20},{1,9},{5... | collective-permute-start | bytes 786440 | tf_op jit(solution)/shard_map/ppermute | solution.py:67
  64.4 5.3 %collective-permute-done.21 = bf16[512,256]{0,1:T(8,128)(2,1)S(1)} collective-permute-done((bf16[512,256]{0,1:T(8,128)(2,1)S(1)}, bf16[512,256]{0,1:T(8,128)(2,1)S(1)}, u32[]{:S(2)}, u32[]{:S(2)}) %collective-permute-start.21) | collective-permute-done | bytes 262176 | tf_op jit(solution)/shard_map/ppermute | solution.py:67
  69.7 2.1 %collective-permute-start.23 = (bf16[512,256]{0,1:T(8,128)(2,1)S(1)}, bf16[512,256]{0,1:T(8,128)(2,1)S(1)}, u32[]{:S(2)}, u32[]{:S(2)}) collective-permute-start(bf16[512,256]{0,1:T(8,128)(2,1)S(1)} %get-tuple-element.41), channel_id=1, source_target_pairs={{0,8},{4,12},{8,0},{12,4},{16,24},{20,28},{24,16},{28,20},{1,9},{5... | collective-permute-start | bytes 786440 | tf_op jit(solution)/shard_map/ppermute | solution.py:67
  71.9 3.4 %collective-permute-done.17 = bf16[512,256]{0,1:T(8,128)(2,1)S(1)} collective-permute-done((bf16[512,256]{0,1:T(8,128)(2,1)S(1)}, bf16[512,256]{0,1:T(8,128)(2,1)S(1)}, u32[]{:S(2)}, u32[]{:S(2)}) %collective-permute-start.17) | collective-permute-done | bytes 262176 | tf_op jit(solution)/shard_map/ppermute | solution.py:67
  75.5 3.6 %collective-permute-start.18 = (bf16[512,256]{0,1:T(8,128)(2,1)S(1)}, bf16[512,256]{0,1:T(8,128)(2,1)S(1)}, u32[]{:S(2)}, u32[]{:S(2)}) collective-permute-start(bf16[512,256]{0,1:T(8,128)(2,1)S(1)} %get-tuple-element.36), channel_id=1, source_target_pairs={{0,8},{4,12},{8,0},{12,4},{16,24},{20,28},{24,16},{28,20},{1,9},{5... | collective-permute-start | bytes 786440 | tf_op jit(solution)/shard_map/ppermute | solution.py:67
  80.0 0.6 collective-permute-start.28
  81.3 0.4 fusion.6
  81.7 1.3 %collective-permute-start.29 = (bf16[384,256]{0,1:T(8,128)(2,1)S(1)}, bf16[384,256]{0,1:T(8,128)(2,1)S(1)}, u32[]{:S(2)}, u32[]{:S(2)}) collective-permute-start(bf16[384,256]{0,1:T(8,128)(2,1)S(1)} %get-tuple-element.79), channel_id=1, source_target_pairs={{0,4},{4,0},{8,12},{12,8},{16,20},{20,16},{24,28},{28,24},{1,5},{5... | collective-permute-start | bytes 589832 | tf_op jit(solution)/shard_map/ppermute | solution.py:60
  83.3 3.5 %collective-permute-done.28 = bf16[384,256]{0,1:T(8,128)(2,1)S(1)} collective-permute-done((bf16[384,256]{0,1:T(8,128)(2,1)S(1)}, bf16[384,256]{0,1:T(8,128)(2,1)S(1)}, u32[]{:S(2)}, u32[]{:S(2)}) %collective-permute-start.28) | collective-permute-done | bytes 196640 | tf_op jit(solution)/shard_map/ppermute | solution.py:60
  86.8 0.4 collective-permute-start.24
  87.2 1.7 %collective-permute-done.29 = bf16[384,256]{0,1:T(8,128)(2,1)S(1)} collective-permute-done((bf16[384,256]{0,1:T(8,128)(2,1)S(1)}, bf16[384,256]{0,1:T(8,128)(2,1)S(1)}, u32[]{:S(2)}, u32[]{:S(2)}) %collective-permute-start.29) | collective-permute-done | bytes 196640 | tf_op jit(solution)/shard_map/ppermute | solution.py:60
  89.3 0.6 collective-permute-start.26
  89.9 3.3 %collective-permute-done.24 = bf16[512,256]{0,1:T(8,128)(2,1)S(1)} collective-permute-done((bf16[512,256]{0,1:T(8,128)(2,1)S(1)}, bf16[512,256]{0,1:T(8,128)(2,1)S(1)}, u32[]{:S(2)}, u32[]{:S(2)}) %collective-permute-start.24) | collective-permute-done | bytes 262176 | tf_op jit(solution)/shard_map/ppermute | solution.py:67
  93.3 0.6 collective-permute-start.27
  94.0 1.2 %copy.20 = bf16[384,1024]{1,0:T(8,128)(2,1)} copy(bf16[384,1024]{0,1:T(8,128)(2,1)S(1)} %pad_maximum_fusion.2) | data formatting | bytes 1572864
  95.2 3.1 %collective-permute-done.27 = bf16[256,256]{0,1:T(8,128)(2,1)S(1)} collective-permute-done((bf16[256,256]{0,1:T(8,128)(2,1)S(1)}, bf16[256,256]{0,1:T(8,128)(2,1)S(1)}, u32[]{:S(2)}, u32[]{:S(2)}) %collective-permute-start.27) | collective-permute-done | bytes 131104 | tf_op jit(solution)/shard_map/ppermute | solution.py:60
  98.5 1.0 %copy.19 = bf16[256,1024]{1,0:T(8,128)(2,1)} copy(bf16[256,1024]{0,1:T(8,128)(2,1)S(1)} %pad_maximum_fusion.3) | data formatting | bytes 1048576
  (86 shorter events, 6.5 us)
Async XLA Ops:
  0.6 5.2 %copy-start.5 = (bf16[64,3072]{1,0:T(8,128)(2,1)S(1)}, bf16[64,3072]{1,0:T(8,128)(2,1)}, u32[]{:S(2)}) copy-start(bf16[64,3072]{1,0:T(8,128)(2,1)} %param.4) | copy-start | bytes 1179652
  0.6 9.7 %copy-start.4 = (bf16[256,1024]{1,0:T(8,128)(2,1)S(1)}, bf16[256,1024]{1,0:T(8,128)(2,1)}, u32[]{:S(2)}) copy-start(bf16[256,1024]{1,0:T(8,128)(2,1)} %param.5) | copy-start | bytes 1572868
  2.8 17.7 %collective-permute-start.5 = (bf16[512,384]{1,0:T(8,128)(2,1)S(1)}, bf16[512,384]{1,0:T(8,128)(2,1)S(1)}, u32[]{:S(2)}, u32[]{:S(2)}) collective-permute-start(bf16[512,384]{1,0:T(8,128)(2,1)S(1)} %constant_dynamic-slice_fusion.6), channel_id=1, source_target_pairs={{0,4},{4,0},{8,12},{12,8},{16,20},{20,16},{24,28},{28,24},{1,5},{5... | collective-permute-start | bytes 1179656 | tf_op jit(solution)/shard_map/ppermute | solution.py:60
  5.9 7.6 %collective-permute-start.2 = (bf16[64,768]{1,0:T(8,128)(2,1)S(1)}, bf16[64,768]{1,0:T(8,128)(2,1)S(1)}, u32[]{:S(2)}, u32[]{:S(2)}) collective-permute-start(bf16[64,768]{1,0:T(8,128)(2,1)S(1)} %get-tuple-element.83), channel_id=1, source_target_pairs={{0,24},{4,28},{8,16},{12,20},{16,8},{20,12},{24,0},{28,4},{1,25},{... | collective-permute-start | bytes 294920 | tf_op jit(solution)/shard_map/ppermute | solution.py:67
  9.5 8.0 %collective-permute-start.1 = (bf16[64,768]{1,0:T(8,128)(2,1)S(1)}, bf16[64,768]{1,0:T(8,128)(2,1)S(1)}, u32[]{:S(2)}, u32[]{:S(2)}) collective-permute-start(bf16[64,768]{1,0:T(8,128)(2,1)S(1)} %get-tuple-element.84), channel_id=1, source_target_pairs={{0,16},{4,20},{8,24},{12,28},{16,0},{20,4},{24,8},{28,12},{1,17},{... | collective-permute-start | bytes 294920 | tf_op jit(solution)/shard_map/ppermute | solution.py:67
  9.5 8.0 %collective-permute-start = (bf16[64,768]{1,0:T(8,128)(2,1)S(1)}, bf16[64,768]{1,0:T(8,128)(2,1)S(1)}, u32[]{:S(2)}, u32[]{:S(2)}) collective-permute-start(bf16[64,768]{1,0:T(8,128)(2,1)S(1)} %get-tuple-element.82), channel_id=1, source_target_pairs={{0,8},{4,12},{8,0},{12,4},{16,24},{20,28},{24,16},{28,20},{1,9},{5... | collective-permute-start | bytes 294920 | tf_op jit(solution)/shard_map/ppermute | solution.py:67
  10.5 8.1 %collective-permute-start.3 = (bf16[256,256]{0,1:T(8,128)(2,1)S(1)}, bf16[256,256]{0,1:T(8,128)(2,1)S(1)}, u32[]{:S(2)}, u32[]{:S(2)}) collective-permute-start(bf16[256,256]{0,1:T(8,128)(2,1)S(1)} %copy.21), channel_id=1, source_target_pairs={{0,4},{4,0},{8,12},{12,8},{16,20},{20,16},{24,28},{28,24},{1,5},{5... | collective-permute-start | bytes 393224 | tf_op jit(solution)/shard_map/ppermute | solution.py:60
  13.5 7.1 %collective-permute-start.4 = (bf16[256,256]{0,1:T(8,128)(2,1)S(1)}, bf16[256,256]{0,1:T(8,128)(2,1)S(1)}, u32[]{:S(2)}, u32[]{:S(2)}) collective-permute-start(bf16[256,256]{0,1:T(8,128)(2,1)S(1)} %copy.22), channel_id=1, source_target_pairs={{0,4},{4,0},{8,12},{12,8},{16,20},{20,16},{24,28},{28,24},{1,5},{5... | collective-permute-start | bytes 393224 | tf_op jit(solution)/shard_map/ppermute | solution.py:60
  18.6 16.0 %copy-start.2 = (bf16[256,256]{0,1:T(8,128)(2,1)}, bf16[256,256]{0,1:T(8,128)(2,1)S(1)}, u32[]{:S(2)}) copy-start(bf16[256,256]{0,1:T(8,128)(2,1)S(1)} %collective-permute-done.3) | copy-start | bytes 393220
  20.6 3.4 %copy-start.6 = (bf16[512,384]{1,0:T(8,128)(2,1)}, bf16[512,384]{1,0:T(8,128)(2,1)S(1)}, u32[]{:S(2)}) copy-start(bf16[512,384]{1,0:T(8,128)(2,1)S(1)} %collective-permute-done.5) | copy-start | bytes 1179652
  20.6 10.3 %collective-permute-start.6 = (bf16[4,64,768]{2,1,0:T(8,128)(2,1)S(1)}, bf16[4,64,768]{2,1,0:T(8,128)(2,1)S(1)}, u32[]{:S(2)}, u32[]{:S(2)}) collective-permute-start(bf16[4,64,768]{2,1,0:T(8,128)(2,1)S(1)} %pad_maximum_fusion.6), channel_id=1, source_target_pairs={{0,4},{4,0},{8,12},{12,8},{16,20},{20,16},{24,28},{28,24},{1,5},{5... | collective-permute-start | bytes 1179656 | tf_op jit(solution)/shard_map/ppermute | solution.py:60
  22.3 9.8 %collective-permute-start.7 = (bf16[4,64,768]{2,1,0:T(8,128)(2,1)S(1)}, bf16[4,64,768]{2,1,0:T(8,128)(2,1)}, u32[]{:S(2)}, u32[]{:S(2)}) collective-permute-start(bf16[4,64,768]{2,1,0:T(8,128)(2,1)S(1)} %pad_maximum_fusion.6), channel_id=1, source_target_pairs={{0,2},{1,3},{2,0},{3,1},{4,6},{5,7},{6,4},{7,5},{8,10},{9,11},{10,... | collective-permute-start | bytes 1179656 | tf_op jit(solution)/shard_map/ppermute | solution.py:63
  24.0 6.7 %collective-permute-start.8 = (bf16[512,256]{0,1:T(8,128)(2,1)S(1)}, bf16[512,256]{0,1:T(8,128)(2,1)S(1)}, u32[]{:S(2)}, u32[]{:S(2)}) collective-permute-start(bf16[512,256]{0,1:T(8,128)(2,1)S(1)} %pad_maximum_fusion.8), channel_id=1, source_target_pairs={{0,8},{4,12},{8,0},{12,4},{16,24},{20,28},{24,16},{28,20},{1,9},{5... | collective-permute-start | bytes 786440 | tf_op jit(solution)/shard_map/ppermute | solution.py:67
  25.6 5.0 %collective-permute-start.9 = (bf16[512,256]{0,1:T(8,128)(2,1)S(1)}, bf16[512,256]{0,1:T(8,128)(2,1)S(1)}, u32[]{:S(2)}, u32[]{:S(2)}) collective-permute-start(bf16[512,256]{0,1:T(8,128)(2,1)S(1)} %pad_maximum_fusion.8), channel_id=1, source_target_pairs={{0,1},{1,0},{2,3},{3,2},{4,5},{5,4},{6,7},{7,6},{8,16},{9,17},{10,... | collective-permute-start | bytes 786440 | tf_op jit(solution)/shard_map/ppermute | solution.py:83
  30.7 0.7 copy-start.7
  30.7 12.4 %copy-start = (bf16[512,256]{0,1:T(8,128)(2,1)}, bf16[512,256]{0,1:T(8,128)(2,1)S(1)}, u32[]{:S(2)}) copy-start(bf16[512,256]{0,1:T(8,128)(2,1)S(1)} %collective-permute-done.9) | copy-start | bytes 786436
  33.9 8.1 %collective-permute-start.10 = (bf16[4,64,768]{2,1,0:T(8,128)(2,1)}, bf16[4,64,768]{2,1,0:T(8,128)(2,1)}, u32[]{:S(2)}, u32[]{:S(2)}) collective-permute-start(bf16[4,64,768]{2,1,0:T(8,128)(2,1)} %get-tuple-element.80), channel_id=1, source_target_pairs={{0,4},{1,3},{2,6},{3,1},{4,0},{5,7},{6,2},{7,5},{8,12},{9,11},{10,... | collective-permute-start | bytes 1179656 | tf_op jit(solution)/shard_map/ppermute | solution.py:120
  34.7 8.6 %collective-permute-start.11 = (bf16[512,256]{0,1:T(8,128)(2,1)S(1)}, bf16[512,256]{0,1:T(8,128)(2,1)S(1)}, u32[]{:S(2)}, u32[]{:S(2)}) collective-permute-start(bf16[512,256]{0,1:T(8,128)(2,1)S(1)} %pad_maximum_fusion.9), channel_id=1, source_target_pairs={{0,8},{4,12},{8,0},{12,4},{16,24},{20,28},{24,16},{28,20},{1,9},{5... | collective-permute-start | bytes 786440 | tf_op jit(solution)/shard_map/ppermute | solution.py:67
  36.3 7.8 %collective-permute-start.12 = (bf16[512,256]{0,1:T(8,128)(2,1)S(1)}, bf16[512,256]{0,1:T(8,128)(2,1)}, u32[]{:S(2)}, u32[]{:S(2)}) collective-permute-start(bf16[512,256]{0,1:T(8,128)(2,1)S(1)} %pad_maximum_fusion.9), channel_id=1, source_target_pairs={{0,1},{1,0},{2,3},{3,2},{4,5},{5,4},{6,7},{7,6},{8,16},{9,17},{10,... | collective-permute-start | bytes 786440 | tf_op jit(solution)/shard_map/ppermute | solution.py:83
  43.3 0.7 copy-start.9
  44.0 3.5 %collective-permute-start.13 = (bf16[4,2,2,64,768]{4,3,2,1,0:T(8,128)(2,1)S(1)}, bf16[4,2,2,64,768]{4,3,2,1,0:T(8,128)(2,1)}, u32[]{:S(2)}, u32[]{:S(2)}) collective-permute-start(bf16[4,2,2,64,768]{4,3,2,1,0:T(8,128)(2,1)S(1)} %pad_maximum_fusion.1), channel_id=1, source_target_pairs={{0,1},{1,0},{2,3},{3,2},{4,5},{5,4},{6,7},{7,6},{8,9},{9,8},{10,11... | collective-permute-start | bytes 4718600 | tf_op jit(solution)/shard_map/ppermute | solution.py:63
  45.2 6.7 %collective-permute-start.14 = (bf16[512,256]{0,1:T(8,128)(2,1)}, bf16[512,256]{0,1:T(8,128)(2,1)S(1)}, u32[]{:S(2)}, u32[]{:S(2)}) collective-permute-start(bf16[512,256]{0,1:T(8,128)(2,1)} %copy-done.7), channel_id=1, source_target_pairs={{0,1},{1,0},{2,3},{3,2},{4,5},{5,4},{6,7},{7,6},{8,16},{9,17},{10,... | collective-permute-start | bytes 786440 | tf_op jit(solution)/shard_map/ppermute | solution.py:83
  45.7 11.3 %collective-permute-start.20 = (bf16[512,256]{0,1:T(8,128)(2,1)}, bf16[512,256]{0,1:T(8,128)(2,1)S(1)}, u32[]{:S(2)}, u32[]{:S(2)}) collective-permute-start(bf16[512,256]{0,1:T(8,128)(2,1)} %copy-done.9), channel_id=1, source_target_pairs={{0,1},{1,0},{2,3},{3,2},{4,5},{5,4},{6,7},{7,6},{8,16},{9,17},{10,... | collective-permute-start | bytes 786440 | tf_op jit(solution)/shard_map/ppermute | solution.py:83
  51.5 1.0 copy-start.1
  51.5 4.8 %copy-start.8 = (bf16[512,256]{0,1:T(8,128)(2,1)S(1)}, bf16[512,256]{0,1:T(8,128)(2,1)}, u32[]{:S(2)}) copy-start(bf16[512,256]{0,1:T(8,128)(2,1)} %copy-done.7) | copy-start | bytes 786436
  51.9 4.8 %copy-start.10 = (bf16[512,256]{0,1:T(8,128)(2,1)S(1)}, bf16[512,256]{0,1:T(8,128)(2,1)}, u32[]{:S(2)}) copy-start(bf16[512,256]{0,1:T(8,128)(2,1)} %copy-done.9) | copy-start | bytes 786436
  52.6 10.3 %collective-permute-start.15 = (bf16[512,256]{0,1:T(8,128)(2,1)S(1)}, bf16[512,256]{0,1:T(8,128)(2,1)S(1)}, u32[]{:S(2)}, u32[]{:S(2)}) collective-permute-start(bf16[512,256]{0,1:T(8,128)(2,1)S(1)} %get-tuple-element.60), channel_id=1, source_target_pairs={{0,8},{4,12},{8,0},{12,4},{16,24},{20,28},{24,16},{28,20},{1,9},{5... | collective-permute-start | bytes 786440 | tf_op jit(solution)/shard_map/ppermute | solution.py:67
  56.7 5.8 %copy-start.3 = (bf16[256,256]{0,1:T(8,128)(2,1)S(1)}, bf16[256,256]{0,1:T(8,128)(2,1)}, u32[]{:S(2)}) copy-start(bf16[256,256]{0,1:T(8,128)(2,1)} %copy-done.2) | copy-start | bytes 393220
  57.2 12.4 %collective-permute-start.21 = (bf16[512,256]{0,1:T(8,128)(2,1)S(1)}, bf16[512,256]{0,1:T(8,128)(2,1)S(1)}, u32[]{:S(2)}, u32[]{:S(2)}) collective-permute-start(bf16[512,256]{0,1:T(8,128)(2,1)S(1)} %get-tuple-element.56), channel_id=1, source_target_pairs={{0,8},{4,12},{8,0},{12,4},{16,24},{20,28},{24,16},{28,20},{1,9},{5... | collective-permute-start | bytes 786440 | tf_op jit(solution)/shard_map/ppermute | solution.py:67
  63.0 12.3 %collective-permute-start.17 = (bf16[512,256]{0,1:T(8,128)(2,1)S(1)}, bf16[512,256]{0,1:T(8,128)(2,1)S(1)}, u32[]{:S(2)}, u32[]{:S(2)}) collective-permute-start(bf16[512,256]{0,1:T(8,128)(2,1)S(1)} %get-tuple-element.35), channel_id=1, source_target_pairs={{0,8},{4,12},{8,0},{12,4},{16,24},{20,28},{24,16},{28,20},{1,9},{5... | collective-permute-start | bytes 786440 | tf_op jit(solution)/shard_map/ppermute | solution.py:67
  64.0 11.3 %collective-permute-start.16 = (bf16[512,256]{0,1:T(8,128)(2,1)S(1)}, bf16[512,256]{0,1:T(8,128)(2,1)S(1)}, u32[]{:S(2)}, u32[]{:S(2)}) collective-permute-start(bf16[512,256]{0,1:T(8,128)(2,1)S(1)} %add_convert_fusion.3), channel_id=1, source_target_pairs={{0,1},{1,0},{2,3},{3,2},{4,5},{5,4},{6,7},{7,6},{8,16},{9,17},{10,... | collective-permute-start | bytes 786440 | tf_op jit(solution)/shard_map/ppermute | solution.py:83
  69.7 11.1 %collective-permute-start.23 = (bf16[512,256]{0,1:T(8,128)(2,1)S(1)}, bf16[512,256]{0,1:T(8,128)(2,1)S(1)}, u32[]{:S(2)}, u32[]{:S(2)}) collective-permute-start(bf16[512,256]{0,1:T(8,128)(2,1)S(1)} %get-tuple-element.41), channel_id=1, source_target_pairs={{0,8},{4,12},{8,0},{12,4},{16,24},{20,28},{24,16},{28,20},{1,9},{5... | collective-permute-start | bytes 786440 | tf_op jit(solution)/shard_map/ppermute | solution.py:67
  71.8 11.2 %collective-permute-start.22 = (bf16[512,256]{0,1:T(8,128)(2,1)S(1)}, bf16[512,256]{0,1:T(8,128)(2,1)S(1)}, u32[]{:S(2)}, u32[]{:S(2)}) collective-permute-start(bf16[512,256]{0,1:T(8,128)(2,1)S(1)} %add_convert_fusion.1), channel_id=1, source_target_pairs={{0,1},{1,0},{2,3},{3,2},{4,5},{5,4},{6,7},{7,6},{8,16},{9,17},{10,... | collective-permute-start | bytes 786440 | tf_op jit(solution)/shard_map/ppermute | solution.py:83
  75.4 13.6 %collective-permute-start.19 = (bf16[512,256]{0,1:T(8,128)(2,1)S(1)}, bf16[512,256]{0,1:T(8,128)(2,1)S(1)}, u32[]{:S(2)}, u32[]{:S(2)}) collective-permute-start(bf16[512,256]{0,1:T(8,128)(2,1)S(1)} %get-tuple-element.37), channel_id=1, source_target_pairs={{0,1},{1,0},{2,3},{3,2},{4,5},{5,4},{6,7},{7,6},{8,16},{9,17},{10,... | collective-permute-start | bytes 786440 | tf_op jit(solution)/shard_map/ppermute | solution.py:83
  75.5 13.6 %collective-permute-start.18 = (bf16[512,256]{0,1:T(8,128)(2,1)S(1)}, bf16[512,256]{0,1:T(8,128)(2,1)S(1)}, u32[]{:S(2)}, u32[]{:S(2)}) collective-permute-start(bf16[512,256]{0,1:T(8,128)(2,1)S(1)} %get-tuple-element.36), channel_id=1, source_target_pairs={{0,8},{4,12},{8,0},{12,4},{16,24},{20,28},{24,16},{28,20},{1,9},{5... | collective-permute-start | bytes 786440 | tf_op jit(solution)/shard_map/ppermute | solution.py:67
  80.0 6.8 %collective-permute-start.28 = (bf16[384,256]{0,1:T(8,128)(2,1)S(1)}, bf16[384,256]{0,1:T(8,128)(2,1)S(1)}, u32[]{:S(2)}, u32[]{:S(2)}) collective-permute-start(bf16[384,256]{0,1:T(8,128)(2,1)S(1)} %get-tuple-element.77), channel_id=1, source_target_pairs={{0,4},{4,0},{8,12},{12,8},{16,20},{20,16},{24,28},{28,24},{1,5},{5... | collective-permute-start | bytes 589832 | tf_op jit(solution)/shard_map/ppermute | solution.py:60
  81.7 7.2 %collective-permute-start.29 = (bf16[384,256]{0,1:T(8,128)(2,1)S(1)}, bf16[384,256]{0,1:T(8,128)(2,1)S(1)}, u32[]{:S(2)}, u32[]{:S(2)}) collective-permute-start(bf16[384,256]{0,1:T(8,128)(2,1)S(1)} %get-tuple-element.79), channel_id=1, source_target_pairs={{0,4},{4,0},{8,12},{12,8},{16,20},{20,16},{24,28},{28,24},{1,5},{5... | collective-permute-start | bytes 589832 | tf_op jit(solution)/shard_map/ppermute | solution.py:60
  83.2 6.7 %collective-permute-start.25 = (bf16[512,256]{0,1:T(8,128)(2,1)S(1)}, bf16[512,256]{0,1:T(8,128)(2,1)S(1)}, u32[]{:S(2)}, u32[]{:S(2)}) collective-permute-start(bf16[512,256]{0,1:T(8,128)(2,1)S(1)} %get-tuple-element.43), channel_id=1, source_target_pairs={{0,1},{1,0},{2,3},{3,2},{4,5},{5,4},{6,7},{7,6},{8,16},{9,17},{10,... | collective-permute-start | bytes 786440 | tf_op jit(solution)/shard_map/ppermute | solution.py:83
  86.8 6.4 %collective-permute-start.24 = (bf16[512,256]{0,1:T(8,128)(2,1)S(1)}, bf16[512,256]{0,1:T(8,128)(2,1)S(1)}, u32[]{:S(2)}, u32[]{:S(2)}) collective-permute-start(bf16[512,256]{0,1:T(8,128)(2,1)S(1)} %get-tuple-element.42), channel_id=1, source_target_pairs={{0,8},{4,12},{8,0},{12,4},{16,24},{20,28},{24,16},{28,20},{1,9},{5... | collective-permute-start | bytes 786440 | tf_op jit(solution)/shard_map/ppermute | solution.py:67
  89.3 6.0 %collective-permute-start.26 = (bf16[256,256]{0,1:T(8,128)(2,1)S(1)}, bf16[256,256]{0,1:T(8,128)(2,1)S(1)}, u32[]{:S(2)}, u32[]{:S(2)}) collective-permute-start(bf16[256,256]{0,1:T(8,128)(2,1)S(1)} %get-tuple-element.86), channel_id=1, source_target_pairs={{0,4},{4,0},{8,12},{12,8},{16,20},{20,16},{24,28},{28,24},{1,5},{5... | collective-permute-start | bytes 393224 | tf_op jit(solution)/shard_map/ppermute | solution.py:60
  93.3 5.0 %collective-permute-start.27 = (bf16[256,256]{0,1:T(8,128)(2,1)S(1)}, bf16[256,256]{0,1:T(8,128)(2,1)S(1)}, u32[]{:S(2)}, u32[]{:S(2)}) collective-permute-start(bf16[256,256]{0,1:T(8,128)(2,1)S(1)} %get-tuple-element.88), channel_id=1, source_target_pairs={{0,4},{4,0},{8,12},{12,8},{16,20},{20,16},{24,28},{28,24},{1,5},{5... | collective-permute-start | bytes 393224 | tf_op jit(solution)/shard_map/ppermute | solution.py:60

commit v4 on v3

v4 whole, which is shorter than its diff:
```python
import math

import jax
import jax.numpy as jnp
from jax import lax
from jax.sharding import PartitionSpec as P

BLOCK = 32
PAIR = 2
LINE = 4


def dequantize(codes_part, scales_part):
    expanded = jnp.repeat(scales_part.astype(jnp.float32), BLOCK, axis=0)
    return (codes_part.astype(jnp.float32) * expanded).astype(jnp.bfloat16)


def halves(own, other, side, axis):
    first = jnp.where(side == 0, own, other)
    second = jnp.where(side == 0, other, own)
    return jnp.concatenate([first, second], axis)


def pair(own, other, side, axis):
    return halves(jnp.expand_dims(own, axis), jnp.expand_dims(other, axis), side, axis)


def together(*arrays):
    return lax.optimization_barrier(arrays)


def by_feature(rows, weight):
    return lax.dot_general(
        rows, weight, (((1,), (1,)), ((), ())), preferred_element_type=jnp.float32
    )


def by_token(columns, rows):
    return lax.dot_general(
        columns, rows, (((0,), (0,)), ((), ())), preferred_element_type=jnp.float32
    )


def body(grad_out, attn_out, weight_codes, block_scales):
    n_dp, n_mp = lax.axis_size("dp"), lax.axis_size("mp")
    layers = n_dp // PAIR
    bits = n_mp.bit_length() - 1
    group_rows, heads = attn_out.shape
    own_features = weight_codes.shape[1]
    half = heads // PAIR
    layer_features = PAIR * own_features
    scaling = 1.0 / math.sqrt(group_rows * n_dp)

    dp, mp = lax.axis_index("dp"), lax.axis_index("mp")
    layer, side = dp // PAIR, dp % PAIR
    middle = (layer > 0) & (layer < layers - 1)

    def swap_x(piece):
        return lax.ppermute(piece, "dp", [(i, i ^ 1) for i in range(n_dp)])

    def with_mp(piece, k):
        bit = n_mp >> (k + 1)
        other = lax.ppermute(piece, "mp", [(i, i ^ bit) for i in range(n_mp)])
        return pair(piece, other, (mp // bit) % 2, 1 + k)

    def move_layers(piece, to):
        moves = [(i, to(i // PAIR) * PAIR + i % PAIR) for i in range(n_dp)]
        return lax.ppermute(piece, "dp", moves)

    def outer(piece):
        return move_layers(piece, lambda z: z ^ 1)

    between = []
    for i in range(n_dp):
        z, x = i // PAIR, i % PAIR
        for j in range(n_mp):
            if z in (0, layers - 1):
                there = i, j ^ 1
            else:
                there = (((z - 1) ^ 1) + 1) * PAIR + x, j
            between.append((i * n_mp + j, there[0] * n_mp + there[1]))

    def inner(piece):
        return lax.ppermute(piece, ("dp", "mp"), between)

    slots = []
    for s in range(layers):
        piece = lax.dynamic_slice_in_dim(
            grad_out, (layer ^ s) * layer_features, layer_features, 1
        )
        slots.append(move_layers(piece, lambda z: z ^ s) if s else piece)
    held = jnp.stack(slots)

    attn_own = lax.dynamic_slice_in_dim(attn_out, side * half, half, 1)
    attn_other = swap_x(lax.dynamic_slice_in_dim(attn_out, (1 - side) * half, half, 1))
    weight = dequantize(weight_codes, block_scales)
    weight_other = swap_x(weight)
    weight_slab = halves(weight, weight_other, side, 1)

    held, attn_other = together(held, attn_other)
    attn = jnp.stack([attn_own, attn_other])
    if layers == LINE:
        attn_1, attn_in = outer(attn), inner(attn)

    for k in range(bits - 1):
        held = with_mp(held, k)
    cols = with_mp(held, bits - 1).reshape(layers, group_rows, layer_features)
    held_other = swap_x(held)
    cols_other = with_mp(held_other, bits - 1).reshape(cols.shape)

    def terms(k):
        stream = weight_slab[k * half : (k + 1) * half]
        part = by_feature(cols.reshape(-1, layer_features), stream)
        return part.reshape(layers, group_rows, half)

    streams = range(PAIR)
    part = [terms(k) for k in streams]
    if layers == LINE:
        outer_2, inner_2, outer_3, inner_3, gas = [], [], [], [], []
        for k in streams:
            send = jnp.where(middle, attn_in[k], part[k][3].astype(jnp.bfloat16))
            send_outer, send_inner = together(send, attn_1[k])
            outer_2.append(outer(send_outer))
            inner_2.append(inner(send_inner))
        for k in streams:
            send_outer = jnp.where(middle, inner_2[k], part[k][2].astype(jnp.bfloat16))
            send_inner = (part[k][2] + outer_2[k].astype(jnp.float32)).astype(jnp.bfloat16)
            send_outer, send_inner = together(send_outer, send_inner)
            outer_3.append(outer(send_outer))
            inner_3.append(inner(send_inner))
        for k in streams:
            send_inner = (part[k][3] + outer_3[k].astype(jnp.float32)).astype(jnp.bfloat16)
            send_outer = part[k][1] + jnp.where(middle, inner_3[k].astype(jnp.float32), 0.0)
            send_outer, send_inner = together(send_outer.astype(jnp.bfloat16), send_inner)
            outer_4, inner_4 = outer(send_outer), inner(send_inner)
            ga = part[k][0] + outer_4.astype(jnp.float32)
            gas.append(ga + jnp.where(middle, inner_4.astype(jnp.float32), 0.0))
        total = 0.0
        for k, side_cols in enumerate((cols, cols_other)):
            attn_2 = jnp.where(middle, inner_2[k], outer_2[k])
            total = total + by_token(side_cols[0], attn[k]) + by_token(side_cols[1], attn_1[k])
            total = total + by_token(side_cols[2], attn_2)
        for k, side_cols in enumerate((cols, cols_other)):
            attn_3 = jnp.where(middle, attn_in[k], outer_3[k])
            total = total + by_token(side_cols[3], attn_3)
    else:
        lines = [[z * PAIR + x for z in range(layers)] for x in range(PAIR)]
        total = 0.0
        for k, side_cols in enumerate((cols, cols_other)):
            attn_all = lax.all_gather(
                attn[k], "dp", axis=0, tiled=True, axis_index_groups=lines
            )
            ordered = side_cols[jnp.arange(layers) ^ layer].reshape(-1, layer_features)
            total = total + by_token(ordered, attn_all)
        gas = []
        for k in streams:
            ordered = part[k][jnp.arange(layers) ^ layer].reshape(-1, half)
            gas.append(
                lax.psum_scatter(
                    ordered, "dp", scatter_dimension=0, tiled=True, axis_index_groups=lines
                )
            )

    gw = (scaling * total).astype(jnp.bfloat16)
    gw_own = lax.dynamic_slice_in_dim(gw, side * own_features, own_features, 0)
    gw_other = swap_x(lax.dynamic_slice_in_dim(gw, (1 - side) * own_features, own_features, 0))
    grad_weight_t = halves(gw_own, gw_other, side, 1)
    grad_attn = jnp.concatenate(gas, 1).astype(jnp.bfloat16)
    return grad_attn, grad_weight_t


def solution(mesh):
    placed = (P(("dp", "mp"), None), P("dp", "mp"), P("mp", "dp"), P("mp", "dp"))
    return jax.shard_map(
        body, mesh=mesh, in_specs=placed, out_specs=(P("dp", "mp"), P("dp", "mp")), check_vma=False
    )
```

time: 99.9 us -> 86.4 us (0.86)
  starting transfers between devices: 35.2 us -> 22.1 us
  waiting for transfers between devices: 43.4 us -> 47.1 us
  other arithmetic: 9.99 us -> 6.66 us
    ppermute x11 -> x10, starting transfers between devices: 23.9 us -> 14.6 us  [move_layers(): return lax.ppermute(piece, 'dp', moves)]
    ppermute x8 -> x4, waiting for transfers between devices: 11.5 us -> 15.4 us  [swap_x(): return lax.ppermute(piece, 'dp', [(i, i ^ 1) for i in range(n_dp)])]
    ppermute x8 -> x4, starting transfers between devices: 8.45 us -> 4.66 us  [swap_x(): return lax.ppermute(piece, 'dp', [(i, i ^ 1) for i in range(n_dp)])]
    unnamed x30 -> x9, local copies, waits for them, and re-layouts: 4.38 us -> 2.32 us
    convert_element_type x1, other arithmetic: 1.28 us -> 0.15 us  [dequantize(): return (codes_part.astype(jnp.float32) * expanded).astype(jnp.bfloat16)]
    dynamic_slice x4 -> x3, local copies, waits for them, and re-layouts: 0.22 us -> 1.33 us  [the longest x2 1.29 us: body(): attn_own = lax.dynamic_slice_in_dim(attn_out, side * half, half, 1)]
    ppermute x3, waiting for transfers between devices: 8.29 us -> 7.24 us  [with_mp(): other = lax.ppermute(piece, 'mp', [(i, i ^ bit) for i in range(n_mp)])]
    select_n x1, other arithmetic: 1.15 us -> 0.11 us  [halves(): second = jnp.where(side == 0, other, own)]
  transfers between devices with their start and end apart: 30 -> 24, of which waited for: 16 -> 11; matrix products, arithmetic and copies ran while one was open for 13% -> 15% of each run, Pallas kernels for 0% -> 0%
where the time goes in v4:
time: 86.4 us; the launch traced here: 86.1 us
  waiting for transfers between devices  47.1 us (55%)
  starting transfers between devices  22.1 us (26%)
  other arithmetic  6.66 us (8%)
  matrix products  5.39 us (6%)
  local copies, waits for them, and re-layouts  3.83 us (4%)
  between operations  1.01 us (1%)
    ppermute x10, waiting for transfers between devices, move_layers(): return lax.ppermute(piece, 'dp', moves)  24.5 us
    ppermute x4, waiting for transfers between devices, swap_x(): return lax.ppermute(piece, 'dp', [(i, i ^ 1) for i in range(n_dp)])  15.4 us
    ppermute x10, starting transfers between devices, move_layers(): return lax.ppermute(piece, 'dp', moves)  14.6 us
    ppermute x3, waiting for transfers between devices, with_mp(): other = lax.ppermute(piece, 'mp', [(i, i ^ bit) for i in range(n_mp)])  7.24 us
    ppermute x4, starting transfers between devices, swap_x(): return lax.ppermute(piece, 'dp', [(i, i ^ 1) for i in range(n_dp)])  4.66 us
    select_n x4, other arithmetic, halves(): first = jnp.where(side == 0, own, other)  3.76 us
    dot_general x8, matrix products, by_token(): lax.dot_general(columns, rows, (((0,), (0,)), ((), ())), preferred_elemen...  3.37 us
    unnamed x9, local copies, waits for them, and re-layouts  2.32 us
  transfers between devices with their start and end apart: 24, of which 11 were waited for; matrix products, arithmetic and copies ran while one was open for 15% of the time, Pallas kernels for 0%

profile of v4, /device:TPU:0, one launch (start us, length us, event | category | flops | bytes accessed | tf_op | source)
XLA Modules:
  0.0 86.1 jit_solution(16538037428092499193)
XLA Ops:
  0.7 1.2 %constant_dynamic-slice_fusion.1 = (bf16[256,512]{1,0:T(8,128)(2,1)S(1)}, bf16[256,512]{1,0:T(8,128)(2,1)S(1)}) fusion(bf16[256,1024]{1,0:T(8,128)(2,1)} %param.5, s32[]{:T(128)S(6)} %select_n.202, s32[]{:T(128)S(6)} %select_n.189), kind=kLoop, calls=%fused_computation.88 | loop fusion | bytes 1048584 | tf_op jit(solution)/shard_map/dynamic_slice | solution.py:94
  2.0 3.0 %collective-permute-start.3 = (bf16[256,512]{0,1:T(8,128)(2,1)S(1)}, bf16[256,512]{0,1:T(8,128)(2,1)S(1)}, u32[]{:S(2)}, u32[]{:S(2)}) collective-permute-start(bf16[256,512]{0,1:T(8,128)(2,1)S(1)} %copy.20), channel_id=1, source_target_pairs={{0,4},{4,0},{8,12},{12,8},{16,20},{20,16},{24,28},{28,24},{1,5},{5... | collective-permute-start | bytes 786440 | tf_op jit(solution)/shard_map/ppermute | solution.py:59
  5.0 3.7 %collective-permute-start.2 = (bf16[64,768]{1,0:T(8,128)(2,1)S(1)}, bf16[64,768]{1,0:T(8,128)(2,1)S(1)}, u32[]{:S(2)}, u32[]{:S(2)}) collective-permute-start(bf16[64,768]{1,0:T(8,128)(2,1)S(1)} %get-tuple-element.64), channel_id=1, source_target_pairs={{0,24},{4,28},{8,16},{12,20},{16,8},{20,12},{24,0},{28,4},{1,25},{... | collective-permute-start | bytes 294920 | tf_op jit(solution)/shard_map/ppermute | solution.py:68
  8.7 0.8 collective-permute-start
  9.5 3.1 %collective-permute-done.2 = bf16[64,768]{1,0:T(8,128)(2,1)S(1)} collective-permute-done((bf16[64,768]{1,0:T(8,128)(2,1)S(1)}, bf16[64,768]{1,0:T(8,128)(2,1)S(1)}, u32[]{:S(2)}, u32[]{:S(2)}) %collective-permute-start.2) | collective-permute-done | bytes 98336 | tf_op jit(solution)/shard_map/ppermute | solution.py:68
  12.6 4.1 %collective-permute-done.1 = bf16[64,768]{1,0:T(8,128)(2,1)S(1)} collective-permute-done((bf16[64,768]{1,0:T(8,128)(2,1)S(1)}, bf16[64,768]{1,0:T(8,128)(2,1)S(1)}, u32[]{:S(2)}, u32[]{:S(2)}) %collective-permute-start.1) | collective-permute-done | bytes 98336 | tf_op jit(solution)/shard_map/ppermute | solution.py:68
  16.8 1.6 %collective-permute-start.4 = (bf16[4,64,768]{2,1,0:T(8,128)(2,1)S(1)}, bf16[4,64,768]{2,1,0:T(8,128)(2,1)}, u32[]{:S(2)}, u32[]{:S(2)}) collective-permute-start(bf16[4,64,768]{2,1,0:T(8,128)(2,1)S(1)} %pad_maximum_fusion.8), channel_id=1, source_target_pairs={{0,2},{1,3},{2,0},{3,1},{4,6},{5,7},{6,4},{7,5},{8,10},{9,11},{10,... | collective-permute-start | bytes 1179656 | tf_op jit(solution)/shard_map/ppermute | solution.py:63
  18.4 0.1 fusion
  18.5 0.6 collective-permute-start.6
  19.3 0.6 collective-permute-start.8
  19.9 7.2 %collective-permute-done.4 = bf16[4,64,768]{2,1,0:T(8,128)(2,1)} collective-permute-done((bf16[4,64,768]{2,1,0:T(8,128)(2,1)S(1)}, bf16[4,64,768]{2,1,0:T(8,128)(2,1)}, u32[]{:S(2)}, u32[]{:S(2)}) %collective-permute-start.4) | collective-permute-done | bytes 393248 | tf_op jit(solution)/shard_map/ppermute | solution.py:63
  27.1 1.1 %select_bitcast_fusion.5 = (bf16[4,1,64,768]{3,2,1,0:T(8,128)(2,1)S(1)}, bf16[4,1,64,768]{3,2,1,0:T(8,128)(2,1)S(1)}) fusion(bf16[4,64,768]{2,1,0:T(8,128)(2,1)S(1)} %pad_maximum_fusion.8, bf16[4,64,768]{2,1,0:T(8,128)(2,1)} %collective-permute-done.4, pred[]{:T(512)S(6)} %eq.22), kind=kLoop, calls=%fused_computation.63 | loop fusion | flops 393216 | bytes 1572865 | tf_op jit(solution)/shard_map/jit(_where)/select_n | solution.py:19
  28.2 1.0 %pad_maximum_fusion.3 = bf16[4,2,64,768]{3,2,1,0:T(8,128)(2,1)} fusion(bf16[4,1,64,768]{3,2,1,0:T(8,128)(2,1)S(1)} %get-tuple-element.55, bf16[4,1,64,768]{3,2,1,0:T(8,128)(2,1)S(1)} %get-tuple-element.54), kind=kLoop, calls=%fused_computation.25 | loop fusion | flops 393216 | bytes 1572864 | tf_op jit(solution)/shard_map/concatenate | solution.py:21
  29.2 0.5 collective-permute-start.7
  29.7 0.4 collective-permute-start.21
  30.1 1.7 %collective-permute-done.8 = bf16[2,256,512]{1,2,0:T(8,128)(2,1)S(1)} collective-permute-done((bf16[2,256,512]{1,2,0:T(8,128)(2,1)S(1)}, bf16[2,256,512]{1,2,0:T(8,128)(2,1)S(1)}, u32[]{:S(2)}, u32[]{:S(2)}) %collective-permute-start.8) | collective-permute-done | bytes 524320 | tf_op jit(solution)/shard_map/ppermute | solution.py:68
  31.9 7.3 %collective-permute-done.6 = bf16[1024,384]{1,0:T(8,128)(2,1)} collective-permute-done((bf16[1024,384]{1,0:T(8,128)(2,1)S(1)}, bf16[1024,384]{1,0:T(8,128)(2,1)}, u32[]{:S(2)}, u32[]{:S(2)}) %collective-permute-start.6) | collective-permute-done | bytes 786464 | tf_op jit(solution)/shard_map/ppermute | solution.py:59
  39.2 1.3 %broadcast_select_fusion.1 = (bf16[1024,384]{1,0:T(8,128)(2,1)S(1)}, bf16[1024,384]{1,0:T(8,128)(2,1)S(1)}) fusion(bf16[1024,384]{1,0:T(8,128)(2,1)S(1)} %fusion, bf16[1024,384]{1,0:T(8,128)(2,1)} %collective-permute-done.6, pred[]{:T(512)S(6)} %eq.23), kind=kLoop, calls=%fused_computation.32 | loop fusion | flops 786432 | bytes 3145729 | tf_op jit(solution)/shard_map/jit(_where)/select_n | solution.py:19
  40.5 1.2 %select_bitcast_fusion.3 = (bf16[4,2,1,64,768]{4,3,2,1,0:T(8,128)(2,1)S(1)}, bf16[4,2,1,64,768]{4,3,2,1,0:T(8,128)(2,1)S(1)}) fusion(bf16[4,2,64,768]{3,2,1,0:T(8,128)(2,1)} %collective-permute-done.5, pred[]{:T(512)S(6)} %eq.11, bf16[4,1,64,768]{3,2,1,0:T(8,128)(2,1)S(1)} %get-tuple-element.55, bf16[4,1,64,768]{3,2,1,0:T(8,128)(2,1)S(1)} %get-tuple-element.54), kind=kLoop, calls=%fused_computation.30 | loop fusion | flops 1179648 | bytes 3145729 | tf_op jit(solution)/shard_map/jit(_where)/select_n | solution.py:19
  41.7 0.2 pad_maximum_fusion
  41.9 1.0 %fusion.4 = f32[1024,512]{0,1:T(8,128)S(1)} fusion(bf16[1024,768]{1,0:T(8,128)(2,1)S(1)} %bitcast.69, bf16[1024,384]{1,0:T(8,128)(2,1)S(1)} %get-tuple-element.49, bf16[1024,384]{1,0:T(8,128)(2,1)S(1)} %get-tuple-element.48), kind=kOutput, calls=%fused_computation.23 | convolution fusion | flops 806879232 | bytes 5242880 | tf_op jit(solution)/shard_map/dot_general | solution.py:33
  42.9 1.0 %fusion.2 = f32[1024,512]{0,1:T(8,128)S(1)} fusion(bf16[1024,768]{1,0:T(8,128)(2,1)S(1)} %bitcast.70, bf16[1024,384]{1,0:T(8,128)(2,1)S(1)} %get-tuple-element.48, bf16[1024,384]{1,0:T(8,128)(2,1)S(1)} %get-tuple-element.49), kind=kOutput, calls=%fused_computation.21 | convolution fusion | flops 806879232 | bytes 5242880 | tf_op jit(solution)/shard_map/dot_general | solution.py:33
  44.1 0.7 collective-permute-start.16
  44.8 3.0 %collective-permute-start.10 = (bf16[256,512]{0,1:T(8,128)(2,1)S(1)}, bf16[256,512]{0,1:T(8,128)(2,1)S(1)}, u32[]{:S(2)}, u32[]{:S(2)}) collective-permute-start(bf16[256,512]{0,1:T(8,128)(2,1)S(1)} %get-tuple-element.19), channel_id=1, source_target_pairs={{0,8},{4,12},{8,0},{12,4},{16,24},{20,28},{24,16},{28,20},{1,9},{5... | collective-permute-start | bytes 786440 | tf_op jit(solution)/shard_map/ppermute | solution.py:68
  47.9 0.4 fusion.41
  48.3 5.5 %collective-permute-done.21 = bf16[4,2,64,768]{3,2,1,0:T(8,128)(2,1)S(1)} collective-permute-done((bf16[4,2,64,768]{3,2,1,0:T(8,128)(2,1)}, bf16[4,2,64,768]{3,2,1,0:T(8,128)(2,1)S(1)}, u32[]{:S(2)}, u32[]{:S(2)}) %collective-permute-start.21) | collective-permute-done | bytes 786464 | tf_op jit(solution)/shard_map/ppermute | solution.py:59
  53.8 0.4 fusion.39
  54.5 0.6 collective-permute-start.17
  55.1 3.8 %collective-permute-done.10 = bf16[256,512]{0,1:T(8,128)(2,1)S(1)} collective-permute-done((bf16[256,512]{0,1:T(8,128)(2,1)S(1)}, bf16[256,512]{0,1:T(8,128)(2,1)S(1)}, u32[]{:S(2)}, u32[]{:S(2)}) %collective-permute-start.10) | collective-permute-done | bytes 262176 | tf_op jit(solution)/shard_map/ppermute | solution.py:68
  59.0 0.7 collective-permute-start.12
  59.7 0.4 fusion.31
  60.0 4.5 %collective-permute-done.18 = bf16[256,512]{0,1:T(8,128)(2,1)S(1)} collective-permute-done((bf16[256,512]{0,1:T(8,128)(2,1)S(1)}, bf16[256,512]{0,1:T(8,128)(2,1)S(1)}, u32[]{:S(2)}, u32[]{:S(2)}) %collective-permute-start.18) | collective-permute-done | bytes 262176 | tf_op jit(solution)/shard_map/ppermute | solution.py:68
  64.5 0.2 add_convert_fusion
  64.8 2.5 %collective-permute-start.19 = (bf16[256,512]{0,1:T(8,128)(2,1)S(1)}, bf16[256,512]{0,1:T(8,128)(2,1)S(1)}, u32[]{:S(2)}, u32[]{:S(2)}) collective-permute-start(bf16[256,512]{0,1:T(8,128)(2,1)S(1)} %get-tuple-element.28), channel_id=1, source_target_pairs={{0,8},{4,12},{8,0},{12,4},{16,24},{20,28},{24,16},{28,20},{1,9},{5... | collective-permute-start | bytes 786440 | tf_op jit(solution)/shard_map/ppermute | solution.py:68
  67.3 2.8 %collective-permute-done.12 = bf16[256,512]{0,1:T(8,128)(2,1)S(1)} collective-permute-done((bf16[256,512]{0,1:T(8,128)(2,1)S(1)}, bf16[256,512]{0,1:T(8,128)(2,1)S(1)}, u32[]{:S(2)}, u32[]{:S(2)}) %collective-permute-start.12) | collective-permute-done | bytes 262176 | tf_op jit(solution)/shard_map/ppermute | solution.py:68
  70.1 0.2 add_convert_fusion.2
  70.4 2.5 %collective-permute-start.13 = (bf16[256,512]{0,1:T(8,128)(2,1)S(1)}, bf16[256,512]{0,1:T(8,128)(2,1)S(1)}, u32[]{:S(2)}, u32[]{:S(2)}) collective-permute-start(bf16[256,512]{0,1:T(8,128)(2,1)S(1)} %get-tuple-element.22), channel_id=1, source_target_pairs={{0,8},{4,12},{8,0},{12,4},{16,24},{20,28},{24,16},{28,20},{1,9},{5... | collective-permute-start | bytes 786440 | tf_op jit(solution)/shard_map/ppermute | solution.py:68
  72.9 0.4 fusion.27
  73.7 0.4 fusion.42
  74.1 0.4 fusion.29
  74.5 0.4 fusion.40
  74.9 0.7 multiply_convert_fusion
  75.6 0.6 collective-permute-start.23
  76.4 4.5 %collective-permute-done.13 = bf16[256,512]{0,1:T(8,128)(2,1)S(1)} collective-permute-done((bf16[256,512]{0,1:T(8,128)(2,1)S(1)}, bf16[256,512]{0,1:T(8,128)(2,1)S(1)}, u32[]{:S(2)}, u32[]{:S(2)}) %collective-permute-start.13) | collective-permute-done | bytes 262176 | tf_op jit(solution)/shard_map/ppermute | solution.py:68
  81.0 1.0 %copy.18 = bf16[256,1024]{1,0:T(8,128)(2,1)} copy(bf16[256,1024]{0,1:T(8,128)(2,1)S(1)} %pad_maximum_fusion.6) | data formatting | bytes 1048576
  82.0 2.6 %collective-permute-done.23 = bf16[384,512]{0,1:T(8,128)(2,1)S(1)} collective-permute-done((bf16[384,512]{0,1:T(8,128)(2,1)S(1)}, bf16[384,512]{0,1:T(8,128)(2,1)S(1)}, u32[]{:S(2)}, u32[]{:S(2)}) %collective-permute-start.23) | collective-permute-done | bytes 393248 | tf_op jit(solution)/shard_map/ppermute | solution.py:59
  84.7 0.2 broadcast_select_fusion.3
  85.0 1.2 %copy.19 = bf16[384,1024]{1,0:T(8,128)(2,1)} copy(bf16[384,1024]{0,1:T(8,128)(2,1)S(1)} %pad_maximum_fusion.4) | data formatting | bytes 1572864
  (52 shorter events, 2.1 us)
Async XLA Ops:
  0.6 4.4 %copy-start.1 = (bf16[64,3072]{1,0:T(8,128)(2,1)S(1)}, bf16[64,3072]{1,0:T(8,128)(2,1)}, u32[]{:S(2)}) copy-start(bf16[64,3072]{1,0:T(8,128)(2,1)} %param.4) | copy-start | bytes 1179652
  0.7 17.7 %copy-start.2 = (bf16[32,384]{1,0:T(8,128)(2,1)S(1)}, bf16[32,384]{1,0:T(8,128)(2,1)}, u32[]{:S(2)}) copy-start(bf16[32,384]{1,0:T(8,128)(2,1)} %param.7) | copy-start | bytes 73732
  0.7 17.7 %copy-start = (bf16[1024,384]{1,0:T(8,128)(2,1)S(1)}, bf16[1024,384]{1,0:T(8,128)(2,1)}, u32[]{:S(2)}) copy-start(bf16[1024,384]{1,0:T(8,128)(2,1)} %param.6) | copy-start | bytes 2359300
  2.0 14.8 %collective-permute-start.3 = (bf16[256,512]{0,1:T(8,128)(2,1)S(1)}, bf16[256,512]{0,1:T(8,128)(2,1)S(1)}, u32[]{:S(2)}, u32[]{:S(2)}) collective-permute-start(bf16[256,512]{0,1:T(8,128)(2,1)S(1)} %copy.20), channel_id=1, source_target_pairs={{0,4},{4,0},{8,12},{12,8},{16,20},{20,16},{24,28},{28,24},{1,5},{5... | collective-permute-start | bytes 786440 | tf_op jit(solution)/shard_map/ppermute | solution.py:59
  5.0 7.6 %collective-permute-start.2 = (bf16[64,768]{1,0:T(8,128)(2,1)S(1)}, bf16[64,768]{1,0:T(8,128)(2,1)S(1)}, u32[]{:S(2)}, u32[]{:S(2)}) collective-permute-start(bf16[64,768]{1,0:T(8,128)(2,1)S(1)} %get-tuple-element.64), channel_id=1, source_target_pairs={{0,24},{4,28},{8,16},{12,20},{16,8},{20,12},{24,0},{28,4},{1,25},{... | collective-permute-start | bytes 294920 | tf_op jit(solution)/shard_map/ppermute | solution.py:68
  8.7 8.0 %collective-permute-start.1 = (bf16[64,768]{1,0:T(8,128)(2,1)S(1)}, bf16[64,768]{1,0:T(8,128)(2,1)S(1)}, u32[]{:S(2)}, u32[]{:S(2)}) collective-permute-start(bf16[64,768]{1,0:T(8,128)(2,1)S(1)} %get-tuple-element.65), channel_id=1, source_target_pairs={{0,16},{4,20},{8,24},{12,28},{16,0},{20,4},{24,8},{28,12},{1,17},{... | collective-permute-start | bytes 294920 | tf_op jit(solution)/shard_map/ppermute | solution.py:68
  8.7 8.0 %collective-permute-start = (bf16[64,768]{1,0:T(8,128)(2,1)S(1)}, bf16[64,768]{1,0:T(8,128)(2,1)S(1)}, u32[]{:S(2)}, u32[]{:S(2)}) collective-permute-start(bf16[64,768]{1,0:T(8,128)(2,1)S(1)} %get-tuple-element.63), channel_id=1, source_target_pairs={{0,8},{4,12},{8,0},{12,4},{16,24},{20,28},{24,16},{28,20},{1,9},{5... | collective-permute-start | bytes 294920 | tf_op jit(solution)/shard_map/ppermute | solution.py:68
  16.8 10.4 %collective-permute-start.4 = (bf16[4,64,768]{2,1,0:T(8,128)(2,1)S(1)}, bf16[4,64,768]{2,1,0:T(8,128)(2,1)}, u32[]{:S(2)}, u32[]{:S(2)}) collective-permute-start(bf16[4,64,768]{2,1,0:T(8,128)(2,1)S(1)} %pad_maximum_fusion.8), channel_id=1, source_target_pairs={{0,2},{1,3},{2,0},{3,1},{4,6},{5,7},{6,4},{7,5},{8,10},{9,11},{10,... | collective-permute-start | bytes 1179656 | tf_op jit(solution)/shard_map/ppermute | solution.py:63
  18.5 20.6 %collective-permute-start.6 = (bf16[1024,384]{1,0:T(8,128)(2,1)S(1)}, bf16[1024,384]{1,0:T(8,128)(2,1)}, u32[]{:S(2)}, u32[]{:S(2)}) collective-permute-start(bf16[1024,384]{1,0:T(8,128)(2,1)S(1)} %fusion), channel_id=1, source_target_pairs={{0,4},{4,0},{8,12},{12,8},{16,20},{20,16},{24,28},{28,24},{1,5},{5... | collective-permute-start | bytes 2359304 | tf_op jit(solution)/shard_map/ppermute | solution.py:59
  19.3 12.5 %collective-permute-start.8 = (bf16[2,256,512]{1,2,0:T(8,128)(2,1)S(1)}, bf16[2,256,512]{1,2,0:T(8,128)(2,1)S(1)}, u32[]{:S(2)}, u32[]{:S(2)}) collective-permute-start(bf16[2,256,512]{1,2,0:T(8,128)(2,1)S(1)} %pad_maximum_fusion.5), channel_id=1, source_target_pairs={{0,8},{4,12},{8,0},{12,4},{16,24},{20,28},{24,16},{28,20},{1,9},{5... | collective-permute-start | bytes 1572872 | tf_op jit(solution)/shard_map/ppermute | solution.py:68
  29.2 11.3 %collective-permute-start.5 = (bf16[4,2,64,768]{3,2,1,0:T(8,128)(2,1)}, bf16[4,2,64,768]{3,2,1,0:T(8,128)(2,1)}, u32[]{:S(2)}, u32[]{:S(2)}) collective-permute-start(bf16[4,2,64,768]{3,2,1,0:T(8,128)(2,1)} %pad_maximum_fusion.3), channel_id=1, source_target_pairs={{0,1},{1,0},{2,3},{3,2},{4,5},{5,4},{6,7},{7,6},{8,9},{9,8},{10,11... | collective-permute-start | bytes 2359304 | tf_op jit(solution)/shard_map/ppermute | solution.py:63
  29.2 14.7 %collective-permute-start.7 = (bf16[2,256,512]{1,2,0:T(8,128)(2,1)S(1)}, bf16[2,256,512]{1,2,0:T(8,128)(2,1)S(1)}, u32[]{:S(2)}, u32[]{:S(2)}) collective-permute-start(bf16[2,256,512]{1,2,0:T(8,128)(2,1)S(1)} %pad_maximum_fusion.5), channel_id=1, source_target_pairs={{0,1},{1,0},{2,3},{3,2},{4,5},{5,4},{6,7},{7,6},{8,16},{9,17},{10,... | collective-permute-start | bytes 1572872 | tf_op jit(solution)/shard_map/ppermute | solution.py:84
  29.7 24.1 %collective-permute-start.21 = (bf16[4,2,64,768]{3,2,1,0:T(8,128)(2,1)}, bf16[4,2,64,768]{3,2,1,0:T(8,128)(2,1)S(1)}, u32[]{:S(2)}, u32[]{:S(2)}) collective-permute-start(bf16[4,2,64,768]{3,2,1,0:T(8,128)(2,1)} %pad_maximum_fusion.3), channel_id=1, source_target_pairs={{0,4},{4,0},{8,12},{12,8},{16,20},{20,16},{24,28},{28,24},{1,5},{5... | collective-permute-start | bytes 2359304 | tf_op jit(solution)/shard_map/ppermute | solution.py:59
  44.0 10.2 %collective-permute-start.15 = (bf16[256,512]{0,1:T(8,128)(2,1)S(1)}, bf16[256,512]{0,1:T(8,128)(2,1)S(1)}, u32[]{:S(2)}, u32[]{:S(2)}) collective-permute-start(bf16[256,512]{0,1:T(8,128)(2,1)S(1)} %get-tuple-element.24), channel_id=1, source_target_pairs={{0,1},{1,0},{2,3},{3,2},{4,5},{5,4},{6,7},{7,6},{8,16},{9,17},{10,... | collective-permute-start | bytes 786440 | tf_op jit(solution)/shard_map/ppermute | solution.py:84
  44.1 10.2 %collective-permute-start.16 = (bf16[256,512]{0,1:T(8,128)(2,1)S(1)}, bf16[256,512]{0,1:T(8,128)(2,1)S(1)}, u32[]{:S(2)}, u32[]{:S(2)}) collective-permute-start(bf16[256,512]{0,1:T(8,128)(2,1)S(1)} %get-tuple-element.25), channel_id=1, source_target_pairs={{0,8},{4,12},{8,0},{12,4},{16,24},{20,28},{24,16},{28,20},{1,9},{5... | collective-permute-start | bytes 786440 | tf_op jit(solution)/shard_map/ppermute | solution.py:68
  44.8 10.2 %collective-permute-start.9 = (bf16[256,512]{0,1:T(8,128)(2,1)S(1)}, bf16[256,512]{0,1:T(8,128)(2,1)S(1)}, u32[]{:S(2)}, u32[]{:S(2)}) collective-permute-start(bf16[256,512]{0,1:T(8,128)(2,1)S(1)} %get-tuple-element.18), channel_id=1, source_target_pairs={{0,1},{1,0},{2,3},{3,2},{4,5},{5,4},{6,7},{7,6},{8,16},{9,17},{10,... | collective-permute-start | bytes 786440 | tf_op jit(solution)/shard_map/ppermute | solution.py:84
  44.8 14.0 %collective-permute-start.10 = (bf16[256,512]{0,1:T(8,128)(2,1)S(1)}, bf16[256,512]{0,1:T(8,128)(2,1)S(1)}, u32[]{:S(2)}, u32[]{:S(2)}) collective-permute-start(bf16[256,512]{0,1:T(8,128)(2,1)S(1)} %get-tuple-element.19), channel_id=1, source_target_pairs={{0,8},{4,12},{8,0},{12,4},{16,24},{20,28},{24,16},{28,20},{1,9},{5... | collective-permute-start | bytes 786440 | tf_op jit(solution)/shard_map/ppermute | solution.py:68
  53.8 19.5 %collective-permute-start.22 = (bf16[4,2,64,768]{3,2,1,0:T(8,128)(2,1)S(1)}, bf16[4,2,64,768]{3,2,1,0:T(8,128)(2,1)S(1)}, u32[]{:S(2)}, u32[]{:S(2)}) collective-permute-start(bf16[4,2,64,768]{3,2,1,0:T(8,128)(2,1)S(1)} %collective-permute-done.21), channel_id=1, source_target_pairs={{0,1},{1,0},{2,3},{3,2},{4,5},{5,4},{6,7},{7,6},{8,9},{9,8},{10,11... | collective-permute-start | bytes 2359304 | tf_op jit(solution)/shard_map/ppermute | solution.py:63
  54.4 10.1 %collective-permute-start.18 = (bf16[256,512]{0,1:T(8,128)(2,1)S(1)}, bf16[256,512]{0,1:T(8,128)(2,1)S(1)}, u32[]{:S(2)}, u32[]{:S(2)}) collective-permute-start(bf16[256,512]{0,1:T(8,128)(2,1)S(1)} %fusion.22), channel_id=1, source_target_pairs={{0,8},{4,12},{8,0},{12,4},{16,24},{20,28},{24,16},{28,20},{1,9},{5... | collective-permute-start | bytes 786440 | tf_op jit(solution)/shard_map/ppermute | solution.py:68
  54.5 10.0 %collective-permute-start.17 = (bf16[256,512]{0,1:T(8,128)(2,1)S(1)}, bf16[256,512]{0,1:T(8,128)(2,1)S(1)}, u32[]{:S(2)}, u32[]{:S(2)}) collective-permute-start(bf16[256,512]{0,1:T(8,128)(2,1)S(1)} %add_convert_fusion.1), channel_id=1, source_target_pairs={{0,1},{1,0},{2,3},{3,2},{4,5},{5,4},{6,7},{7,6},{8,16},{9,17},{10,... | collective-permute-start | bytes 786440 | tf_op jit(solution)/shard_map/ppermute | solution.py:84
  59.0 11.1 %collective-permute-start.12 = (bf16[256,512]{0,1:T(8,128)(2,1)S(1)}, bf16[256,512]{0,1:T(8,128)(2,1)S(1)}, u32[]{:S(2)}, u32[]{:S(2)}) collective-permute-start(bf16[256,512]{0,1:T(8,128)(2,1)S(1)} %fusion.20), channel_id=1, source_target_pairs={{0,8},{4,12},{8,0},{12,4},{16,24},{20,28},{24,16},{28,20},{1,9},{5... | collective-permute-start | bytes 786440 | tf_op jit(solution)/shard_map/ppermute | solution.py:68
  59.7 10.5 %collective-permute-start.11 = (bf16[256,512]{0,1:T(8,128)(2,1)S(1)}, bf16[256,512]{0,1:T(8,128)(2,1)S(1)}, u32[]{:S(2)}, u32[]{:S(2)}) collective-permute-start(bf16[256,512]{0,1:T(8,128)(2,1)S(1)} %add_convert_fusion.3), channel_id=1, source_target_pairs={{0,1},{1,0},{2,3},{3,2},{4,5},{5,4},{6,7},{7,6},{8,16},{9,17},{10,... | collective-permute-start | bytes 786440 | tf_op jit(solution)/shard_map/ppermute | solution.py:84
  64.7 11.6 %collective-permute-start.20 = (bf16[256,512]{0,1:T(8,128)(2,1)S(1)}, bf16[256,512]{0,1:T(8,128)(2,1)S(1)}, u32[]{:S(2)}, u32[]{:S(2)}) collective-permute-start(bf16[256,512]{0,1:T(8,128)(2,1)S(1)} %get-tuple-element.29), channel_id=1, source_target_pairs={{0,1},{1,0},{2,3},{3,2},{4,5},{5,4},{6,7},{7,6},{8,16},{9,17},{10,... | collective-permute-start | bytes 786440 | tf_op jit(solution)/shard_map/ppermute | solution.py:84
  64.8 11.5 %collective-permute-start.19 = (bf16[256,512]{0,1:T(8,128)(2,1)S(1)}, bf16[256,512]{0,1:T(8,128)(2,1)S(1)}, u32[]{:S(2)}, u32[]{:S(2)}) collective-permute-start(bf16[256,512]{0,1:T(8,128)(2,1)S(1)} %get-tuple-element.28), channel_id=1, source_target_pairs={{0,8},{4,12},{8,0},{12,4},{16,24},{20,28},{24,16},{28,20},{1,9},{5... | collective-permute-start | bytes 786440 | tf_op jit(solution)/shard_map/ppermute | solution.py:68
  70.3 6.1 %collective-permute-start.14 = (bf16[256,512]{0,1:T(8,128)(2,1)S(1)}, bf16[256,512]{0,1:T(8,128)(2,1)S(1)}, u32[]{:S(2)}, u32[]{:S(2)}) collective-permute-start(bf16[256,512]{0,1:T(8,128)(2,1)S(1)} %get-tuple-element.23), channel_id=1, source_target_pairs={{0,1},{1,0},{2,3},{3,2},{4,5},{5,4},{6,7},{7,6},{8,16},{9,17},{10,... | collective-permute-start | bytes 786440 | tf_op jit(solution)/shard_map/ppermute | solution.py:84
  70.4 10.5 %collective-permute-start.13 = (bf16[256,512]{0,1:T(8,128)(2,1)S(1)}, bf16[256,512]{0,1:T(8,128)(2,1)S(1)}, u32[]{:S(2)}, u32[]{:S(2)}) collective-permute-start(bf16[256,512]{0,1:T(8,128)(2,1)S(1)} %get-tuple-element.22), channel_id=1, source_target_pairs={{0,8},{4,12},{8,0},{12,4},{16,24},{20,28},{24,16},{28,20},{1,9},{5... | collective-permute-start | bytes 786440 | tf_op jit(solution)/shard_map/ppermute | solution.py:68
  75.6 9.0 %collective-permute-start.23 = (bf16[384,512]{0,1:T(8,128)(2,1)S(1)}, bf16[384,512]{0,1:T(8,128)(2,1)S(1)}, u32[]{:S(2)}, u32[]{:S(2)}) collective-permute-start(bf16[384,512]{0,1:T(8,128)(2,1)S(1)} %constant_dynamic-slice_fusion), channel_id=1, source_target_pairs={{0,4},{4,0},{8,12},{12,8},{16,20},{20,16},{24,28},{28,24},{1,5},{5... | collective-permute-start | bytes 1179656 | tf_op jit(solution)/shard_map/ppermute | solution.py:59

commit v5 on v4

--- a/solution.py
+++ b/solution.py
@@ -3,6 +3,8 @@
 import jax
 import jax.numpy as jnp
 from jax import lax
+from jax.experimental import pallas as pl
+from jax.experimental.pallas import tpu as pltpu
 from jax.sharding import PartitionSpec as P
 
 BLOCK = 32
@@ -13,6 +15,38 @@
 def dequantize(codes_part, scales_part):
     expanded = jnp.repeat(scales_part.astype(jnp.float32), BLOCK, axis=0)
     return (codes_part.astype(jnp.float32) * expanded).astype(jnp.bfloat16)
+
+
+def pack(side, codes, scales, attn_out):
+    heads, features = codes.shape
+    group_rows = attn_out.shape[0]
+    count = heads // group_rows
+    width = heads // PAIR // count
+
+    def kernel(side_ref, codes_ref, scales_ref, attn_ref, out_ref):
+        scale = scales_ref[...].astype(jnp.float32)
+        for k in range(heads // BLOCK):
+            rows = slice(k * BLOCK, (k + 1) * BLOCK)
+            values = codes_ref[rows].astype(jnp.float32) * scale[k : k + 1]
+            out_ref[rows, :features] = values.astype(out_ref.dtype)
+        for other in range(PAIR):
+
+            @pl.when(side_ref[0] == 1 - other)
+            def _():
+                for k in range(count):
+                    first = other * (heads // PAIR) + k * width
+                    rows = slice(k * group_rows, (k + 1) * group_rows)
+                    out_ref[rows, features:] = attn_ref[:, first : first + width]
+
+    in_vmem = pl.BlockSpec(memory_space=pltpu.VMEM)
+    size = heads * (features + width)
+    return pl.pallas_call(
+        kernel,
+        out_shape=jax.ShapeDtypeStruct((heads, features + width), codes.dtype),
+        in_specs=[pl.BlockSpec(memory_space=pltpu.SMEM), in_vmem, in_vmem, in_vmem],
+        out_specs=in_vmem,
+        cost_estimate=pl.CostEstimate(flops=size, bytes_accessed=4 * size, transcendentals=0),
+    )(side[None].astype(jnp.int32), codes, scales, attn_out)
 
 
 def halves(own, other, side, axis):
@@ -92,46 +126,74 @@
     held = jnp.stack(slots)
 
     attn_own = lax.dynamic_slice_in_dim(attn_out, side * half, half, 1)
-    attn_other = swap_x(lax.dynamic_slice_in_dim(attn_out, (1 - side) * half, half, 1))
-    weight = dequantize(weight_codes, block_scales)
-    weight_other = swap_x(weight)
-    weight_slab = halves(weight, weight_other, side, 1)
-
-    held, attn_other = together(held, attn_other)
-    attn = jnp.stack([attn_own, attn_other])
-    if layers == LINE:
-        attn_1, attn_in = outer(attn), inner(attn)
+    packed = heads % group_rows == 0
+    if packed:
+        sent = pack(side, weight_codes, block_scales, attn_out)
+        weight = sent[:, :own_features]
+        got = [swap_x(sent)]
+    else:
+        weight = dequantize(weight_codes, block_scales)
+        attn_send = lax.dynamic_slice_in_dim(attn_out, (1 - side) * half, half, 1)
+        got = [swap_x(weight), swap_x(attn_send)]
+
+    if layers == LINE:
+        attn_1, attn_in = [outer(attn_own)], [inner(attn_own)]
 
     for k in range(bits - 1):
         held = with_mp(held, k)
+    if layers == LINE:
+        held, attn_1[0], attn_in[0] = together(held, attn_1[0], attn_in[0])
+    held, got = together(held, got)
+    if packed:
+        weight_other, blocks = got[0][:, :own_features], got[0][:, own_features:]
+        attn_other = jnp.concatenate(jnp.split(blocks, heads // group_rows), 1)
+    else:
+        weight_other, attn_other = got
+    attn = [attn_own, attn_other]
+    if layers == LINE:
+        attn_1.append(outer(attn_other))
+        attn_in.append(inner(attn_other))
     cols = with_mp(held, bits - 1).reshape(layers, group_rows, layer_features)
-    held_other = swap_x(held)
-    cols_other = with_mp(held_other, bits - 1).reshape(cols.shape)
+    held_other, _ = together(held, weight_other)
+    held_other = swap_x(held_other)
+
+    weight_slab = halves(weight, weight_other, side, 1)
 
     def terms(k):
         stream = weight_slab[k * half : (k + 1) * half]
         part = by_feature(cols.reshape(-1, layer_features), stream)
         return part.reshape(layers, group_rows, half)
 
+    if layers != LINE:
+        cols_other = with_mp(held_other, bits - 1).reshape(cols.shape)
     streams = range(PAIR)
     part = [terms(k) for k in streams]
     if layers == LINE:
         outer_2, inner_2, outer_3, inner_3, gas = [], [], [], [], []
+        before = []
         for k in streams:
             send = jnp.where(middle, attn_in[k], part[k][3].astype(jnp.bfloat16))
-            send_outer, send_inner = together(send, attn_1[k])
+            send_outer, send_inner, *before = together(send, attn_1[k], *before)
+            before = [send_outer, send_inner]
             outer_2.append(outer(send_outer))
             inner_2.append(inner(send_inner))
+        held_other, _ = together(held_other, outer_2[0])
+        cols_other = with_mp(held_other, bits - 1).reshape(cols.shape)
+        before = []
         for k in streams:
             send_outer = jnp.where(middle, inner_2[k], part[k][2].astype(jnp.bfloat16))
             send_inner = (part[k][2] + outer_2[k].astype(jnp.float32)).astype(jnp.bfloat16)
-            send_outer, send_inner = together(send_outer, send_inner)
+            send_outer, send_inner, *before = together(send_outer, send_inner, *before)
+            before = [send_outer, send_inner]
             outer_3.append(outer(send_outer))
             inner_3.append(inner(send_inner))
+        before = []
         for k in streams:
             send_inner = (part[k][3] + outer_3[k].astype(jnp.float32)).astype(jnp.bfloat16)
             send_outer = part[k][1] + jnp.where(middle, inner_3[k].astype(jnp.float32), 0.0)
-            send_outer, send_inner = together(send_outer.astype(jnp.bfloat16), send_inner)
+            send_outer = send_outer.astype(jnp.bfloat16)
+            send_outer, send_inner, *before = together(send_outer, send_inner, *before)
+            before = [send_outer, send_inner]
             outer_4, inner_4 = outer(send_outer), inner(send_inner)
             ga = part[k][0] + outer_4.astype(jnp.float32)
             gas.append(ga + jnp.where(middle, inner_4.astype(jnp.float32), 0.0))

time: 86.4 us -> 80.9 us (0.936)
  waiting for transfers between devices: 47.1 us -> 36.4 us
  starting transfers between devices: 22.1 us -> 28.4 us
  Pallas kernels: 0 us -> 2.54 us
  other arithmetic: 6.66 us -> 4.23 us
  local copies, waits for them, and re-layouts: 3.83 us -> 1.44 us
  matrix products: 5.39 us -> 6.62 us
    ppermute x4 -> x3, waiting for transfers between devices: 15.4 us -> 3.99 us  [swap_x(): return lax.ppermute(piece, 'dp', [(i, i ^ 1) for i in range(n_dp)])]
    ppermute x10 -> x11, starting transfers between devices: 14.6 us -> 20.4 us  [move_layers(): return lax.ppermute(piece, 'dp', moves)]
    pallas_call x0 -> x1, Pallas kernels: none -> 2.54 us  [pack(): pl.pallas_call(kernel, out_shape=jax.ShapeDtypeStruct((heads, features +...]
    select_n x4, other arithmetic: 3.76 us -> 1.66 us  [halves(): first = jnp.where(side == 0, own, other)]
    dynamic_slice x2 -> x1, local copies, waits for them, and re-layouts: 1.29 us -> 0.02 us  [body(): attn_own = lax.dynamic_slice_in_dim(attn_out, side * half, half, 1)]
    dot_general x8, matrix products: 3.37 us -> 4.61 us  [by_token(): lax.dot_general(columns, rows, (((0,), (0,)), ((), ())), preferred_elemen...]
    unnamed x9 -> x7, local copies, waits for them, and re-layouts: 2.32 us -> 1.18 us
    concatenate x5, other arithmetic: 1.47 us -> 0.59 us  [halves(): return jnp.concatenate([first, second], axis)]
  transfers between devices with their start and end apart: 24 -> 25, of which waited for: 11 -> 10; matrix products, arithmetic and copies ran while one was open for 15% -> 13% of each run, Pallas kernels for 0% -> 0%
where the time goes in v5:
time: 80.9 us; the launch traced here: 80.7 us
  waiting for transfers between devices  36.4 us (45%)
  starting transfers between devices  28.4 us (35%)
  matrix products  6.62 us (8%)
  other arithmetic  4.23 us (5%)
  Pallas kernels  2.54 us (3%)
  local copies, waits for them, and re-layouts  1.44 us (2%)
  between operations  1.01 us (1%)
    ppermute x11, waiting for transfers between devices, move_layers(): return lax.ppermute(piece, 'dp', moves)  24.4 us
    ppermute x11, starting transfers between devices, move_layers(): return lax.ppermute(piece, 'dp', moves)  20.4 us
    ppermute x3, waiting for transfers between devices, with_mp(): other = lax.ppermute(piece, 'mp', [(i, i ^ bit) for i in range(n_mp)])  8.09 us
    ppermute x3, starting transfers between devices, swap_x(): return lax.ppermute(piece, 'dp', [(i, i ^ 1) for i in range(n_dp)])  5.02 us
    dot_general x8, matrix products, by_token(): lax.dot_general(columns, rows, (((0,), (0,)), ((), ())), preferred_elemen...  4.61 us
    ppermute x3, waiting for transfers between devices, swap_x(): return lax.ppermute(piece, 'dp', [(i, i ^ 1) for i in range(n_dp)])  3.99 us
    pallas_call x1, Pallas kernels, pack(): pl.pallas_call(kernel, out_shape=jax.ShapeDtypeStruct((heads, features +...  2.54 us
    ppermute x3, starting transfers between devices, with_mp(): other = lax.ppermute(piece, 'mp', [(i, i ^ bit) for i in range(n_mp)])  2.1 us
  transfers between devices with their start and end apart: 25, of which 10 were waited for; matrix products, arithmetic and copies ran while one was open for 13% of the time, Pallas kernels for 0%

profile of v5, /device:TPU:0, one launch (start us, length us, event | category | flops | bytes accessed | tf_op | source)
XLA Modules:
  0.0 80.7 jit_solution(4024688547451557373)
XLA Ops:
  0.7 2.5 %shard_map.59 = bf16[1024,512]{1,0:T(8,128)(2,1)} custom-call(s32[1]{0:T(128)} %bitcast.7.side_ref, bf16[1024,384]{1,0:T(8,128)(2,1)} %codes_ref.1, bf16[32,384]{1,0:T(8,128)(2,1)} %scales_ref.1, bf16[256,1024]{1,0:T(8,128)(2,1)} %attn_ref.1), custom_call_target="tpu_custom_call" | custom-call | flops 524288 | bytes 2097152 | tf_op jit(solution)/shard_map/pallas_call | solution.py:43
  3.2 2.9 %collective-permute-start.6 = (bf16[1024,512]{1,0:T(8,128)(2,1)}, bf16[1024,512]{1,0:T(8,128)(2,1)S(1)}, u32[]{:S(2)}, u32[]{:S(2)}) collective-permute-start(bf16[1024,512]{1,0:T(8,128)(2,1)} %shard_map.59), channel_id=1, source_target_pairs={{0,4},{4,0},{8,12},{12,8},{16,20},{20,16},{24,28},{28,24},{1,5},{5... | collective-permute-start | bytes 3145736 | tf_op jit(solution)/shard_map/ppermute | solution.py:93
  6.2 3.7 %collective-permute-start.2 = (bf16[64,768]{1,0:T(8,128)(2,1)S(1)}, bf16[64,768]{1,0:T(8,128)(2,1)S(1)}, u32[]{:S(2)}, u32[]{:S(2)}) collective-permute-start(bf16[64,768]{1,0:T(8,128)(2,1)S(1)} %get-tuple-element.72), channel_id=1, source_target_pairs={{0,24},{4,28},{8,16},{12,20},{16,8},{20,12},{24,0},{28,4},{1,25},{... | collective-permute-start | bytes 294920 | tf_op jit(solution)/shard_map/ppermute | solution.py:102
  9.9 0.8 collective-permute-start
  10.6 3.1 %collective-permute-done.2 = bf16[64,768]{1,0:T(8,128)(2,1)S(1)} collective-permute-done((bf16[64,768]{1,0:T(8,128)(2,1)S(1)}, bf16[64,768]{1,0:T(8,128)(2,1)S(1)}, u32[]{:S(2)}, u32[]{:S(2)}) %collective-permute-start.2) | collective-permute-done | bytes 98336 | tf_op jit(solution)/shard_map/ppermute | solution.py:102
  13.8 4.1 %collective-permute-done.1 = bf16[64,768]{1,0:T(8,128)(2,1)S(1)} collective-permute-done((bf16[64,768]{1,0:T(8,128)(2,1)S(1)}, bf16[64,768]{1,0:T(8,128)(2,1)S(1)}, u32[]{:S(2)}, u32[]{:S(2)}) %collective-permute-start.1) | collective-permute-done | bytes 98336 | tf_op jit(solution)/shard_map/ppermute | solution.py:102
  17.9 1.6 %collective-permute-start.3 = (bf16[4,64,768]{2,1,0:T(8,128)(2,1)S(1)}, bf16[4,64,768]{2,1,0:T(8,128)(2,1)S(1)}, u32[]{:S(2)}, u32[]{:S(2)}) collective-permute-start(bf16[4,64,768]{2,1,0:T(8,128)(2,1)S(1)} %pad_maximum_fusion.7), channel_id=1, source_target_pairs={{0,2},{1,3},{2,0},{3,1},{4,6},{5,7},{6,4},{7,5},{8,10},{9,11},{10,... | collective-permute-start | bytes 1179656 | tf_op jit(solution)/shard_map/ppermute | solution.py:97
  19.5 0.6 collective-permute-start.4
  20.1 8.1 %collective-permute-done.3 = bf16[4,64,768]{2,1,0:T(8,128)(2,1)S(1)} collective-permute-done((bf16[4,64,768]{2,1,0:T(8,128)(2,1)S(1)}, bf16[4,64,768]{2,1,0:T(8,128)(2,1)S(1)}, u32[]{:S(2)}, u32[]{:S(2)}) %collective-permute-start.3) | collective-permute-done | bytes 393248 | tf_op jit(solution)/shard_map/ppermute | solution.py:97
  28.4 1.1 %collective-permute-done.6 = bf16[1024,512]{1,0:T(8,128)(2,1)S(1)} collective-permute-done((bf16[1024,512]{1,0:T(8,128)(2,1)}, bf16[1024,512]{1,0:T(8,128)(2,1)S(1)}, u32[]{:S(2)}, u32[]{:S(2)}) %collective-permute-start.6) | collective-permute-done | bytes 1048608 | tf_op jit(solution)/shard_map/ppermute | solution.py:93
  29.6 0.6 collective-permute-start.14
  30.2 2.9 %collective-permute-start.15 = (bf16[256,512]{1,0:T(8,128)(2,1)S(1)}, bf16[256,512]{1,0:T(8,128)(2,1)S(1)}, u32[]{:S(2)}, u32[]{:S(2)}) collective-permute-start(bf16[256,512]{1,0:T(8,128)(2,1)S(1)} %pad_maximum_fusion.8), channel_id=1, source_target_pairs={{0,8},{4,12},{8,0},{12,4},{16,24},{20,28},{24,16},{28,20},{1,9},{5... | collective-permute-start | bytes 786440 | tf_op jit(solution)/shard_map/ppermute | solution.py:102
  33.1 1.5 %collective-permute-start.22 = (bf16[4,2,64,768]{3,2,1,0:T(8,128)(2,1)S(1)}, bf16[4,2,64,768]{3,2,1,0:T(8,128)(2,1)S(1)}, u32[]{:S(2)}, u32[]{:S(2)}) collective-permute-start(bf16[4,2,64,768]{3,2,1,0:T(8,128)(2,1)S(1)} %pad_maximum_fusion.3), channel_id=1, source_target_pairs={{0,4},{4,0},{8,12},{12,8},{16,20},{20,16},{24,28},{28,24},{1,5},{5... | collective-permute-start | bytes 2359304 | tf_op jit(solution)/shard_map/ppermute | solution.py:93
  34.6 0.1 broadcast_select_fusion.1
  34.7 1.2 %select_bitcast_fusion.3 = (bf16[4,2,1,64,768]{4,3,2,1,0:T(8,128)(2,1)S(1)}, bf16[4,2,1,64,768]{4,3,2,1,0:T(8,128)(2,1)S(1)}) fusion(bf16[4,2,64,768]{3,2,1,0:T(8,128)(2,1)S(1)} %pad_maximum_fusion.3, bf16[4,2,64,768]{3,2,1,0:T(8,128)(2,1)} %collective-permute-done.7, pred[]{:T(512)S(6)} %eq.11), kind=kLoop, calls=%fused_computation.28 | loop fusion | flops 786432 | bytes 3145729 | tf_op jit(solution)/shard_map/jit(_where)/select_n | solution.py:53
  36.0 0.1 pad_maximum_fusion
  36.1 1.0 %fusion.3 = f32[1024,512]{1,0:T(8,128)S(1)} fusion(bf16[1024,768]{1,0:T(8,128)(2,1)S(1)} %bitcast.45, bf16[1024,384]{1,0:T(8,128)(2,1)S(1)} %get-tuple-element.49, bf16[1024,384]{1,0:T(8,128)(2,1)S(1)} %get-tuple-element.48), kind=kOutput, calls=%fused_computation.21 | convolution fusion | flops 806879232 | bytes 5242880 | tf_op jit(solution)/shard_map/dot_general | solution.py:67
  37.1 1.0 %fusion.1 = f32[1024,512]{1,0:T(8,128)S(1)} fusion(bf16[1024,768]{1,0:T(8,128)(2,1)S(1)} %bitcast.46, bf16[1024,384]{1,0:T(8,128)(2,1)S(1)} %get-tuple-element.48, bf16[1024,384]{1,0:T(8,128)(2,1)S(1)} %get-tuple-element.49), kind=kOutput, calls=%fused_computation.19 | convolution fusion | flops 806879232 | bytes 5242880 | tf_op jit(solution)/shard_map/dot_general | solution.py:67
  38.2 0.1 fusion.15
  38.4 2.1 %collective-permute-start.9 = (bf16[256,512]{1,0:T(8,128)(2,1)S(1)}, bf16[256,512]{1,0:T(8,128)(2,1)S(1)}, u32[]{:S(2)}, u32[]{:S(2)}) collective-permute-start(bf16[256,512]{1,0:T(8,128)(2,1)S(1)} %fusion.18), channel_id=1, source_target_pairs={{0,8},{4,12},{8,0},{12,4},{16,24},{20,28},{24,16},{28,20},{1,9},{5... | collective-permute-start | bytes 786440 | tf_op jit(solution)/shard_map/ppermute | solution.py:102
  40.6 1.3 %collective-permute-start.17 = (bf16[256,512]{1,0:T(8,128)(2,1)S(1)}, bf16[256,512]{1,0:T(8,128)(2,1)S(1)}, u32[]{:S(2)}, u32[]{:S(2)}) collective-permute-start(bf16[256,512]{1,0:T(8,128)(2,1)S(1)} %fusion.20), channel_id=1, source_target_pairs={{0,8},{4,12},{8,0},{12,4},{16,24},{20,28},{24,16},{28,20},{1,9},{5... | collective-permute-start | bytes 786440 | tf_op jit(solution)/shard_map/ppermute | solution.py:102
  42.0 0.4 fusion.40
  42.4 1.4 %fusion.41 = f32[768,512]{0,1:T(8,128)S(1)} fusion(bf16[256,768]{1,0:T(8,128)(2,1)S(1)} %bitcast.49, bf16[256,512]{1,0:T(8,128)(2,1)} %collective-permute-done.4), kind=kOutput, calls=%fused_computation.91 | convolution fusion | flops 201326592 | bytes 2228224 | tf_op jit(solution)/shard_map/dot_general | solution.py:73
  43.8 3.8 %collective-permute-done.9 = bf16[256,512]{1,0:T(8,128)(2,1)S(1)} collective-permute-done((bf16[256,512]{1,0:T(8,128)(2,1)S(1)}, bf16[256,512]{1,0:T(8,128)(2,1)S(1)}, u32[]{:S(2)}, u32[]{:S(2)}) %collective-permute-start.9) | collective-permute-done | bytes 262176 | tf_op jit(solution)/shard_map/ppermute | solution.py:102
  47.7 2.2 %collective-permute-start.11 = (bf16[256,512]{1,0:T(8,128)(2,1)S(1)}, bf16[256,512]{1,0:T(8,128)(2,1)S(1)}, u32[]{:S(2)}, u32[]{:S(2)}) collective-permute-start(bf16[256,512]{1,0:T(8,128)(2,1)S(1)} %fusion.19), channel_id=1, source_target_pairs={{0,8},{4,12},{8,0},{12,4},{16,24},{20,28},{24,16},{28,20},{1,9},{5... | collective-permute-start | bytes 786440 | tf_op jit(solution)/shard_map/ppermute | solution.py:102
  50.0 3.3 %collective-permute-done.17 = bf16[256,512]{1,0:T(8,128)(2,1)S(1)} collective-permute-done((bf16[256,512]{1,0:T(8,128)(2,1)S(1)}, bf16[256,512]{1,0:T(8,128)(2,1)S(1)}, u32[]{:S(2)}, u32[]{:S(2)}) %collective-permute-start.17) | collective-permute-done | bytes 262176 | tf_op jit(solution)/shard_map/ppermute | solution.py:102
  53.3 2.2 %collective-permute-start.19 = (bf16[256,512]{1,0:T(8,128)(2,1)S(1)}, bf16[256,512]{1,0:T(8,128)(2,1)S(1)}, u32[]{:S(2)}, u32[]{:S(2)}) collective-permute-start(bf16[256,512]{1,0:T(8,128)(2,1)S(1)} %fusion.21), channel_id=1, source_target_pairs={{0,8},{4,12},{8,0},{12,4},{16,24},{20,28},{24,16},{28,20},{1,9},{5... | collective-permute-start | bytes 786440 | tf_op jit(solution)/shard_map/ppermute | solution.py:102
  55.5 0.5 collective-permute-start.23
  56.0 0.4 fusion.30
  56.5 2.4 %collective-permute-done.11 = bf16[256,512]{1,0:T(8,128)(2,1)S(1)} collective-permute-done((bf16[256,512]{1,0:T(8,128)(2,1)S(1)}, bf16[256,512]{1,0:T(8,128)(2,1)S(1)}, u32[]{:S(2)}, u32[]{:S(2)}) %collective-permute-start.11) | collective-permute-done | bytes 262176 | tf_op jit(solution)/shard_map/ppermute | solution.py:102
  58.8 0.2 add_convert_fusion.2
  59.1 2.3 %collective-permute-start.12 = (bf16[256,512]{1,0:T(8,128)(2,1)S(1)}, bf16[256,512]{1,0:T(8,128)(2,1)S(1)}, u32[]{:S(2)}, u32[]{:S(2)}) collective-permute-start(bf16[256,512]{1,0:T(8,128)(2,1)S(1)} %get-tuple-element.30), channel_id=1, source_target_pairs={{0,8},{4,12},{8,0},{12,4},{16,24},{20,28},{24,16},{28,20},{1,9},{5... | collective-permute-start | bytes 786440 | tf_op jit(solution)/shard_map/ppermute | solution.py:102
  61.4 3.0 %collective-permute-done.19 = bf16[256,512]{1,0:T(8,128)(2,1)S(1)} collective-permute-done((bf16[256,512]{1,0:T(8,128)(2,1)S(1)}, bf16[256,512]{1,0:T(8,128)(2,1)S(1)}, u32[]{:S(2)}, u32[]{:S(2)}) %collective-permute-start.19) | collective-permute-done | bytes 262176 | tf_op jit(solution)/shard_map/ppermute | solution.py:102
  64.5 0.2 add_convert_fusion
  64.7 2.3 %collective-permute-start.20 = (bf16[256,512]{1,0:T(8,128)(2,1)S(1)}, bf16[256,512]{1,0:T(8,128)(2,1)S(1)}, u32[]{:S(2)}, u32[]{:S(2)}) collective-permute-start(bf16[256,512]{1,0:T(8,128)(2,1)S(1)} %get-tuple-element.36), channel_id=1, source_target_pairs={{0,8},{4,12},{8,0},{12,4},{16,24},{20,28},{24,16},{28,20},{1,9},{5... | collective-permute-start | bytes 786440 | tf_op jit(solution)/shard_map/ppermute | solution.py:102
  67.0 0.4 fusion.26
  67.6 0.1 pad_maximum_fusion.6
  67.8 0.4 fusion.38
  68.3 0.4 fusion.28
  68.7 0.4 fusion.42
  69.1 0.8 multiply_convert_fusion
  70.0 0.6 collective-permute-start.24
  70.6 4.7 %collective-permute-done.20 = bf16[256,512]{1,0:T(8,128)(2,1)S(1)} collective-permute-done((bf16[256,512]{1,0:T(8,128)(2,1)S(1)}, bf16[256,512]{1,0:T(8,128)(2,1)S(1)}, u32[]{:S(2)}, u32[]{:S(2)}) %collective-permute-start.20) | collective-permute-done | bytes 262176 | tf_op jit(solution)/shard_map/ppermute | solution.py:102
  75.4 0.1 fusion.10
  75.5 0.9 %pad_maximum_fusion.5 = bf16[256,1024]{1,0:T(8,128)(2,1)} fusion(bf16[256,512]{1,0:T(8,128)(2,1)S(1)} %fusion.7, bf16[256,512]{1,0:T(8,128)(2,1)S(1)} %fusion.10), kind=kLoop, calls=%fused_computation.41 | loop fusion | flops 1048576 | bytes 1048576 | tf_op jit(solution)/shard_map/concatenate | solution.py:230
  76.4 2.9 %collective-permute-done.24 = bf16[384,512]{0,1:T(8,128)(2,1)S(1)} collective-permute-done((bf16[384,512]{0,1:T(8,128)(2,1)S(1)}, bf16[384,512]{0,1:T(8,128)(2,1)S(1)}, u32[]{:S(2)}, u32[]{:S(2)}) %collective-permute-start.24) | collective-permute-done | bytes 393248 | tf_op jit(solution)/shard_map/ppermute | solution.py:93
  79.2 0.2 broadcast_select_fusion.3
  79.5 1.2 %copy.29 = bf16[384,1024]{1,0:T(8,128)(2,1)} copy(bf16[384,1024]{0,1:T(8,128)(2,1)S(1)} %pad_maximum_fusion.4) | data formatting | bytes 1572864
  (51 shorter events, 1.5 us)
Async XLA Ops:
  0.6 5.5 %copy-start.2 = (bf16[64,3072]{1,0:T(8,128)(2,1)S(1)}, bf16[64,3072]{1,0:T(8,128)(2,1)}, u32[]{:S(2)}) copy-start(bf16[64,3072]{1,0:T(8,128)(2,1)} %param.4) | copy-start | bytes 1179652
  0.7 18.8 %copy-start.1 = (bf16[256,1024]{1,0:T(8,128)(2,1)S(1)}, bf16[256,1024]{1,0:T(8,128)(2,1)}, u32[]{:S(2)}) copy-start(bf16[256,1024]{1,0:T(8,128)(2,1)} %attn_ref.1) | copy-start | bytes 1572868
  3.2 26.3 %collective-permute-start.6 = (bf16[1024,512]{1,0:T(8,128)(2,1)}, bf16[1024,512]{1,0:T(8,128)(2,1)S(1)}, u32[]{:S(2)}, u32[]{:S(2)}) collective-permute-start(bf16[1024,512]{1,0:T(8,128)(2,1)} %shard_map.59), channel_id=1, source_target_pairs={{0,4},{4,0},{8,12},{12,8},{16,20},{20,16},{24,28},{28,24},{1,5},{5... | collective-permute-start | bytes 3145736 | tf_op jit(solution)/shard_map/ppermute | solution.py:93
  6.2 7.6 %collective-permute-start.2 = (bf16[64,768]{1,0:T(8,128)(2,1)S(1)}, bf16[64,768]{1,0:T(8,128)(2,1)S(1)}, u32[]{:S(2)}, u32[]{:S(2)}) collective-permute-start(bf16[64,768]{1,0:T(8,128)(2,1)S(1)} %get-tuple-element.72), channel_id=1, source_target_pairs={{0,24},{4,28},{8,16},{12,20},{16,8},{20,12},{24,0},{28,4},{1,25},{... | collective-permute-start | bytes 294920 | tf_op jit(solution)/shard_map/ppermute | solution.py:102
  9.9 8.0 %collective-permute-start.1 = (bf16[64,768]{1,0:T(8,128)(2,1)S(1)}, bf16[64,768]{1,0:T(8,128)(2,1)S(1)}, u32[]{:S(2)}, u32[]{:S(2)}) collective-permute-start(bf16[64,768]{1,0:T(8,128)(2,1)S(1)} %get-tuple-element.73), channel_id=1, source_target_pairs={{0,16},{4,20},{8,24},{12,28},{16,0},{20,4},{24,8},{28,12},{1,17},{... | collective-permute-start | bytes 294920 | tf_op jit(solution)/shard_map/ppermute | solution.py:102
  9.9 8.0 %collective-permute-start = (bf16[64,768]{1,0:T(8,128)(2,1)S(1)}, bf16[64,768]{1,0:T(8,128)(2,1)S(1)}, u32[]{:S(2)}, u32[]{:S(2)}) collective-permute-start(bf16[64,768]{1,0:T(8,128)(2,1)S(1)} %get-tuple-element.71), channel_id=1, source_target_pairs={{0,8},{4,12},{8,0},{12,4},{16,24},{20,28},{24,16},{28,20},{1,9},{5... | collective-permute-start | bytes 294920 | tf_op jit(solution)/shard_map/ppermute | solution.py:102
  17.9 10.3 %collective-permute-start.3 = (bf16[4,64,768]{2,1,0:T(8,128)(2,1)S(1)}, bf16[4,64,768]{2,1,0:T(8,128)(2,1)S(1)}, u32[]{:S(2)}, u32[]{:S(2)}) collective-permute-start(bf16[4,64,768]{2,1,0:T(8,128)(2,1)S(1)} %pad_maximum_fusion.7), channel_id=1, source_target_pairs={{0,2},{1,3},{2,0},{3,1},{4,6},{5,7},{6,4},{7,5},{8,10},{9,11},{10,... | collective-permute-start | bytes 1179656 | tf_op jit(solution)/shard_map/ppermute | solution.py:97
  19.5 8.8 %collective-permute-start.4 = (bf16[256,512]{1,0:T(8,128)(2,1)S(1)}, bf16[256,512]{1,0:T(8,128)(2,1)}, u32[]{:S(2)}, u32[]{:S(2)}) collective-permute-start(bf16[256,512]{1,0:T(8,128)(2,1)S(1)} %constant_dynamic-slice_fusion.1), channel_id=1, source_target_pairs={{0,8},{4,12},{8,0},{12,4},{16,24},{20,28},{24,16},{28,20},{1,9},{5... | collective-permute-start | bytes 786440 | tf_op jit(solution)/shard_map/ppermute | solution.py:102
  20.1 8.3 %collective-permute-start.5 = (bf16[256,512]{1,0:T(8,128)(2,1)S(1)}, bf16[256,512]{1,0:T(8,128)(2,1)S(1)}, u32[]{:S(2)}, u32[]{:S(2)}) collective-permute-start(bf16[256,512]{1,0:T(8,128)(2,1)S(1)} %constant_dynamic-slice_fusion.1), channel_id=1, source_target_pairs={{0,1},{1,0},{2,3},{3,2},{4,5},{5,4},{6,7},{7,6},{8,16},{9,17},{10,... | collective-permute-start | bytes 786440 | tf_op jit(solution)/shard_map/ppermute | solution.py:118
  28.3 6.3 %copy-start = (bf16[1024,512]{1,0:T(8,128)(2,1)S(1)}, bf16[1024,512]{1,0:T(8,128)(2,1)}, u32[]{:S(2)}) copy-start(bf16[1024,512]{1,0:T(8,128)(2,1)} %shard_map.59) | copy-start | bytes 3145732
  29.5 5.2 %collective-permute-start.7 = (bf16[4,2,64,768]{3,2,1,0:T(8,128)(2,1)S(1)}, bf16[4,2,64,768]{3,2,1,0:T(8,128)(2,1)}, u32[]{:S(2)}, u32[]{:S(2)}) collective-permute-start(bf16[4,2,64,768]{3,2,1,0:T(8,128)(2,1)S(1)} %pad_maximum_fusion.3), channel_id=1, source_target_pairs={{0,1},{1,0},{2,3},{3,2},{4,5},{5,4},{6,7},{7,6},{8,9},{9,8},{10,11... | collective-permute-start | bytes 2359304 | tf_op jit(solution)/shard_map/ppermute | solution.py:97
  29.6 10.9 %collective-permute-start.14 = (bf16[256,512]{1,0:T(8,128)(2,1)S(1)}, bf16[256,512]{1,0:T(8,128)(2,1)S(1)}, u32[]{:S(2)}, u32[]{:S(2)}) collective-permute-start(bf16[256,512]{1,0:T(8,128)(2,1)S(1)} %pad_maximum_fusion.8), channel_id=1, source_target_pairs={{0,1},{1,0},{2,3},{3,2},{4,5},{5,4},{6,7},{7,6},{8,16},{9,17},{10,... | collective-permute-start | bytes 786440 | tf_op jit(solution)/shard_map/ppermute | solution.py:118
  30.2 10.4 %collective-permute-start.15 = (bf16[256,512]{1,0:T(8,128)(2,1)S(1)}, bf16[256,512]{1,0:T(8,128)(2,1)S(1)}, u32[]{:S(2)}, u32[]{:S(2)}) collective-permute-start(bf16[256,512]{1,0:T(8,128)(2,1)S(1)} %pad_maximum_fusion.8), channel_id=1, source_target_pairs={{0,8},{4,12},{8,0},{12,4},{16,24},{20,28},{24,16},{28,20},{1,9},{5... | collective-permute-start | bytes 786440 | tf_op jit(solution)/shard_map/ppermute | solution.py:102
  33.1 22.4 %collective-permute-start.22 = (bf16[4,2,64,768]{3,2,1,0:T(8,128)(2,1)S(1)}, bf16[4,2,64,768]{3,2,1,0:T(8,128)(2,1)S(1)}, u32[]{:S(2)}, u32[]{:S(2)}) collective-permute-start(bf16[4,2,64,768]{3,2,1,0:T(8,128)(2,1)S(1)} %pad_maximum_fusion.3), channel_id=1, source_target_pairs={{0,4},{4,0},{8,12},{12,8},{16,20},{20,16},{24,28},{28,24},{1,5},{5... | collective-permute-start | bytes 2359304 | tf_op jit(solution)/shard_map/ppermute | solution.py:93
  38.4 5.4 %collective-permute-start.8 = (bf16[256,512]{1,0:T(8,128)(2,1)}, bf16[256,512]{1,0:T(8,128)(2,1)S(1)}, u32[]{:S(2)}, u32[]{:S(2)}) collective-permute-start(bf16[256,512]{1,0:T(8,128)(2,1)} %collective-permute-done.4), channel_id=1, source_target_pairs={{0,1},{1,0},{2,3},{3,2},{4,5},{5,4},{6,7},{7,6},{8,16},{9,17},{10,... | collective-permute-start | bytes 786440 | tf_op jit(solution)/shard_map/ppermute | solution.py:118
  38.4 9.2 %collective-permute-start.9 = (bf16[256,512]{1,0:T(8,128)(2,1)S(1)}, bf16[256,512]{1,0:T(8,128)(2,1)S(1)}, u32[]{:S(2)}, u32[]{:S(2)}) collective-permute-start(bf16[256,512]{1,0:T(8,128)(2,1)S(1)} %fusion.18), channel_id=1, source_target_pairs={{0,8},{4,12},{8,0},{12,4},{16,24},{20,28},{24,16},{28,20},{1,9},{5... | collective-permute-start | bytes 786440 | tf_op jit(solution)/shard_map/ppermute | solution.py:102
  40.6 9.3 %collective-permute-start.16 = (bf16[256,512]{1,0:T(8,128)(2,1)S(1)}, bf16[256,512]{1,0:T(8,128)(2,1)S(1)}, u32[]{:S(2)}, u32[]{:S(2)}) collective-permute-start(bf16[256,512]{1,0:T(8,128)(2,1)S(1)} %collective-permute-done.15), channel_id=1, source_target_pairs={{0,1},{1,0},{2,3},{3,2},{4,5},{5,4},{6,7},{7,6},{8,16},{9,17},{10,... | collective-permute-start | bytes 786440 | tf_op jit(solution)/shard_map/ppermute | solution.py:118
  40.6 12.6 %collective-permute-start.17 = (bf16[256,512]{1,0:T(8,128)(2,1)S(1)}, bf16[256,512]{1,0:T(8,128)(2,1)S(1)}, u32[]{:S(2)}, u32[]{:S(2)}) collective-permute-start(bf16[256,512]{1,0:T(8,128)(2,1)S(1)} %fusion.20), channel_id=1, source_target_pairs={{0,8},{4,12},{8,0},{12,4},{16,24},{20,28},{24,16},{28,20},{1,9},{5... | collective-permute-start | bytes 786440 | tf_op jit(solution)/shard_map/ppermute | solution.py:102
  47.7 11.2 %collective-permute-start.11 = (bf16[256,512]{1,0:T(8,128)(2,1)S(1)}, bf16[256,512]{1,0:T(8,128)(2,1)S(1)}, u32[]{:S(2)}, u32[]{:S(2)}) collective-permute-start(bf16[256,512]{1,0:T(8,128)(2,1)S(1)} %fusion.19), channel_id=1, source_target_pairs={{0,8},{4,12},{8,0},{12,4},{16,24},{20,28},{24,16},{28,20},{1,9},{5... | collective-permute-start | bytes 786440 | tf_op jit(solution)/shard_map/ppermute | solution.py:102
  49.9 8.9 %collective-permute-start.10 = (bf16[256,512]{1,0:T(8,128)(2,1)S(1)}, bf16[256,512]{1,0:T(8,128)(2,1)S(1)}, u32[]{:S(2)}, u32[]{:S(2)}) collective-permute-start(bf16[256,512]{1,0:T(8,128)(2,1)S(1)} %add_convert_fusion.3), channel_id=1, source_target_pairs={{0,1},{1,0},{2,3},{3,2},{4,5},{5,4},{6,7},{7,6},{8,16},{9,17},{10,... | collective-permute-start | bytes 786440 | tf_op jit(solution)/shard_map/ppermute | solution.py:118
  53.3 11.2 %collective-permute-start.19 = (bf16[256,512]{1,0:T(8,128)(2,1)S(1)}, bf16[256,512]{1,0:T(8,128)(2,1)S(1)}, u32[]{:S(2)}, u32[]{:S(2)}) collective-permute-start(bf16[256,512]{1,0:T(8,128)(2,1)S(1)} %fusion.21), channel_id=1, source_target_pairs={{0,8},{4,12},{8,0},{12,4},{16,24},{20,28},{24,16},{28,20},{1,9},{5... | collective-permute-start | bytes 786440 | tf_op jit(solution)/shard_map/ppermute | solution.py:102
  55.5 8.9 %collective-permute-start.18 = (bf16[256,512]{1,0:T(8,128)(2,1)S(1)}, bf16[256,512]{1,0:T(8,128)(2,1)S(1)}, u32[]{:S(2)}, u32[]{:S(2)}) collective-permute-start(bf16[256,512]{1,0:T(8,128)(2,1)S(1)} %add_convert_fusion.1), channel_id=1, source_target_pairs={{0,1},{1,0},{2,3},{3,2},{4,5},{5,4},{6,7},{7,6},{8,16},{9,17},{10,... | collective-permute-start | bytes 786440 | tf_op jit(solution)/shard_map/ppermute | solution.py:118
  55.5 11.9 %collective-permute-start.23 = (bf16[4,2,64,768]{3,2,1,0:T(8,128)(2,1)S(1)}, bf16[4,2,64,768]{3,2,1,0:T(8,128)(2,1)S(1)}, u32[]{:S(2)}, u32[]{:S(2)}) collective-permute-start(bf16[4,2,64,768]{3,2,1,0:T(8,128)(2,1)S(1)} %collective-permute-done.22), channel_id=1, source_target_pairs={{0,1},{1,0},{2,3},{3,2},{4,5},{5,4},{6,7},{7,6},{8,9},{9,8},{10,11... | collective-permute-start | bytes 2359304 | tf_op jit(solution)/shard_map/ppermute | solution.py:97
  59.0 16.3 %collective-permute-start.13 = (bf16[256,512]{1,0:T(8,128)(2,1)S(1)}, bf16[256,512]{1,0:T(8,128)(2,1)S(1)}, u32[]{:S(2)}, u32[]{:S(2)}) collective-permute-start(bf16[256,512]{1,0:T(8,128)(2,1)S(1)} %get-tuple-element.31), channel_id=1, source_target_pairs={{0,1},{1,0},{2,3},{3,2},{4,5},{5,4},{6,7},{7,6},{8,16},{9,17},{10,... | collective-permute-start | bytes 786440 | tf_op jit(solution)/shard_map/ppermute | solution.py:118
  59.1 16.3 %collective-permute-start.12 = (bf16[256,512]{1,0:T(8,128)(2,1)S(1)}, bf16[256,512]{1,0:T(8,128)(2,1)S(1)}, u32[]{:S(2)}, u32[]{:S(2)}) collective-permute-start(bf16[256,512]{1,0:T(8,128)(2,1)S(1)} %get-tuple-element.30), channel_id=1, source_target_pairs={{0,8},{4,12},{8,0},{12,4},{16,24},{20,28},{24,16},{28,20},{1,9},{5... | collective-permute-start | bytes 786440 | tf_op jit(solution)/shard_map/ppermute | solution.py:102
  64.6 5.9 %collective-permute-start.21 = (bf16[256,512]{1,0:T(8,128)(2,1)S(1)}, bf16[256,512]{1,0:T(8,128)(2,1)S(1)}, u32[]{:S(2)}, u32[]{:S(2)}) collective-permute-start(bf16[256,512]{1,0:T(8,128)(2,1)S(1)} %get-tuple-element.37), channel_id=1, source_target_pairs={{0,1},{1,0},{2,3},{3,2},{4,5},{5,4},{6,7},{7,6},{8,16},{9,17},{10,... | collective-permute-start | bytes 786440 | tf_op jit(solution)/shard_map/ppermute | solution.py:118
  64.7 10.5 %collective-permute-start.20 = (bf16[256,512]{1,0:T(8,128)(2,1)S(1)}, bf16[256,512]{1,0:T(8,128)(2,1)S(1)}, u32[]{:S(2)}, u32[]{:S(2)}) collective-permute-start(bf16[256,512]{1,0:T(8,128)(2,1)S(1)} %get-tuple-element.36), channel_id=1, source_target_pairs={{0,8},{4,12},{8,0},{12,4},{16,24},{20,28},{24,16},{28,20},{1,9},{5... | collective-permute-start | bytes 786440 | tf_op jit(solution)/shard_map/ppermute | solution.py:102
  70.0 9.3 %collective-permute-start.24 = (bf16[384,512]{0,1:T(8,128)(2,1)S(1)}, bf16[384,512]{0,1:T(8,128)(2,1)S(1)}, u32[]{:S(2)}, u32[]{:S(2)}) collective-permute-start(bf16[384,512]{0,1:T(8,128)(2,1)S(1)} %constant_dynamic-slice_fusion), channel_id=1, source_target_pairs={{0,4},{4,0},{8,12},{12,8},{16,20},{20,16},{24,28},{28,24},{1,5},{5... | collective-permute-start | bytes 1179656 | tf_op jit(solution)/shard_map/ppermute | solution.py:93

commit v6 on v5

--- a/solution.py
+++ b/solution.py
@@ -10,6 +10,7 @@
 BLOCK = 32
 PAIR = 2
 LINE = 4
+STEPS = 2
 
 
 def dequantize(codes_part, scales_part):
@@ -20,31 +21,36 @@
 def pack(side, codes, scales, attn_out):
     heads, features = codes.shape
     group_rows = attn_out.shape[0]
-    count = heads // group_rows
-    width = heads // PAIR // count
+    blocks = heads // group_rows // STEPS
+    width = group_rows // PAIR
+    rows = heads // STEPS
 
     def kernel(side_ref, codes_ref, scales_ref, attn_ref, out_ref):
         scale = scales_ref[...].astype(jnp.float32)
-        for k in range(heads // BLOCK):
-            rows = slice(k * BLOCK, (k + 1) * BLOCK)
-            values = codes_ref[rows].astype(jnp.float32) * scale[k : k + 1]
-            out_ref[rows, :features] = values.astype(out_ref.dtype)
-        for other in range(PAIR):
-
-            @pl.when(side_ref[0] == 1 - other)
-            def _():
-                for k in range(count):
-                    first = other * (heads // PAIR) + k * width
-                    rows = slice(k * group_rows, (k + 1) * group_rows)
-                    out_ref[rows, features:] = attn_ref[:, first : first + width]
-
-    in_vmem = pl.BlockSpec(memory_space=pltpu.VMEM)
+        for k in range(rows // BLOCK):
+            part = slice(k * BLOCK, (k + 1) * BLOCK)
+            values = codes_ref[part].astype(jnp.float32) * scale[k : k + 1]
+            out_ref[part, :features] = values.astype(out_ref.dtype)
+        for k in range(blocks):
+            part = slice(k * group_rows, (k + 1) * group_rows)
+            out_ref[part, features:] = attn_ref[:, k * width : (k + 1) * width]
+
     size = heads * (features + width)
     return pl.pallas_call(
         kernel,
         out_shape=jax.ShapeDtypeStruct((heads, features + width), codes.dtype),
-        in_specs=[pl.BlockSpec(memory_space=pltpu.SMEM), in_vmem, in_vmem, in_vmem],
-        out_specs=in_vmem,
+        grid_spec=pltpu.PrefetchScalarGridSpec(
+            num_scalar_prefetch=1,
+            grid=(STEPS,),
+            in_specs=[
+                pl.BlockSpec((rows, features), lambda i, side_ref: (i, 0)),
+                pl.BlockSpec((rows // BLOCK, features), lambda i, side_ref: (i, 0)),
+                pl.BlockSpec(
+                    (group_rows, blocks * width), lambda i, side_ref: (0, (1 - side_ref[0]) * STEPS + i)
+                ),
+            ],
+            out_specs=pl.BlockSpec((rows, features + width), lambda i, side_ref: (i, 0)),
+        ),
         cost_estimate=pl.CostEstimate(flops=size, bytes_accessed=4 * size, transcendentals=0),
     )(side[None].astype(jnp.int32), codes, scales, attn_out)
 
@@ -126,7 +132,7 @@
     held = jnp.stack(slots)
 
     attn_own = lax.dynamic_slice_in_dim(attn_out, side * half, half, 1)
-    packed = heads % group_rows == 0
+    packed = heads % (STEPS * group_rows) == 0
     if packed:
         sent = pack(side, weight_codes, block_scales, attn_out)
         weight = sent[:, :own_features]
@@ -187,6 +193,12 @@
             before = [send_outer, send_inner]
             outer_3.append(outer(send_outer))
             inner_3.append(inner(send_inner))
+        total, partial = 0.0, []
+        for k, side_cols in enumerate((cols, cols_other)):
+            attn_2 = jnp.where(middle, inner_2[k], outer_2[k])
+            sums = by_token(side_cols[0], attn[k]) + by_token(side_cols[1], attn_1[k])
+            partial.append(sums + by_token(side_cols[2], attn_2))
+        outer_3[1], inner_3[1], partial = together(outer_3[1], inner_3[1], partial)
         before = []
         for k in streams:
             send_inner = (part[k][3] + outer_3[k].astype(jnp.float32)).astype(jnp.bfloat16)
@@ -197,11 +209,7 @@
             outer_4, inner_4 = outer(send_outer), inner(send_inner)
             ga = part[k][0] + outer_4.astype(jnp.float32)
             gas.append(ga + jnp.where(middle, inner_4.astype(jnp.float32), 0.0))
-        total = 0.0
-        for k, side_cols in enumerate((cols, cols_other)):
-            attn_2 = jnp.where(middle, inner_2[k], outer_2[k])
-            total = total + by_token(side_cols[0], attn[k]) + by_token(side_cols[1], attn_1[k])
-            total = total + by_token(side_cols[2], attn_2)
+        total = partial[0] + partial[1]
         for k, side_cols in enumerate((cols, cols_other)):
             attn_3 = jnp.where(middle, attn_in[k], outer_3[k])
             total = total + by_token(side_cols[3], attn_3)

time: 80.9 us -> 77.9 us (0.963)
  waiting for transfers between devices: 36.4 us -> 34.6 us
  local copies, waits for them, and re-layouts: 1.44 us -> 0.26 us
  other arithmetic: 4.23 us -> 5.09 us
    ppermute x3, waiting for transfers between devices: 3.99 us -> 1.78 us  [swap_x(): return lax.ppermute(piece, 'dp', [(i, i ^ 1) for i in range(n_dp)])]
    unnamed x7 -> x6, local copies, waits for them, and re-layouts: 1.18 us -> 0.01 us
    concatenate x5, other arithmetic: 0.59 us -> 1.5 us  [halves(): return jnp.concatenate([first, second], axis)]
  transfers between devices with their start and end apart: 25 -> 25, of which waited for: 10 -> 11; matrix products, arithmetic and copies ran while one was open for 13% -> 13% of each run, Pallas kernels for 0% -> 0%
where the time goes in v6:
time: 77.9 us; the launch traced here: 77.7 us
  waiting for transfers between devices  34.6 us (44%)
  starting transfers between devices  28.4 us (36%)
  matrix products  6.18 us (8%)
  other arithmetic  5.09 us (7%)
  Pallas kernels  2.22 us (3%)
  between operations  0.98 us (1%)
    ppermute x11, waiting for transfers between devices, move_layers(): return lax.ppermute(piece, 'dp', moves)  24.7 us
    ppermute x11, starting transfers between devices, move_layers(): return lax.ppermute(piece, 'dp', moves)  20.4 us
    ppermute x3, waiting for transfers between devices, with_mp(): other = lax.ppermute(piece, 'mp', [(i, i ^ bit) for i in range(n_mp)])  8.09 us
    ppermute x3, starting transfers between devices, swap_x(): return lax.ppermute(piece, 'dp', [(i, i ^ 1) for i in range(n_dp)])  5.02 us
    dot_general x8, matrix products, by_token(): lax.dot_general(columns, rows, (((0,), (0,)), ((), ())), preferred_elemen...  4.17 us
    pallas_call x1, Pallas kernels, pack(): pl.pallas_call(kernel, out_shape=jax.ShapeDtypeStruct((heads, features +...  2.22 us
    ppermute x3, starting transfers between devices, with_mp(): other = lax.ppermute(piece, 'mp', [(i, i ^ bit) for i in range(n_mp)])  2.1 us
    dot_general x2, matrix products, by_feature(): lax.dot_general(rows, weight, (((1,), (1,)), ((), ())), preferred_element...  2.01 us
  transfers between devices with their start and end apart: 25, of which 11 were waited for; matrix products, arithmetic and copies ran while one was open for 13% of the time, Pallas kernels for 0%

profile of v6, /device:TPU:0, one launch (start us, length us, event | category | flops | bytes accessed | tf_op | source)
XLA Modules:
  0.0 77.7 jit_solution(13440961639028342261)
XLA Ops:
  0.7 2.2 %shard_map.59 = bf16[1024,512]{1,0:T(8,128)(2,1)} custom-call(s32[1]{0:T(128)} %bitcast.7.side_ref, bf16[1024,384]{1,0:T(8,128)(2,1)} %codes_ref.1, bf16[32,384]{1,0:T(8,128)(2,1)} %scales_ref.1, bf16[256,1024]{1,0:T(8,128)(2,1)} %attn_ref.1), custom_call_target="tpu_custom_call" | custom-call | flops 524288 | bytes 2097152 | tf_op jit(solution)/shard_map/pallas_call | solution.py:39
  2.9 2.9 %collective-permute-start.6 = (bf16[1024,512]{1,0:T(8,128)(2,1)}, bf16[1024,512]{1,0:T(8,128)(2,1)S(1)}, u32[]{:S(2)}, u32[]{:S(2)}) collective-permute-start(bf16[1024,512]{1,0:T(8,128)(2,1)} %shard_map.59), channel_id=1, source_target_pairs={{0,4},{4,0},{8,12},{12,8},{16,20},{20,16},{24,28},{28,24},{1,5},{5... | collective-permute-start | bytes 3145736 | tf_op jit(solution)/shard_map/ppermute | solution.py:99
  5.9 3.7 %collective-permute-start.2 = (bf16[64,768]{1,0:T(8,128)(2,1)S(1)}, bf16[64,768]{1,0:T(8,128)(2,1)S(1)}, u32[]{:S(2)}, u32[]{:S(2)}) collective-permute-start(bf16[64,768]{1,0:T(8,128)(2,1)S(1)} %get-tuple-element.76), channel_id=1, source_target_pairs={{0,24},{4,28},{8,16},{12,20},{16,8},{20,12},{24,0},{28,4},{1,25},{... | collective-permute-start | bytes 294920 | tf_op jit(solution)/shard_map/ppermute | solution.py:108
  9.5 0.8 %collective-permute-start = (bf16[64,768]{1,0:T(8,128)(2,1)S(1)}, bf16[64,768]{1,0:T(8,128)(2,1)S(1)}, u32[]{:S(2)}, u32[]{:S(2)}) collective-permute-start(bf16[64,768]{1,0:T(8,128)(2,1)S(1)} %get-tuple-element.75), channel_id=1, source_target_pairs={{0,8},{4,12},{8,0},{12,4},{16,24},{20,28},{24,16},{28,20},{1,9},{5... | collective-permute-start | bytes 294920 | tf_op jit(solution)/shard_map/ppermute | solution.py:108
  10.3 3.1 %collective-permute-done.2 = bf16[64,768]{1,0:T(8,128)(2,1)S(1)} collective-permute-done((bf16[64,768]{1,0:T(8,128)(2,1)S(1)}, bf16[64,768]{1,0:T(8,128)(2,1)S(1)}, u32[]{:S(2)}, u32[]{:S(2)}) %collective-permute-start.2) | collective-permute-done | bytes 98336 | tf_op jit(solution)/shard_map/ppermute | solution.py:108
  13.5 4.1 %collective-permute-done.1 = bf16[64,768]{1,0:T(8,128)(2,1)S(1)} collective-permute-done((bf16[64,768]{1,0:T(8,128)(2,1)S(1)}, bf16[64,768]{1,0:T(8,128)(2,1)S(1)}, u32[]{:S(2)}, u32[]{:S(2)}) %collective-permute-start.1) | collective-permute-done | bytes 98336 | tf_op jit(solution)/shard_map/ppermute | solution.py:108
  17.6 1.6 %collective-permute-start.3 = (bf16[4,64,768]{2,1,0:T(8,128)(2,1)S(1)}, bf16[4,64,768]{2,1,0:T(8,128)(2,1)S(1)}, u32[]{:S(2)}, u32[]{:S(2)}) collective-permute-start(bf16[4,64,768]{2,1,0:T(8,128)(2,1)S(1)} %pad_maximum_fusion.7), channel_id=1, source_target_pairs={{0,2},{1,3},{2,0},{3,1},{4,6},{5,7},{6,4},{7,5},{8,10},{9,11},{10,... | collective-permute-start | bytes 1179656 | tf_op jit(solution)/shard_map/ppermute | solution.py:103
  19.2 0.6 collective-permute-start.4
  19.8 8.1 %collective-permute-done.3 = bf16[4,64,768]{2,1,0:T(8,128)(2,1)S(1)} collective-permute-done((bf16[4,64,768]{2,1,0:T(8,128)(2,1)S(1)}, bf16[4,64,768]{2,1,0:T(8,128)(2,1)S(1)}, u32[]{:S(2)}, u32[]{:S(2)}) %collective-permute-start.3) | collective-permute-done | bytes 393248 | tf_op jit(solution)/shard_map/ppermute | solution.py:103
  28.1 1.1 %collective-permute-done.6 = bf16[1024,512]{1,0:T(8,128)(2,1)S(1)} collective-permute-done((bf16[1024,512]{1,0:T(8,128)(2,1)}, bf16[1024,512]{1,0:T(8,128)(2,1)S(1)}, u32[]{:S(2)}, u32[]{:S(2)}) %collective-permute-start.6) | collective-permute-done | bytes 1048608 | tf_op jit(solution)/shard_map/ppermute | solution.py:99
  29.3 0.6 collective-permute-start.14
  29.9 2.9 %collective-permute-start.15 = (bf16[256,512]{1,0:T(8,128)(2,1)S(1)}, bf16[256,512]{1,0:T(8,128)(2,1)S(1)}, u32[]{:S(2)}, u32[]{:S(2)}) collective-permute-start(bf16[256,512]{1,0:T(8,128)(2,1)S(1)} %pad_maximum_fusion.8), channel_id=1, source_target_pairs={{0,8},{4,12},{8,0},{12,4},{16,24},{20,28},{24,16},{28,20},{1,9},{5... | collective-permute-start | bytes 786440 | tf_op jit(solution)/shard_map/ppermute | solution.py:108
  32.8 1.5 %collective-permute-start.20 = (bf16[4,2,64,768]{3,2,1,0:T(8,128)(2,1)S(1)}, bf16[4,2,64,768]{3,2,1,0:T(8,128)(2,1)S(1)}, u32[]{:S(2)}, u32[]{:S(2)}) collective-permute-start(bf16[4,2,64,768]{3,2,1,0:T(8,128)(2,1)S(1)} %pad_maximum_fusion.3), channel_id=1, source_target_pairs={{0,4},{4,0},{8,12},{12,8},{16,20},{20,16},{24,28},{28,24},{1,5},{5... | collective-permute-start | bytes 2359304 | tf_op jit(solution)/shard_map/ppermute | solution.py:99
  34.2 0.1 broadcast_select_fusion.1
  34.4 1.2 %select_bitcast_fusion.3 = (bf16[4,2,1,64,768]{4,3,2,1,0:T(8,128)(2,1)S(1)}, bf16[4,2,1,64,768]{4,3,2,1,0:T(8,128)(2,1)S(1)}) fusion(bf16[4,2,64,768]{3,2,1,0:T(8,128)(2,1)S(1)} %pad_maximum_fusion.3, bf16[4,2,64,768]{3,2,1,0:T(8,128)(2,1)} %collective-permute-done.7, pred[]{:T(512)S(6)} %eq.11), kind=kLoop, calls=%fused_computation.30 | loop fusion | flops 786432 | bytes 3145729 | tf_op jit(solution)/shard_map/jit(_where)/select_n | solution.py:59
  35.7 0.1 pad_maximum_fusion
  35.8 1.0 %fusion.3 = f32[1024,512]{1,0:T(8,128)S(1)} fusion(bf16[1024,768]{1,0:T(8,128)(2,1)S(1)} %bitcast.45, bf16[1024,384]{1,0:T(8,128)(2,1)S(1)} %get-tuple-element.53, bf16[1024,384]{1,0:T(8,128)(2,1)S(1)} %get-tuple-element.52), kind=kOutput, calls=%fused_computation.23 | convolution fusion | flops 806879232 | bytes 5242880 | tf_op jit(solution)/shard_map/dot_general | solution.py:73
  36.8 1.0 %fusion.1 = f32[1024,512]{1,0:T(8,128)S(1)} fusion(bf16[1024,768]{1,0:T(8,128)(2,1)S(1)} %bitcast.46, bf16[1024,384]{1,0:T(8,128)(2,1)S(1)} %get-tuple-element.52, bf16[1024,384]{1,0:T(8,128)(2,1)S(1)} %get-tuple-element.53), kind=kOutput, calls=%fused_computation.21 | convolution fusion | flops 806879232 | bytes 5242880 | tf_op jit(solution)/shard_map/dot_general | solution.py:73
  37.9 0.1 fusion.17
  38.1 2.1 %collective-permute-start.9 = (bf16[256,512]{1,0:T(8,128)(2,1)S(1)}, bf16[256,512]{1,0:T(8,128)(2,1)S(1)}, u32[]{:S(2)}, u32[]{:S(2)}) collective-permute-start(bf16[256,512]{1,0:T(8,128)(2,1)S(1)} %fusion.18), channel_id=1, source_target_pairs={{0,8},{4,12},{8,0},{12,4},{16,24},{20,28},{24,16},{28,20},{1,9},{5... | collective-permute-start | bytes 786440 | tf_op jit(solution)/shard_map/ppermute | solution.py:108
  40.3 1.3 %collective-permute-start.17 = (bf16[256,512]{1,0:T(8,128)(2,1)S(1)}, bf16[256,512]{1,0:T(8,128)(2,1)S(1)}, u32[]{:S(2)}, u32[]{:S(2)}) collective-permute-start(bf16[256,512]{1,0:T(8,128)(2,1)S(1)} %fusion.20), channel_id=1, source_target_pairs={{0,8},{4,12},{8,0},{12,4},{16,24},{20,28},{24,16},{28,20},{1,9},{5... | collective-permute-start | bytes 786440 | tf_op jit(solution)/shard_map/ppermute | solution.py:108
  41.6 0.4 fusion.38
  42.0 1.3 %fusion.39 = f32[768,512]{1,0:T(8,128)S(1)} fusion(bf16[256,768]{1,0:T(8,128)(2,1)S(1)} %bitcast.50, bf16[256,512]{1,0:T(8,128)(2,1)} %collective-permute-done.4), kind=kOutput, calls=%fused_computation.91 | convolution fusion | flops 201326592 | bytes 2228224 | tf_op jit(solution)/shard_map/dot_general | solution.py:79
  43.4 3.9 %collective-permute-done.9 = bf16[256,512]{1,0:T(8,128)(2,1)S(1)} collective-permute-done((bf16[256,512]{1,0:T(8,128)(2,1)S(1)}, bf16[256,512]{1,0:T(8,128)(2,1)S(1)}, u32[]{:S(2)}, u32[]{:S(2)}) %collective-permute-start.9) | collective-permute-done | bytes 262176 | tf_op jit(solution)/shard_map/ppermute | solution.py:108
  47.4 2.2 %collective-permute-start.11 = (bf16[256,512]{1,0:T(8,128)(2,1)S(1)}, bf16[256,512]{1,0:T(8,128)(2,1)S(1)}, u32[]{:S(2)}, u32[]{:S(2)}) collective-permute-start(bf16[256,512]{1,0:T(8,128)(2,1)S(1)} %fusion.19), channel_id=1, source_target_pairs={{0,8},{4,12},{8,0},{12,4},{16,24},{20,28},{24,16},{28,20},{1,9},{5... | collective-permute-start | bytes 786440 | tf_op jit(solution)/shard_map/ppermute | solution.py:108
  49.6 3.3 %collective-permute-done.17 = bf16[256,512]{1,0:T(8,128)(2,1)S(1)} collective-permute-done((bf16[256,512]{1,0:T(8,128)(2,1)S(1)}, bf16[256,512]{1,0:T(8,128)(2,1)S(1)}, u32[]{:S(2)}, u32[]{:S(2)}) %collective-permute-start.17) | collective-permute-done | bytes 262176 | tf_op jit(solution)/shard_map/ppermute | solution.py:108
  53.0 2.2 %collective-permute-start.18 = (bf16[256,512]{1,0:T(8,128)(2,1)S(1)}, bf16[256,512]{1,0:T(8,128)(2,1)S(1)}, u32[]{:S(2)}, u32[]{:S(2)}) collective-permute-start(bf16[256,512]{1,0:T(8,128)(2,1)S(1)} %fusion.21), channel_id=1, source_target_pairs={{0,8},{4,12},{8,0},{12,4},{16,24},{20,28},{24,16},{28,20},{1,9},{5... | collective-permute-start | bytes 786440 | tf_op jit(solution)/shard_map/ppermute | solution.py:108
  55.2 0.5 collective-permute-start.21
  55.7 0.4 add_add_fusion.1
  56.1 2.4 %collective-permute-done.11 = bf16[256,512]{1,0:T(8,128)(2,1)S(1)} collective-permute-done((bf16[256,512]{1,0:T(8,128)(2,1)S(1)}, bf16[256,512]{1,0:T(8,128)(2,1)S(1)}, u32[]{:S(2)}, u32[]{:S(2)}) %collective-permute-start.11) | collective-permute-done | bytes 262176 | tf_op jit(solution)/shard_map/ppermute | solution.py:108
  58.5 0.2 add_convert_fusion.2
  58.8 2.3 %collective-permute-start.12 = (bf16[256,512]{1,0:T(8,128)(2,1)S(1)}, bf16[256,512]{1,0:T(8,128)(2,1)S(1)}, u32[]{:S(2)}, u32[]{:S(2)}) collective-permute-start(bf16[256,512]{1,0:T(8,128)(2,1)S(1)} %get-tuple-element.34), channel_id=1, source_target_pairs={{0,8},{4,12},{8,0},{12,4},{16,24},{20,28},{24,16},{28,20},{1,9},{5... | collective-permute-start | bytes 786440 | tf_op jit(solution)/shard_map/ppermute | solution.py:108
  61.1 0.4 fusion.26
  61.6 0.1 pad_maximum_fusion.6
  61.8 0.4 fusion.36
  62.3 0.4 fusion.40
  62.7 0.4 add_add_fusion
  63.1 1.0 %collective-permute-done.18 = bf16[256,512]{1,0:T(8,128)(2,1)S(1)} collective-permute-done((bf16[256,512]{1,0:T(8,128)(2,1)S(1)}, bf16[256,512]{1,0:T(8,128)(2,1)S(1)}, u32[]{:S(2)}, u32[]{:S(2)}) %collective-permute-start.18) | collective-permute-done | bytes 262176 | tf_op jit(solution)/shard_map/ppermute | solution.py:108
  64.1 0.2 add_convert_fusion
  64.4 2.3 %collective-permute-start.22 = (bf16[256,512]{1,0:T(8,128)(2,1)S(1)}, bf16[256,512]{1,0:T(8,128)(2,1)S(1)}, u32[]{:S(2)}, u32[]{:S(2)}) collective-permute-start(bf16[256,512]{1,0:T(8,128)(2,1)S(1)} %get-tuple-element.44), channel_id=1, source_target_pairs={{0,8},{4,12},{8,0},{12,4},{16,24},{20,28},{24,16},{28,20},{1,9},{5... | collective-permute-start | bytes 786440 | tf_op jit(solution)/shard_map/ppermute | solution.py:108
  66.8 0.5 multiply_convert_fusion
  67.3 0.6 collective-permute-start.24
  67.9 1.9 %collective-permute-done.12 = bf16[256,512]{1,0:T(8,128)(2,1)S(1)} collective-permute-done((bf16[256,512]{1,0:T(8,128)(2,1)S(1)}, bf16[256,512]{1,0:T(8,128)(2,1)S(1)}, u32[]{:S(2)}, u32[]{:S(2)}) %collective-permute-start.12) | collective-permute-done | bytes 262176 | tf_op jit(solution)/shard_map/ppermute | solution.py:108
  69.9 5.0 %collective-permute-done.22 = bf16[256,512]{1,0:T(8,128)(2,1)S(1)} collective-permute-done((bf16[256,512]{1,0:T(8,128)(2,1)S(1)}, bf16[256,512]{1,0:T(8,128)(2,1)S(1)}, u32[]{:S(2)}, u32[]{:S(2)}) %collective-permute-start.22) | collective-permute-done | bytes 262176 | tf_op jit(solution)/shard_map/ppermute | solution.py:108
  75.0 0.9 %pad_maximum_fusion.5 = bf16[256,1024]{1,0:T(8,128)(2,1)} fusion(bf16[256,512]{1,0:T(8,128)(2,1)S(1)} %fusion.7, bf16[256,512]{1,0:T(8,128)(2,1)S(1)} %fusion.10), kind=kLoop, calls=%fused_computation.43 | loop fusion | flops 1048576 | bytes 1048576 | tf_op jit(solution)/shard_map/concatenate | solution.py:238
  75.9 0.6 collective-permute-done.24
  76.5 0.2 broadcast_select_fusion.3
  76.7 1.0 %pad_maximum_fusion.4 = bf16[384,1024]{1,0:T(8,128)(2,1)} fusion(bf16[384,512]{1,0:T(8,128)(2,1)S(1)} %get-tuple-element.67, bf16[384,512]{1,0:T(8,128)(2,1)S(1)} %get-tuple-element.66), kind=kLoop, calls=%fused_computation.26 | loop fusion | flops 1572864 | bytes 1572864 | tf_op jit(solution)/shard_map/concatenate | solution.py:61
  (50 shorter events, 1.5 us)
Async XLA Ops:
  0.6 5.2 %copy-start.2 = (bf16[64,3072]{1,0:T(8,128)(2,1)S(1)}, bf16[64,3072]{1,0:T(8,128)(2,1)}, u32[]{:S(2)}) copy-start(bf16[64,3072]{1,0:T(8,128)(2,1)} %param.4) | copy-start | bytes 1179652
  0.7 18.5 %copy-start.1 = (bf16[256,1024]{1,0:T(8,128)(2,1)S(1)}, bf16[256,1024]{1,0:T(8,128)(2,1)}, u32[]{:S(2)}) copy-start(bf16[256,1024]{1,0:T(8,128)(2,1)} %attn_ref.1) | copy-start | bytes 1572868
  2.9 26.3 %collective-permute-start.6 = (bf16[1024,512]{1,0:T(8,128)(2,1)}, bf16[1024,512]{1,0:T(8,128)(2,1)S(1)}, u32[]{:S(2)}, u32[]{:S(2)}) collective-permute-start(bf16[1024,512]{1,0:T(8,128)(2,1)} %shard_map.59), channel_id=1, source_target_pairs={{0,4},{4,0},{8,12},{12,8},{16,20},{20,16},{24,28},{28,24},{1,5},{5... | collective-permute-start | bytes 3145736 | tf_op jit(solution)/shard_map/ppermute | solution.py:99
  5.9 7.6 %collective-permute-start.2 = (bf16[64,768]{1,0:T(8,128)(2,1)S(1)}, bf16[64,768]{1,0:T(8,128)(2,1)S(1)}, u32[]{:S(2)}, u32[]{:S(2)}) collective-permute-start(bf16[64,768]{1,0:T(8,128)(2,1)S(1)} %get-tuple-element.76), channel_id=1, source_target_pairs={{0,24},{4,28},{8,16},{12,20},{16,8},{20,12},{24,0},{28,4},{1,25},{... | collective-permute-start | bytes 294920 | tf_op jit(solution)/shard_map/ppermute | solution.py:108
  9.5 8.0 %collective-permute-start.1 = (bf16[64,768]{1,0:T(8,128)(2,1)S(1)}, bf16[64,768]{1,0:T(8,128)(2,1)S(1)}, u32[]{:S(2)}, u32[]{:S(2)}) collective-permute-start(bf16[64,768]{1,0:T(8,128)(2,1)S(1)} %get-tuple-element.77), channel_id=1, source_target_pairs={{0,16},{4,20},{8,24},{12,28},{16,0},{20,4},{24,8},{28,12},{1,17},{... | collective-permute-start | bytes 294920 | tf_op jit(solution)/shard_map/ppermute | solution.py:108
  9.5 8.0 %collective-permute-start = (bf16[64,768]{1,0:T(8,128)(2,1)S(1)}, bf16[64,768]{1,0:T(8,128)(2,1)S(1)}, u32[]{:S(2)}, u32[]{:S(2)}) collective-permute-start(bf16[64,768]{1,0:T(8,128)(2,1)S(1)} %get-tuple-element.75), channel_id=1, source_target_pairs={{0,8},{4,12},{8,0},{12,4},{16,24},{20,28},{24,16},{28,20},{1,9},{5... | collective-permute-start | bytes 294920 | tf_op jit(solution)/shard_map/ppermute | solution.py:108
  17.6 10.3 %collective-permute-start.3 = (bf16[4,64,768]{2,1,0:T(8,128)(2,1)S(1)}, bf16[4,64,768]{2,1,0:T(8,128)(2,1)S(1)}, u32[]{:S(2)}, u32[]{:S(2)}) collective-permute-start(bf16[4,64,768]{2,1,0:T(8,128)(2,1)S(1)} %pad_maximum_fusion.7), channel_id=1, source_target_pairs={{0,2},{1,3},{2,0},{3,1},{4,6},{5,7},{6,4},{7,5},{8,10},{9,11},{10,... | collective-permute-start | bytes 1179656 | tf_op jit(solution)/shard_map/ppermute | solution.py:103
  19.2 8.8 %collective-permute-start.4 = (bf16[256,512]{1,0:T(8,128)(2,1)S(1)}, bf16[256,512]{1,0:T(8,128)(2,1)}, u32[]{:S(2)}, u32[]{:S(2)}) collective-permute-start(bf16[256,512]{1,0:T(8,128)(2,1)S(1)} %constant_dynamic-slice_fusion.1), channel_id=1, source_target_pairs={{0,8},{4,12},{8,0},{12,4},{16,24},{20,28},{24,16},{28,20},{1,9},{5... | collective-permute-start | bytes 786440 | tf_op jit(solution)/shard_map/ppermute | solution.py:108
  19.8 8.3 %collective-permute-start.5 = (bf16[256,512]{1,0:T(8,128)(2,1)S(1)}, bf16[256,512]{1,0:T(8,128)(2,1)S(1)}, u32[]{:S(2)}, u32[]{:S(2)}) collective-permute-start(bf16[256,512]{1,0:T(8,128)(2,1)S(1)} %constant_dynamic-slice_fusion.1), channel_id=1, source_target_pairs={{0,1},{1,0},{2,3},{3,2},{4,5},{5,4},{6,7},{7,6},{8,16},{9,17},{10,... | collective-permute-start | bytes 786440 | tf_op jit(solution)/shard_map/ppermute | solution.py:124
  27.9 6.3 %copy-start = (bf16[1024,512]{1,0:T(8,128)(2,1)S(1)}, bf16[1024,512]{1,0:T(8,128)(2,1)}, u32[]{:S(2)}) copy-start(bf16[1024,512]{1,0:T(8,128)(2,1)} %shard_map.59) | copy-start | bytes 3145732
  29.2 5.2 %collective-permute-start.7 = (bf16[4,2,64,768]{3,2,1,0:T(8,128)(2,1)S(1)}, bf16[4,2,64,768]{3,2,1,0:T(8,128)(2,1)}, u32[]{:S(2)}, u32[]{:S(2)}) collective-permute-start(bf16[4,2,64,768]{3,2,1,0:T(8,128)(2,1)S(1)} %pad_maximum_fusion.3), channel_id=1, source_target_pairs={{0,1},{1,0},{2,3},{3,2},{4,5},{5,4},{6,7},{7,6},{8,9},{9,8},{10,11... | collective-permute-start | bytes 2359304 | tf_op jit(solution)/shard_map/ppermute | solution.py:103
  29.3 10.9 %collective-permute-start.14 = (bf16[256,512]{1,0:T(8,128)(2,1)S(1)}, bf16[256,512]{1,0:T(8,128)(2,1)S(1)}, u32[]{:S(2)}, u32[]{:S(2)}) collective-permute-start(bf16[256,512]{1,0:T(8,128)(2,1)S(1)} %pad_maximum_fusion.8), channel_id=1, source_target_pairs={{0,1},{1,0},{2,3},{3,2},{4,5},{5,4},{6,7},{7,6},{8,16},{9,17},{10,... | collective-permute-start | bytes 786440 | tf_op jit(solution)/shard_map/ppermute | solution.py:124
  29.9 10.4 %collective-permute-start.15 = (bf16[256,512]{1,0:T(8,128)(2,1)S(1)}, bf16[256,512]{1,0:T(8,128)(2,1)S(1)}, u32[]{:S(2)}, u32[]{:S(2)}) collective-permute-start(bf16[256,512]{1,0:T(8,128)(2,1)S(1)} %pad_maximum_fusion.8), channel_id=1, source_target_pairs={{0,8},{4,12},{8,0},{12,4},{16,24},{20,28},{24,16},{28,20},{1,9},{5... | collective-permute-start | bytes 786440 | tf_op jit(solution)/shard_map/ppermute | solution.py:108
  32.8 22.4 %collective-permute-start.20 = (bf16[4,2,64,768]{3,2,1,0:T(8,128)(2,1)S(1)}, bf16[4,2,64,768]{3,2,1,0:T(8,128)(2,1)S(1)}, u32[]{:S(2)}, u32[]{:S(2)}) collective-permute-start(bf16[4,2,64,768]{3,2,1,0:T(8,128)(2,1)S(1)} %pad_maximum_fusion.3), channel_id=1, source_target_pairs={{0,4},{4,0},{8,12},{12,8},{16,20},{20,16},{24,28},{28,24},{1,5},{5... | collective-permute-start | bytes 2359304 | tf_op jit(solution)/shard_map/ppermute | solution.py:99
  38.0 5.3 %collective-permute-start.8 = (bf16[256,512]{1,0:T(8,128)(2,1)}, bf16[256,512]{1,0:T(8,128)(2,1)S(1)}, u32[]{:S(2)}, u32[]{:S(2)}) collective-permute-start(bf16[256,512]{1,0:T(8,128)(2,1)} %collective-permute-done.4), channel_id=1, source_target_pairs={{0,1},{1,0},{2,3},{3,2},{4,5},{5,4},{6,7},{7,6},{8,16},{9,17},{10,... | collective-permute-start | bytes 786440 | tf_op jit(solution)/shard_map/ppermute | solution.py:124
  38.1 9.2 %collective-permute-start.9 = (bf16[256,512]{1,0:T(8,128)(2,1)S(1)}, bf16[256,512]{1,0:T(8,128)(2,1)S(1)}, u32[]{:S(2)}, u32[]{:S(2)}) collective-permute-start(bf16[256,512]{1,0:T(8,128)(2,1)S(1)} %fusion.18), channel_id=1, source_target_pairs={{0,8},{4,12},{8,0},{12,4},{16,24},{20,28},{24,16},{28,20},{1,9},{5... | collective-permute-start | bytes 786440 | tf_op jit(solution)/shard_map/ppermute | solution.py:108
  40.2 9.3 %collective-permute-start.16 = (bf16[256,512]{1,0:T(8,128)(2,1)S(1)}, bf16[256,512]{1,0:T(8,128)(2,1)S(1)}, u32[]{:S(2)}, u32[]{:S(2)}) collective-permute-start(bf16[256,512]{1,0:T(8,128)(2,1)S(1)} %collective-permute-done.15), channel_id=1, source_target_pairs={{0,1},{1,0},{2,3},{3,2},{4,5},{5,4},{6,7},{7,6},{8,16},{9,17},{10,... | collective-permute-start | bytes 786440 | tf_op jit(solution)/shard_map/ppermute | solution.py:124
  40.3 12.6 %collective-permute-start.17 = (bf16[256,512]{1,0:T(8,128)(2,1)S(1)}, bf16[256,512]{1,0:T(8,128)(2,1)S(1)}, u32[]{:S(2)}, u32[]{:S(2)}) collective-permute-start(bf16[256,512]{1,0:T(8,128)(2,1)S(1)} %fusion.20), channel_id=1, source_target_pairs={{0,8},{4,12},{8,0},{12,4},{16,24},{20,28},{24,16},{28,20},{1,9},{5... | collective-permute-start | bytes 786440 | tf_op jit(solution)/shard_map/ppermute | solution.py:108
  47.4 11.2 %collective-permute-start.11 = (bf16[256,512]{1,0:T(8,128)(2,1)S(1)}, bf16[256,512]{1,0:T(8,128)(2,1)S(1)}, u32[]{:S(2)}, u32[]{:S(2)}) collective-permute-start(bf16[256,512]{1,0:T(8,128)(2,1)S(1)} %fusion.19), channel_id=1, source_target_pairs={{0,8},{4,12},{8,0},{12,4},{16,24},{20,28},{24,16},{28,20},{1,9},{5... | collective-permute-start | bytes 786440 | tf_op jit(solution)/shard_map/ppermute | solution.py:108
  49.6 9.0 %collective-permute-start.10 = (bf16[256,512]{1,0:T(8,128)(2,1)S(1)}, bf16[256,512]{1,0:T(8,128)(2,1)S(1)}, u32[]{:S(2)}, u32[]{:S(2)}) collective-permute-start(bf16[256,512]{1,0:T(8,128)(2,1)S(1)} %add_convert_fusion.3), channel_id=1, source_target_pairs={{0,1},{1,0},{2,3},{3,2},{4,5},{5,4},{6,7},{7,6},{8,16},{9,17},{10,... | collective-permute-start | bytes 786440 | tf_op jit(solution)/shard_map/ppermute | solution.py:124
  53.0 11.2 %collective-permute-start.18 = (bf16[256,512]{1,0:T(8,128)(2,1)S(1)}, bf16[256,512]{1,0:T(8,128)(2,1)S(1)}, u32[]{:S(2)}, u32[]{:S(2)}) collective-permute-start(bf16[256,512]{1,0:T(8,128)(2,1)S(1)} %fusion.21), channel_id=1, source_target_pairs={{0,8},{4,12},{8,0},{12,4},{16,24},{20,28},{24,16},{28,20},{1,9},{5... | collective-permute-start | bytes 786440 | tf_op jit(solution)/shard_map/ppermute | solution.py:108
  55.2 9.0 %collective-permute-start.19 = (bf16[256,512]{1,0:T(8,128)(2,1)S(1)}, bf16[256,512]{1,0:T(8,128)(2,1)S(1)}, u32[]{:S(2)}, u32[]{:S(2)}) collective-permute-start(bf16[256,512]{1,0:T(8,128)(2,1)S(1)} %add_convert_fusion.1), channel_id=1, source_target_pairs={{0,1},{1,0},{2,3},{3,2},{4,5},{5,4},{6,7},{7,6},{8,16},{9,17},{10,... | collective-permute-start | bytes 786440 | tf_op jit(solution)/shard_map/ppermute | solution.py:124
  55.2 6.3 %collective-permute-start.21 = (bf16[4,2,64,768]{3,2,1,0:T(8,128)(2,1)S(1)}, bf16[4,2,64,768]{3,2,1,0:T(8,128)(2,1)S(1)}, u32[]{:S(2)}, u32[]{:S(2)}) collective-permute-start(bf16[4,2,64,768]{3,2,1,0:T(8,128)(2,1)S(1)} %collective-permute-done.20), channel_id=1, source_target_pairs={{0,1},{1,0},{2,3},{3,2},{4,5},{5,4},{6,7},{7,6},{8,9},{9,8},{10,11... | collective-permute-start | bytes 2359304 | tf_op jit(solution)/shard_map/ppermute | solution.py:103
  58.7 9.2 %collective-permute-start.13 = (bf16[256,512]{1,0:T(8,128)(2,1)S(1)}, bf16[256,512]{1,0:T(8,128)(2,1)S(1)}, u32[]{:S(2)}, u32[]{:S(2)}) collective-permute-start(bf16[256,512]{1,0:T(8,128)(2,1)S(1)} %get-tuple-element.35), channel_id=1, source_target_pairs={{0,1},{1,0},{2,3},{3,2},{4,5},{5,4},{6,7},{7,6},{8,16},{9,17},{10,... | collective-permute-start | bytes 786440 | tf_op jit(solution)/shard_map/ppermute | solution.py:124
  58.8 11.0 %collective-permute-start.12 = (bf16[256,512]{1,0:T(8,128)(2,1)S(1)}, bf16[256,512]{1,0:T(8,128)(2,1)S(1)}, u32[]{:S(2)}, u32[]{:S(2)}) collective-permute-start(bf16[256,512]{1,0:T(8,128)(2,1)S(1)} %get-tuple-element.34), channel_id=1, source_target_pairs={{0,8},{4,12},{8,0},{12,4},{16,24},{20,28},{24,16},{28,20},{1,9},{5... | collective-permute-start | bytes 786440 | tf_op jit(solution)/shard_map/ppermute | solution.py:108
  64.3 5.5 %collective-permute-start.23 = (bf16[256,512]{1,0:T(8,128)(2,1)S(1)}, bf16[256,512]{1,0:T(8,128)(2,1)S(1)}, u32[]{:S(2)}, u32[]{:S(2)}) collective-permute-start(bf16[256,512]{1,0:T(8,128)(2,1)S(1)} %get-tuple-element.45), channel_id=1, source_target_pairs={{0,1},{1,0},{2,3},{3,2},{4,5},{5,4},{6,7},{7,6},{8,16},{9,17},{10,... | collective-permute-start | bytes 786440 | tf_op jit(solution)/shard_map/ppermute | solution.py:124
  64.4 10.5 %collective-permute-start.22 = (bf16[256,512]{1,0:T(8,128)(2,1)S(1)}, bf16[256,512]{1,0:T(8,128)(2,1)S(1)}, u32[]{:S(2)}, u32[]{:S(2)}) collective-permute-start(bf16[256,512]{1,0:T(8,128)(2,1)S(1)} %get-tuple-element.44), channel_id=1, source_target_pairs={{0,8},{4,12},{8,0},{12,4},{16,24},{20,28},{24,16},{28,20},{1,9},{5... | collective-permute-start | bytes 786440 | tf_op jit(solution)/shard_map/ppermute | solution.py:108
  67.3 9.3 %collective-permute-start.24 = (bf16[384,512]{1,0:T(8,128)(2,1)S(1)}, bf16[384,512]{1,0:T(8,128)(2,1)S(1)}, u32[]{:S(2)}, u32[]{:S(2)}) collective-permute-start(bf16[384,512]{1,0:T(8,128)(2,1)S(1)} %constant_dynamic-slice_fusion), channel_id=1, source_target_pairs={{0,4},{4,0},{8,12},{12,8},{16,20},{20,16},{24,28},{28,24},{1,5},{5... | collective-permute-start | bytes 1179656 | tf_op jit(solution)/shard_map/ppermute | solution.py:99
